TPU v7x, 32 devices: a whole 2x2x4 slice. The times are simulated.
32 devices in a mesh: fsdp: 4 (over y, core), ctx: 8 (over z, x).
Axes of the slice: x: 2, y: 2, z: 4, core: 2. Of those that a mesh axis runs over, the one named last changes fastest.
Arguments:
- tokens: bfloat16 [1024, 8, 1152], P('ctx', 'fsdp'), may hold values from -6 to 6
- w_query: bfloat16 [1152, 1152], P('fsdp'), may hold values from -0.1875 to 0.1875
- w_key: bfloat16 [1152, 384], P('fsdp'), may hold values from -0.1875 to 0.1875
- w_value: bfloat16 [1152, 384], P('fsdp'), may hold values from -0.1875 to 0.1875
- w_out: bfloat16 [1152, 1152], P('fsdp'), may hold values from -1.5 to 1.5
- w_gate: bfloat16 [1152, 3072], P('fsdp'), may hold values from -0.1875 to 0.1875
- w_up: bfloat16 [1152, 3072], P('fsdp'), may hold values from -0.1875 to 0.1875
- w_down: bfloat16 [3072, 1152], P('fsdp'), may hold values from -0.109375 to 0.109375
- gain_attn: bfloat16 [1152], P('fsdp'), may hold values from 0.5 to 1.5
- gain_ffn: bfloat16 [1152], P('fsdp'), may hold values from 0.5 to 1.5
- cotangent: bfloat16 [1024, 8, 1152], P('ctx', 'fsdp'), may hold values from -6 to 6
Outputs:
- layer_out: bfloat16 [1024, 8, 1152], P('ctx', 'fsdp')
- grad_tokens: float32 [1024, 8, 1152], P('ctx', 'fsdp')
- grad_query: float32 [1152, 1152], P('fsdp')
- grad_key: float32 [1152, 384], P('fsdp')
- grad_value: float32 [1152, 384], P('fsdp')
- grad_out: float32 [1152, 1152], P('fsdp')
- grad_gate: float32 [1152, 3072], P('fsdp')
- grad_up: float32 [1152, 3072], P('fsdp')
- grad_down: float32 [3072, 1152], P('fsdp')
- grad_gain_attn: float32 [1152], P('fsdp')
- grad_gain_ffn: float32 [1152], P('fsdp')
All inputs are finite; a program needn't handle non-finite values.
Results may differ from a plain program's by a relative error of at most 0.023.
Values may be sent and summed in bfloat16 or wider, within the bound.
A program may use at most 320 MiB of HBM per device.

v0:
```python
import jax
import jax.numpy as jnp
from jax import lax
from jax.sharding import PartitionSpec as P

H = 18
KVH = 6
HD = 64
FF = 3072


EPSILON = 1e-05
ROTARY_BASE = 10000.0
MASKED_SCORE = -1e30


def rotary(values, positions, direction):
    half = values.shape[-1] // 2
    freqs = ROTARY_BASE ** (-2.0 * jnp.arange(half, dtype=jnp.float32) / values.shape[-1])
    angles = positions.astype(jnp.float32)[:, None] * freqs[None, :]
    cosine = jnp.cos(angles)[:, None, None, :]
    sine = direction * jnp.sin(angles)[:, None, None, :]
    first = values[..., :half]
    second = values[..., half:]
    return jnp.concatenate(
        [first * cosine - second * sine, second * cosine + first * sine], axis=-1
    )


def norm_scale(rows):
    return lax.rsqrt(jnp.mean(rows * rows, axis=-1, keepdims=True) + EPSILON)


def norm_back(rows, scale, gain, upstream):
    scaled = upstream * gain
    inward = scale * scaled - rows * scale**3 * jnp.mean(scaled * rows, axis=-1, keepdims=True)
    return (inward, jnp.sum(upstream * rows * scale, axis=0))


def forward_dot(left, right):
    return jnp.dot(left, right, preferred_element_type=jnp.float32)


def backward_dot(grad, weight):
    return jnp.einsum("rn,cn->rc", grad, weight, preferred_element_type=jnp.float32)


def over_pieces(step, carry, piece, width):
    count = piece.shape[0]
    parts = piece.reshape((count // width, width) + piece.shape[1:])
    starts = width * jnp.arange(count // width, dtype=jnp.int32)

    def inner(state, item):
        return (step(state, item[0], item[1]), None)

    carry, unused = lax.scan(inner, carry, (parts, starts))
    return carry


def on_device(
    tokens, w_query, w_key, w_value, w_out, w_gate, w_up, w_down, gain_attn, gain_ffn, cotangent
):
    block_len, seq_count, width = tokens.shape
    rows_count = block_len * seq_count
    groups = H // KVH
    kv_width = KVH * HD
    seq_len = block_len * lax.axis_size("ctx")
    own_weights = (w_query, w_key, w_value, w_out, w_gate, w_up, w_down, gain_attn, gain_ffn)
    (
        full_query,
        full_key,
        full_value,
        full_out,
        full_gate,
        full_up,
        full_down,
        full_gain_attn,
        full_gain_ffn,
    ) = (
        lax.all_gather(own_weights[0], "fsdp", axis=0, tiled=True),
        lax.all_gather(own_weights[1], "fsdp", axis=0, tiled=True),
        lax.all_gather(own_weights[2], "fsdp", axis=0, tiled=True),
        lax.all_gather(own_weights[3], "fsdp", axis=0, tiled=True),
        lax.all_gather(own_weights[4], "fsdp", axis=0, tiled=True),
        lax.all_gather(own_weights[5], "fsdp", axis=0, tiled=True),
        lax.all_gather(own_weights[6], "fsdp", axis=0, tiled=True),
        lax.all_gather(own_weights[7], "fsdp", axis=0, tiled=True),
        lax.all_gather(own_weights[8], "fsdp", axis=0, tiled=True),
    )
    my_start = lax.axis_index("ctx") * block_len
    my_last = my_start + block_len - 1
    positions = my_start + jnp.arange(block_len, dtype=jnp.int32)
    inputs = tokens.astype(jnp.float32).reshape(rows_count, width)
    scale_attn = norm_scale(inputs)
    normed_attn = (inputs * scale_attn * full_gain_attn.astype(jnp.float32)).astype(jnp.bfloat16)
    query_raw = forward_dot(normed_attn, full_query)
    key_raw = forward_dot(normed_attn, full_key)
    value_raw = forward_dot(normed_attn, full_value)
    queries = (
        rotary(query_raw.reshape(block_len, seq_count, H, HD), positions, 1.0)
        .astype(jnp.bfloat16)
        .reshape(block_len, seq_count, KVH, groups, HD)
    )
    keys_local = (
        rotary(key_raw.reshape(block_len, seq_count, KVH, HD), positions, 1.0)
        .astype(jnp.bfloat16)
        .reshape(block_len, seq_count, kv_width)
    )
    values_local = value_raw.astype(jnp.bfloat16).reshape(block_len, seq_count, kv_width)
    pairs = jnp.concatenate([keys_local, values_local], axis=-1)

    def split_piece(piece):
        count = piece.shape[0]
        keys = piece[..., :kv_width].reshape(count, seq_count, KVH, HD)
        values = piece[..., kv_width:].reshape(count, seq_count, KVH, HD)
        return (keys, values)

    def scores_of(keys, start):
        count = keys.shape[0]
        raw = jnp.einsum(
            "bskgd,pskd->skgbp", queries, keys, preferred_element_type=jnp.float32
        ) * HD ** (-0.5)
        valid = (start + jnp.arange(count, dtype=jnp.int32))[None, :] <= positions[:, None]
        return (jnp.where(valid, raw, MASKED_SCORE), valid)

    def stats_piece(carry, piece, start):
        row_max, row_total = carry
        keys, values = split_piece(piece)
        masked, valid = scores_of(keys, start)
        new_max = jnp.maximum(row_max, jnp.max(masked, axis=-1))
        weights = jnp.where(valid, jnp.exp(masked - new_max[..., None]), 0.0)
        return (new_max, row_total * jnp.exp(row_max - new_max) + jnp.sum(weights, axis=-1))

    stat_shape = (seq_count, KVH, groups, block_len)
    stat_start = (
        jnp.full(stat_shape, MASKED_SCORE, jnp.float32),
        jnp.zeros(stat_shape, jnp.float32),
    )
    piece = lax.all_gather(pairs, "ctx", axis=0, tiled=True)
    row_max, row_total = lax.cond(
        jnp.int32(0) <= my_last,
        lambda: over_pieces(stats_piece, stat_start, piece, block_len),
        lambda: stat_start,
    )
    log_total = row_max + jnp.log(row_total)

    def probs_of(keys, start):
        masked, valid = scores_of(keys, start)
        return jnp.where(valid, jnp.exp(masked - log_total[..., None]), 0.0)

    def mix_piece(carry, piece, start):
        mixed_low, mixed_rest = carry
        keys, values = split_piece(piece)
        probs = probs_of(keys, start)
        probs_high = probs.astype(jnp.bfloat16)
        probs_rest = (probs - probs_high.astype(jnp.float32)).astype(jnp.bfloat16)
        mixed_low = mixed_low + jnp.einsum(
            "skgbp,pskd->bskgd", probs_high, values, preferred_element_type=jnp.float32
        )
        mixed_rest = mixed_rest + jnp.einsum(
            "skgbp,pskd->bskgd", probs_rest, values, preferred_element_type=jnp.float32
        )
        return (mixed_low, mixed_rest)

    def mix_step(carry, piece, start):
        return lax.cond(
            start <= my_last, lambda: over_pieces(mix_piece, carry, piece, block_len), lambda: carry
        )

    mix_shape = (block_len, seq_count, KVH, groups, HD)
    mix_start = (jnp.zeros(mix_shape, jnp.float32), jnp.zeros(mix_shape, jnp.float32))
    mixed_low, mixed_rest = mix_step(
        mix_start, lax.all_gather(pairs, "ctx", axis=0, tiled=True), jnp.int32(0)
    )
    mixed_exact = mixed_low + mixed_rest
    attn_low = mixed_low.astype(jnp.bfloat16).reshape(rows_count, width)
    resid = inputs + forward_dot(attn_low, full_out)
    scale_ffn = norm_scale(resid)
    normed_ffn = (resid * scale_ffn * full_gain_ffn.astype(jnp.float32)).astype(jnp.bfloat16)
    gate = forward_dot(normed_ffn, full_gate)
    upward = forward_dot(normed_ffn, full_up)
    sigmoid_gate = jax.nn.sigmoid(gate)
    act_low = (gate * sigmoid_gate * upward).astype(jnp.bfloat16)
    layer_out = (
        (resid + forward_dot(act_low, full_down))
        .astype(jnp.bfloat16)
        .reshape(block_len, seq_count, width)
    )
    (
        full_query,
        full_key,
        full_value,
        full_out,
        full_gate,
        full_up,
        full_down,
        full_gain_attn,
        full_gain_ffn,
    ) = (
        lax.all_gather(own_weights[0], "fsdp", axis=0, tiled=True),
        lax.all_gather(own_weights[1], "fsdp", axis=0, tiled=True),
        lax.all_gather(own_weights[2], "fsdp", axis=0, tiled=True),
        lax.all_gather(own_weights[3], "fsdp", axis=0, tiled=True),
        lax.all_gather(own_weights[4], "fsdp", axis=0, tiled=True),
        lax.all_gather(own_weights[5], "fsdp", axis=0, tiled=True),
        lax.all_gather(own_weights[6], "fsdp", axis=0, tiled=True),
        lax.all_gather(own_weights[7], "fsdp", axis=0, tiled=True),
        lax.all_gather(own_weights[8], "fsdp", axis=0, tiled=True),
    )
    upstream_low = cotangent.reshape(rows_count, width)
    upstream = upstream_low.astype(jnp.float32)
    grad_act = backward_dot(upstream_low, full_down)
    grad_gate_low = (grad_act * upward * sigmoid_gate * (1.0 + gate * (1.0 - sigmoid_gate))).astype(
        jnp.bfloat16
    )
    grad_up_low = (grad_act * gate * sigmoid_gate).astype(jnp.bfloat16)
    grad_normed_ffn = backward_dot(grad_gate_low, full_gate) + backward_dot(grad_up_low, full_up)
    inward_ffn, gain_term_ffn = norm_back(
        resid, scale_ffn, full_gain_ffn.astype(jnp.float32), grad_normed_ffn
    )
    grad_resid = upstream + inward_ffn
    grad_branch = grad_resid.astype(jnp.bfloat16)
    grad_mix = (
        backward_dot(grad_branch, full_out)
        .astype(jnp.bfloat16)
        .reshape(block_len, seq_count, KVH, groups, HD)
    )
    deltas = jnp.transpose(
        jnp.sum(grad_mix.astype(jnp.float32) * mixed_exact, axis=-1), (1, 2, 3, 0)
    )

    def back_piece(carry, piece, start):
        grad_queries, grad_pairs = carry
        count = piece.shape[0]
        keys, values = split_piece(piece)
        probs = probs_of(keys, start)
        grad_probs = jnp.einsum(
            "bskgd,pskd->skgbp", grad_mix, values, preferred_element_type=jnp.float32
        )
        grad_scores = (probs * (grad_probs - deltas[..., None])).astype(jnp.bfloat16)
        grad_queries = grad_queries + HD ** (-0.5) * jnp.einsum(
            "skgbp,pskd->bskgd", grad_scores, keys, preferred_element_type=jnp.float32
        )
        grad_keys = HD ** (-0.5) * jnp.einsum(
            "skgbp,bskgd->pskd", grad_scores, queries, preferred_element_type=jnp.float32
        )
        grad_values = jnp.einsum(
            "skgbp,bskgd->pskd",
            probs.astype(jnp.bfloat16),
            grad_mix,
            preferred_element_type=jnp.float32,
        )
        update = jnp.concatenate(
            [
                grad_keys.reshape(count, seq_count, kv_width),
                grad_values.reshape(count, seq_count, kv_width),
            ],
            axis=-1,
        )
        current = lax.dynamic_slice_in_dim(grad_pairs, start, count, 0)
        return (
            grad_queries,
            lax.dynamic_update_slice_in_dim(grad_pairs, current + update, start, 0),
        )

    def back_step(carry, piece, start):
        return lax.cond(
            start <= my_last,
            lambda: over_pieces(back_piece, carry, piece, block_len),
            lambda: carry,
        )

    back_start = (
        jnp.zeros(mix_shape, jnp.float32),
        jnp.zeros((seq_len, seq_count, 2 * kv_width), jnp.float32),
    )
    grad_queries, grad_pairs = back_step(
        back_start, lax.all_gather(pairs, "ctx", axis=0, tiled=True), jnp.int32(0)
    )
    summed_pairs = lax.psum_scatter(
        grad_pairs.astype(jnp.bfloat16), "ctx", scatter_dimension=0, tiled=True
    ).astype(jnp.float32)
    grad_query_low = (
        rotary(grad_queries.reshape(block_len, seq_count, H, HD), positions, -1.0)
        .astype(jnp.bfloat16)
        .reshape(rows_count, width)
    )
    grad_key_low = (
        rotary(summed_pairs[..., :kv_width].reshape(block_len, seq_count, KVH, HD), positions, -1.0)
        .astype(jnp.bfloat16)
        .reshape(rows_count, kv_width)
    )
    grad_value_low = summed_pairs[..., kv_width:].astype(jnp.bfloat16).reshape(rows_count, kv_width)
    grad_normed_attn = (
        backward_dot(grad_query_low, full_query)
        + backward_dot(grad_key_low, full_key)
        + backward_dot(grad_value_low, full_value)
    )
    inward_attn, gain_term_attn = norm_back(
        inputs, scale_attn, full_gain_attn.astype(jnp.float32), grad_normed_attn
    )
    grad_tokens = (grad_resid + inward_attn).reshape(block_len, seq_count, width)

    def part(acts, grads):
        return jnp.einsum("rc,rn->cn", acts, grads, preferred_element_type=jnp.float32)

    row_shares = lax.psum_scatter(
        jnp.concatenate(
            [
                part(normed_attn, grad_query_low),
                part(normed_attn, grad_key_low),
                part(normed_attn, grad_value_low),
                part(attn_low, grad_branch),
                part(normed_ffn, grad_gate_low),
                part(normed_ffn, grad_up_low),
            ],
            axis=1,
        ).astype(jnp.bfloat16),
        "fsdp",
        scatter_dimension=0,
        tiled=True,
    )
    down_term = jnp.einsum("rc,rn->cn", act_low, upstream_low, preferred_element_type=jnp.float32)
    gain_term = jnp.stack([gain_term_attn, gain_term_ffn], axis=1)
    down_share, gain_share = (
        lax.psum_scatter(
            down_term.astype(jnp.bfloat16), "fsdp", scatter_dimension=0, tiled=True
        ).astype(jnp.float32),
        lax.psum_scatter(
            gain_term.astype(jnp.bfloat16), "fsdp", scatter_dimension=0, tiled=True
        ).astype(jnp.float32),
    )
    row_total, down_total, gain_total = (
        lax.psum(row_shares, "ctx").astype(jnp.float32),
        lax.psum(down_share.astype(jnp.bfloat16), "ctx").astype(jnp.float32),
        lax.psum(gain_share.astype(jnp.bfloat16), "ctx").astype(jnp.float32),
    )
    edges = [
        0,
        width,
        width + kv_width,
        width + 2 * kv_width,
        2 * width + 2 * kv_width,
        2 * width + 2 * kv_width + FF,
        2 * width + 2 * kv_width + 2 * FF,
    ]
    grad_query = row_total[:, edges[0] : edges[1]]
    grad_key = row_total[:, edges[1] : edges[2]]
    grad_value = row_total[:, edges[2] : edges[3]]
    grad_out = row_total[:, edges[3] : edges[4]]
    grad_gate = row_total[:, edges[4] : edges[5]]
    grad_up = row_total[:, edges[5] : edges[6]]
    return (
        layer_out,
        grad_tokens,
        grad_query,
        grad_key,
        grad_value,
        grad_out,
        grad_gate,
        grad_up,
        down_total,
        gain_total[:, 0],
        gain_total[:, 1],
    )


def solution(mesh):
    return jax.shard_map(
        on_device,
        mesh=mesh,
        in_specs=(
            P("ctx", "fsdp", None),
            P("fsdp", None),
            P("fsdp", None),
            P("fsdp", None),
            P("fsdp", None),
            P("fsdp", None),
            P("fsdp", None),
            P("fsdp", None),
            P("fsdp"),
            P("fsdp"),
            P("ctx", "fsdp", None),
        ),
        out_specs=(
            P("ctx", "fsdp", None),
            P("ctx", "fsdp", None),
            P("fsdp", None),
            P("fsdp", None),
            P("fsdp", None),
            P("fsdp", None),
            P("fsdp", None),
            P("fsdp", None),
            P("fsdp", None),
            P("fsdp"),
            P("fsdp"),
        ),
        check_vma=False,
    )
```

profile of v0, /device:TPU:0, one launch (start us, length us, event | category | flops | bytes accessed | tf_op | source)
XLA Modules:
  0.0 1086.4 jit_solution(4990392299612830215)
XLA Ops:
  11.8 9.1 all-reduce.3
  21.8 13.9 %all_gather.43 = bf16[1152,384]{1,0:T(8,128)(2,1)S(1)} all-gather(bf16[288,384]{1,0:T(8,128)(2,1)S(1)} %copy-done.43), channel_id=1, replica_groups=mesh['fsdp'=4,'ctx'=8] {'fsdp'}, dimensions={0}, use_global_device_ids=true | all-gather | bytes 1105920 | tf_op jit(solution)/shard_map/all_gather | solution.py:82
  38.0 9.2 all_gather.42
  61.6 52.1 %all-gather.7.cloned.1.call-done = bf16[1024,2,768]{2,0,1:T(8,128)(2,1)} async-done(((bf16[128,2,768]{2,0,1:T(8,128)(2,1)}), bf16[1024,2,768]{2,0,1:T(8,128)(2,1)}) %all-gather.7.cloned.1.call-update) | async-done | bytes 3145744 | tf_op jit(solution)/shard_map/all_gather | solution.py:173
  113.6 46.3 %conditional.3 = (f32[2,6,3,128]{3,2,1,0:T(4,128)}, f32[2,6,3,128]{3,2,1,0:T(4,128)S(1)}) conditional(s32[]{:T(128)} %convert_element_type.148, () %tuple.55, (bf16[1024,2,768]{2,0,1:T(8,128)(2,1)}, s32[128]{0:T(128)S(1)}, bf16[128,2,6,3,64]{0,4,3,2,1:T(8,128)(2,1)S(1)}) %tuple.56), branch_computations={%region_1.0_spmd, %region_2.7_spmd} | conditional | flops 80255624 | bytes 7798532 | solution.py:140
  113.6 46.3 %while.40 = (s32[]{:T(128)}, f32[2,6,3,128]{3,2,1,0:T(4,128)}, f32[2,6,3,128]{3,2,1,0:T(4,128)S(1)}, s32[8]{0:T(128)S(1)}, s32[128]{0:T(128)S(1)}, /*index=5*/bf...) while((s32[]{:T(128)}, f32[2,6,3,128]{3,2,1,0:T(4,128)}, ...), condition=%wide.region_6.6_spmd.clone, body=%wide.region_3.5_spmd.clone.sunk | while | flops 80255616 | bytes 7761540 | solution.py:56
  161.3 77.7 %conditional.4 = (f32[128,2,6,3,64]{0,4,3,2,1:T(8,128)}, f32[128,2,6,3,64]{0,4,3,2,1:T(8,128)}, bf16[256,1152]{1,0:T(8,128)(2,1)}) conditional(s32[]{:T(128)} %convert_element_type.148, () %tuple.54, (bf16[1024,2,768]{2,0,1:T(8,128)(2,1)}, s32[128]{0:T(128)S(1)}, bf16[128,2,6,3,64]{0,4,3,2,1:T(8,128)(2,1)S(1)}, f32[2,6,3,128]{3,2,1,0:T(4,128)}) %tuple.57), branch_computations={%region_7.8_spmd, %region_8.11_spmd} | conditional | flops 233291904 | bytes 19517212 | solution.py:166
  161.3 73.0 %while.41 = (s32[]{:T(128)}, f32[128,2,6,3,64]{0,4,3,2,1:T(8,128)}, f32[128,2,6,3,64]{0,4,3,2,1:T(8,128)}, bf16[8,128,2,768]{3,1,0,2:T(8,128)(2,1)}, s32[8]{0:T(...) while((s32[]{:T(128)}, f32[128,2,6,3,64]{0,4,3,2,1:T(8,128)}, ...), condition=%wide.region_10.10_spmd.clone, body=%wide.region_9.9_spmd.clone.sunk | while | flops 232996992 | bytes 15388300 | solution.py:56
  243.2 7.1 fusion.41
  250.3 7.7 fusion.42
  258.0 38.5 %all-gather.17.cloned.1.call-done = bf16[3072,1152]{1,0:T(8,128)(2,1)} async-done(((bf16[768,1152]{1,0:T(8,128)(2,1)}), bf16[3072,1152]{1,0:T(8,128)(2,1)}) %all-gather.17.cloned.1.call-update) | async-done | bytes 7077904 | tf_op jit(solution)/shard_map/all_gather | solution.py:86
  296.5 10.2 multiply_convert_fusion
  306.7 6.4 fusion.43
  325.3 177.7 %conditional.5 = (f32[1024,2,768]{0,2,1:T(8,128)}, f32[128,2,18,32]{0,3,2,1:T(8,128)}, f32[128,2,18,32]{0,3,2,1:T(8,128)}) conditional(s32[]{:T(128)} %convert_element_type.148, () %tuple.58, (bf16[1024,2,768]{2,0,1:T(8,128)(2,1)}, s32[128]{0:T(128)}, bf16[128,2,6,3,64]{0,4,3,2,1:T(8,128)(2,1)S(1)}, f32[2,6,3,128]{3,2,1,0:T(4,128)}, ...), branch_computations={%region_14.15_spmd, %region_15.18_spmd} | conditional | flops 383598720 | bytes 44812660 | solution.py:267
  333.0 167.6 %while.42 = (s32[]{:T(128)}, f32[128,2,6,3,64]{0,4,3,2,1:T(8,128)}, f32[1024,2,768]{0,2,1:T(8,128)}, bf16[8,128,2,768]{3,1,0,2:T(8,128)(2,1)}, s32[8]{0:T(128)S(...) while((s32[]{:T(128)}, f32[128,2,6,3,64]{0,4,3,2,1:T(8,128)}, ...), condition=%wide.region_17.17_spmd.clone, body=%wide.region_16.16_spmd.clone.sunk | while | flops 383598720 | bytes 34945224 | solution.py:56
  390.2 5.7 dynamic_update_slice.5
  474.6 5.7 dynamic_update_slice.5
  536.6 47.1 %reduce-scatter.13.cloned.1.call-done = bf16[128,1536]{1,0:T(8,128)(2,1)} async-done(((bf16[1024,1536]{1,0:T(8,128)(2,1)}), bf16[128,1536]{1,0:T(8,128)(2,1)}) %reduce-scatter.13.cloned.1.call-update) | async-done | bytes 393232
  614.9 34.1 %reduce-scatter.11.cloned.1.call-done = bf16[768,1152]{1,0:T(8,128)(2,1)} async-done(((bf16[3072,1152]{1,0:T(8,128)(2,1)}), bf16[768,1152]{1,0:T(8,128)(2,1)}) %reduce-scatter.11.cloned.1.call-update) | async-done | bytes 1769488 | tf_op jit(solution)/shard_map/reduce_scatter | solution.py:326
  648.9 157.6 %reduce-scatter.9.cloned.1.call-done = bf16[288,9216]{1,0:T(8,128)(2,1)} async-done(((bf16[1152,9216]{1,0:T(8,128)(2,1)}), bf16[288,9216]{1,0:T(8,128)(2,1)}) %reduce-scatter.9.cloned.1.call-update) | async-done | bytes 5308432 | tf_op jit(solution)/shard_map/reduce_scatter | solution.py:307
  807.8 6.5 fusion.22
  821.9 7.9 reduce-scatter.15.cloned.1.call-done
  830.7 21.9 %psum.23 = bf16[288,2]{0,1:T(2,128)(2,1)S(1)} all-reduce(bf16[288,2]{0,1:T(2,128)(2,1)S(1)} %copy.141), channel_id=1, replica_groups=mesh['fsdp'=4,'ctx'=8] {'ctx'}, use_global_device_ids=true, to_apply=%region_27.28 | all-reduce | flops 576 | bytes 2304 | tf_op jit(solution)/shard_map/psum | solution.py:336
  853.2 215.8 %all-reduce.6.cloned.1.call-done = (bf16[288,9216]{1,0:T(8,128)(2,1)}, bf16[768,1152]{1,0:T(8,128)(2,1)}) async-done(((bf16[288,9216]{1,0:T(8,128)(2,1)}, bf16[768,1152]{1,0:T(8,128)(2,1)}), (bf16[288,9216]{1,0:T(8,128)(2,1)}, bf16[768,1152]{1,0:T(8,128)(2,1)})) %all-reduce.6.cloned.1.call-update) | async-done | bytes 7077904 | tf_op jit(solution)/shard_map/psum | solution.py:334
  (659 shorter events, 396.5 us)
Async XLA Ops:
  7.2 13.7 %copy-start.14 = (bf16[128,2,1152]{2,1,0:T(2,128)(2,1)S(1)}, bf16[128,2,1152]{2,1,0:T(2,128)(2,1)}, u32[]{:S(2)}) copy-start(bf16[128,2,1152]{2,1,0:T(2,128)(2,1)} %param.23) | copy-start | bytes 1769476
  7.2 14.6 %copy-start.43 = (bf16[288,384]{1,0:T(8,128)(2,1)S(1)}, bf16[288,384]{1,0:T(8,128)(2,1)}, u32[]{:S(2)}) copy-start(bf16[288,384]{1,0:T(8,128)(2,1)} %param.26) | copy-start | bytes 663556
  7.2 48.8 %all-gather.9.cloned.1.call-start = ((), (), s32[]{:S(2)}) async-start(), calls=%async_computation.5 | async-start | bytes 3317760 | tf_op jit(solution)/shard_map/all_gather | solution.py:80
  8.0 105.7 %all-gather.7.cloned.1.call-start = ((), (), s32[]{:S(2)}) async-start(), calls=%async_computation.4 | async-start | bytes 3538944 | tf_op jit(solution)/shard_map/all_gather | solution.py:173
  9.9 41.0 %copy-start.5 = (f32[256,1152]{1,0:T(8,128)}, f32[256,1152]{1,0:T(8,128)S(1)}, u32[]{:S(2)}) copy-start(f32[256,1152]{1,0:T(8,128)S(1)} %reshape.326) | copy-start | bytes 3538948
  20.9 14.8 %copy-start.40 = (f32[1152]{0:T(1024)}, f32[1152]{0:T(1024)S(1)}, u32[]{:S(2)}) copy-start(f32[1152]{0:T(1024)S(1)} %convert_element_type.149) | copy-start | bytes 13828
  21.6 15.6 %copy-start.31 = (f32[128,2]{1,0:T(8,128)}, f32[128,2]{1,0:T(8,128)S(1)}, u32[]{:S(2)}) copy-start(f32[128,2]{1,0:T(8,128)S(1)} %add_rsqrt_fusion) | copy-start | bytes 3076
  21.8 15.4 %copy-start.51 = (f32[256]{0:T(256)}, f32[256]{0:T(256)S(1)}, u32[]{:S(2)}) copy-start(f32[256]{0:T(256)S(1)} %rsqrt.27) | copy-start | bytes 3076
  52.4 186.6 %all-gather.11.cloned.1.call-start = ((), (), s32[]{:S(2)}) async-start(), calls=%async_computation.6 | async-start | bytes 3317760 | tf_op jit(solution)/shard_map/all_gather | solution.py:83
  53.1 190.0 %all-gather.13.cloned.1.call-start = ((), (), s32[]{:S(2)}) async-start(), calls=%async_computation.7 | async-start | bytes 8847360 | tf_op jit(solution)/shard_map/all_gather | solution.py:84
  53.7 196.5 %all-gather.15.cloned.1.call-start = ((), (), s32[]{:S(2)}) async-start(), calls=%async_computation.8 | async-start | bytes 8847360 | tf_op jit(solution)/shard_map/all_gather | solution.py:85
  54.3 242.2 %all-gather.17.cloned.1.call-start = ((), (), s32[]{:S(2)}) async-start(), calls=%async_computation.9 | async-start | bytes 8847360 | tf_op jit(solution)/shard_map/all_gather | solution.py:86
  54.9 528.8 %reduce-scatter.13.cloned.1.call-start = ((), (), s32[]{:S(2)}) async-start(), calls=%async_computation.12 | async-start | bytes 3538944
  55.0 188.0 %copy-start.49 = (f32[1152]{0:T(1024)}, f32[1152]{0:T(1024)S(1)}, u32[]{:S(2)}) copy-start(f32[1152]{0:T(1024)S(1)} %convert_element_type.155) | copy-start | bytes 13828
  56.0 105.3 %copy-start.48 = (s32[128]{0:T(128)}, s32[128]{0:T(128)S(1)}, u32[]{:S(2)}) copy-start(s32[128]{0:T(128)S(1)} %iota_add_fusion.3) | copy-start | bytes 1540
  242.3 73.9 %copy-start.10 = (f32[256,1152]{1,0:T(8,128)}, f32[256,1152]{1,0:T(8,128)S(1)}, u32[]{:S(2)}) copy-start(f32[256,1152]{1,0:T(8,128)S(1)} %get-tuple-element.493) | copy-start | bytes 3538948
  243.0 70.2 %copy-start.54 = (f32[256]{0:T(256)}, f32[256]{0:T(256)S(1)}, u32[]{:S(2)}) copy-start(f32[256]{0:T(256)S(1)} %get-tuple-element.491) | copy-start | bytes 3076
  250.2 46.2 %copy-start.20 = (bf16[256,1152]{1,0:T(8,128)(2,1)S(1)}, bf16[256,1152]{1,0:T(8,128)(2,1)}, u32[]{:S(2)}) copy-start(bf16[256,1152]{1,0:T(8,128)(2,1)} %reshape.329) | copy-start | bytes 1769476
  472.8 7.5 copy-start.3
  472.8 7.5 copy-start.62
  509.2 139.7 %reduce-scatter.11.cloned.1.call-start = ((), (), s32[]{:S(2)}) async-start(), calls=%async_computation.11 | async-start | bytes 8847360 | tf_op jit(solution)/shard_map/reduce_scatter | solution.py:326
  516.0 290.6 %reduce-scatter.9.cloned.1.call-start = ((), (), s32[]{:S(2)}) async-start(), calls=%async_computation.10 | async-start | bytes 26542080 | tf_op jit(solution)/shard_map/reduce_scatter | solution.py:307
  606.0 223.8 %reduce-scatter.15.cloned.1.call-start = ((), (), s32[]{:S(2)}) async-start(), calls=%async_computation.13 | async-start | bytes 368640
  614.8 454.2 %all-reduce.6.cloned.1.call-start = ((), (), s32[]{:S(2)}) async-start(), calls=%async_computation.14 | async-start | bytes 14155776 | tf_op jit(solution)/shard_map/psum | solution.py:334
  (118 other events, 389.0 us)
Sparse Core Ops, SparseCore 0:
  9.6 33.1 all-gather.8
  52.5 61.0 all-gather.6
  115.2 24.3 all-gather.10
  141.0 50.8 all-gather.12
  193.3 50.8 all-gather.14
  245.6 50.8 all-gather.16
  509.3 74.2 reduce-scatter.12
  586.2 62.7 reduce-scatter.10
  651.7 154.7 reduce-scatter.8
  809.5 20.2 reduce-scatter.14
  834.3 234.6 all-reduce.5
where the time goes:
time: 1100 us; the launch traced here: 1090 us
  waiting for transfers between devices  556 us (51%)
  matrix products  193 us (18%)
  local copies, waits for them, and re-layouts  175 us (16%)
  other arithmetic  73.5 us (7%)
  blocking collectives  54.1 us (5%)
  loops' own time  17.8 us (2%)
  between operations  15.6 us (1%)
    psum x1, waiting for transfers between devices, on_device(): lax.psum(row_shares, 'ctx').astype(jnp.float32)  216 us
    reduce_scatter x1, waiting for transfers between devices, on_device(): lax.psum_scatter(jnp.concatenate([part(normed_attn, grad_query_low), part...  158 us
    unnamed x13, waiting for transfers between devices  58 us
    all_gather x1, waiting for transfers between devices, on_device(): lax.all_gather(pairs, 'ctx', axis=0, tiled=True)  52.1 us
    dynamic_slice x72, local copies, waits for them, and re-layouts, over_pieces(): carry, unused = lax.scan(inner, carry, (parts, starts))  45.8 us
    dynamic_update_slice x8, local copies, waits for them, and re-layouts, back_piece(): lax.dynamic_update_slice_in_dim(grad_pairs, current + update, start, 0)  45 us
    all_gather x1, waiting for transfers between devices, on_device(): lax.all_gather(own_weights[6], 'fsdp', axis=0, tiled=True)  38.5 us
    reduce_scatter x1, waiting for transfers between devices, on_device(): lax.psum_scatter(down_term.astype(jnp.bfloat16), 'fsdp', scatter_dimensio...  34.1 us
  transfers between devices with their start and end apart: 11, of which 7 were waited for; matrix products, arithmetic and copies ran while one was open for 21% of the time, Pallas kernels for 0%

commit v1 on v0

v1 whole, which is shorter than its diff:
```python
import jax
import jax.numpy as jnp
from jax import lax
from jax.experimental import pallas as pl
from jax.experimental.pallas import tpu as pltpu
from jax.sharding import PartitionSpec as P

H = 18
KVH = 6
HD = 64
FF = 3072


EPSILON = 1e-05
ROTARY_BASE = 10000.0
MASKED_SCORE = -1e30


def rotary(values, positions, direction):
    half = values.shape[-1] // 2
    freqs = ROTARY_BASE ** (-2.0 * jnp.arange(half, dtype=jnp.float32) / values.shape[-1])
    angles = positions.astype(jnp.float32)[:, None] * freqs[None, :]
    cosine = jnp.cos(angles)[:, None, None, :]
    sine = direction * jnp.sin(angles)[:, None, None, :]
    first = values[..., :half]
    second = values[..., half:]
    return jnp.concatenate(
        [first * cosine - second * sine, second * cosine + first * sine], axis=-1
    )


def norm_scale(rows):
    return lax.rsqrt(jnp.mean(rows * rows, axis=-1, keepdims=True) + EPSILON)


def norm_back(rows, scale, gain, upstream):
    scaled = upstream * gain
    inward = scale * scaled - rows * scale**3 * jnp.mean(scaled * rows, axis=-1, keepdims=True)
    return (inward, jnp.sum(upstream * rows * scale, axis=0))


def forward_dot(left, right):
    return jnp.dot(left, right, preferred_element_type=jnp.float32)


def backward_dot(grad, weight):
    return jnp.einsum("rn,cn->rc", grad, weight, preferred_element_type=jnp.float32)


def attend_kernel(q_ref, kv_ref, mix_ref, log_ref):
    me = lax.axis_index("ctx")
    units, deep, wide = q_ref.shape
    keys = kv_ref.shape[2]

    def unit_step(unit, unused):
        q = q_ref[unit]

        def attend(block, top, total, mixed, diagonal):
            kv = kv_ref[block, unit]
            scores = jnp.dot(kv, q, preferred_element_type=jnp.float32)
            if diagonal:
                key_at = lax.broadcasted_iota(jnp.int32, scores.shape, 0)
                query_at = lax.rem(lax.broadcasted_iota(jnp.int32, scores.shape, 1), keys)
                scores = jnp.where(key_at <= query_at, scores, MASKED_SCORE)
            new_top = jnp.maximum(top, jnp.max(scores, axis=0, keepdims=True))
            fade = jnp.exp(top - new_top)
            weights = jnp.exp(scores - new_top)
            total = total * fade + jnp.sum(weights, axis=0, keepdims=True)
            added = jnp.dot(
                kv.T, weights.astype(jnp.bfloat16), preferred_element_type=jnp.float32
            )
            return new_top, total, mixed * fade + added[HD:]

        state = (
            jnp.full((1, wide), MASKED_SCORE, jnp.float32),
            jnp.zeros((1, wide), jnp.float32),
            jnp.zeros((HD, wide), jnp.float32),
        )
        state = attend(me, *state, True)
        top, total, mixed = lax.fori_loop(
            0, me, lambda block, state: attend(block, *state, False), state
        )
        mix_ref[unit] = mixed / total
        log_ref[unit] = top + jnp.log(total)
        return unused

    lax.fori_loop(0, units, unit_step, 0)


def attend_back_kernel(q_ref, g_ref, qg_ref, kv_ref, mix_ref, log_ref, grad_q_ref, grad_kv_ref):
    me = lax.axis_index("ctx")
    units, deep, wide = q_ref.shape
    blocks, _, keys, _ = kv_ref.shape

    def clear(block, unused):
        grad_kv_ref[block] = jnp.zeros(grad_kv_ref.shape[1:], grad_kv_ref.dtype)
        return unused

    lax.fori_loop(me + 1, blocks, clear, 0)

    def unit_step(unit, unused):
        q, g, qg, log_total = q_ref[unit], g_ref[unit], qg_ref[unit], log_ref[unit]
        delta = jnp.sum(g[HD:].astype(jnp.float32) * mix_ref[unit], axis=0, keepdims=True)

        def back(block, grad_q, diagonal):
            kv = kv_ref[block, unit]
            scores = jnp.dot(kv, q, preferred_element_type=jnp.float32)
            probs = jnp.exp(scores - log_total)
            if diagonal:
                key_at = lax.broadcasted_iota(jnp.int32, scores.shape, 0)
                query_at = lax.rem(lax.broadcasted_iota(jnp.int32, scores.shape, 1), keys)
                probs = jnp.where(key_at <= query_at, probs, 0.0)
            grad_probs = jnp.dot(kv, g, preferred_element_type=jnp.float32)
            grad_scores = (probs * (grad_probs - delta)).astype(jnp.bfloat16)
            both = jnp.concatenate([grad_scores, probs.astype(jnp.bfloat16)], axis=1)
            grad_kv_ref[block, unit] = jnp.dot(
                both, qg, preferred_element_type=jnp.float32
            ).astype(grad_kv_ref.dtype)
            added = jnp.dot(kv.T, grad_scores, preferred_element_type=jnp.float32)
            return grad_q + added[:HD]

        grad_q = back(me, jnp.zeros((HD, wide), jnp.float32), True)
        grad_q = lax.fori_loop(0, me, lambda block, held: back(block, held, False), grad_q)
        grad_q_ref[unit] = grad_q * HD ** (-0.5)
        return unused

    lax.fori_loop(0, units, unit_step, 0)


def call(kernel, outs, *args):
    return pl.pallas_call(
        kernel,
        out_shape=outs,
        in_specs=[pl.BlockSpec(memory_space=pltpu.VMEM)] * len(args),
        out_specs=[pl.BlockSpec(memory_space=pltpu.VMEM)] * len(outs),
        compiler_params=pltpu.CompilerParams(vmem_limit_bytes=56 << 20),
    )(*args)


def unit_columns(rows, seq_count, block_len):
    groups = H // KVH
    split = rows.reshape(block_len, seq_count, KVH, groups, HD)
    return jnp.transpose(split, (1, 2, 4, 3, 0)).reshape(
        seq_count * KVH, HD, groups * block_len
    )


def unit_rows(columns, seq_count, block_len):
    groups = H // KVH
    split = columns.reshape(seq_count, KVH, HD, groups, block_len)
    return jnp.transpose(split, (4, 0, 1, 3, 2)).reshape(block_len * seq_count, H * HD)


def on_device(
    tokens, w_query, w_key, w_value, w_out, w_gate, w_up, w_down, gain_attn, gain_ffn, cotangent
):
    block_len, seq_count, width = tokens.shape
    rows_count = block_len * seq_count
    groups = H // KVH
    kv_width = KVH * HD
    own_weights = (w_query, w_key, w_value, w_out, w_gate, w_up, w_down, gain_attn, gain_ffn)
    (
        full_query,
        full_key,
        full_value,
        full_out,
        full_gate,
        full_up,
        full_down,
        full_gain_attn,
        full_gain_ffn,
    ) = (
        lax.all_gather(own_weights[0], "fsdp", axis=0, tiled=True),
        lax.all_gather(own_weights[1], "fsdp", axis=0, tiled=True),
        lax.all_gather(own_weights[2], "fsdp", axis=0, tiled=True),
        lax.all_gather(own_weights[3], "fsdp", axis=0, tiled=True),
        lax.all_gather(own_weights[4], "fsdp", axis=0, tiled=True),
        lax.all_gather(own_weights[5], "fsdp", axis=0, tiled=True),
        lax.all_gather(own_weights[6], "fsdp", axis=0, tiled=True),
        lax.all_gather(own_weights[7], "fsdp", axis=0, tiled=True),
        lax.all_gather(own_weights[8], "fsdp", axis=0, tiled=True),
    )
    my_start = lax.axis_index("ctx") * block_len
    positions = my_start + jnp.arange(block_len, dtype=jnp.int32)
    inputs = tokens.astype(jnp.float32).reshape(rows_count, width)
    scale_attn = norm_scale(inputs)
    normed_attn = (inputs * scale_attn * full_gain_attn.astype(jnp.float32)).astype(jnp.bfloat16)
    query_raw = forward_dot(normed_attn, full_query)
    key_raw = forward_dot(normed_attn, full_key)
    value_raw = forward_dot(normed_attn, full_value)
    units = seq_count * KVH
    wide = groups * block_len
    queries = (
        rotary(query_raw.reshape(block_len, seq_count, H, HD), positions, 1.0)
        .astype(jnp.bfloat16)
        .reshape(rows_count, width)
    )
    keys_local = rotary(
        key_raw.reshape(block_len, seq_count, KVH, HD), positions, 1.0
    ).astype(jnp.bfloat16)
    values_local = value_raw.astype(jnp.bfloat16).reshape(block_len, seq_count, KVH, HD)
    pairs = jnp.transpose(
        jnp.concatenate([keys_local, values_local], axis=-1), (1, 2, 0, 3)
    ).reshape(units, block_len, 2 * HD)
    all_pairs = lax.all_gather(pairs, "ctx", axis=0)
    q_unit = unit_columns(queries * jnp.bfloat16(HD ** (-0.5)), seq_count, block_len)
    q_wide = jnp.concatenate([q_unit, jnp.zeros_like(q_unit)], axis=1)
    mix_unit, log_total = call(
        attend_kernel,
        [
            jax.ShapeDtypeStruct((units, HD, wide), jnp.float32),
            jax.ShapeDtypeStruct((units, 1, wide), jnp.float32),
        ],
        q_wide,
        all_pairs,
    )
    attn_low = unit_rows(mix_unit.astype(jnp.bfloat16), seq_count, block_len)
    resid = inputs + forward_dot(attn_low, full_out)
    scale_ffn = norm_scale(resid)
    normed_ffn = (resid * scale_ffn * full_gain_ffn.astype(jnp.float32)).astype(jnp.bfloat16)
    gate = forward_dot(normed_ffn, full_gate)
    upward = forward_dot(normed_ffn, full_up)
    sigmoid_gate = jax.nn.sigmoid(gate)
    act_low = (gate * sigmoid_gate * upward).astype(jnp.bfloat16)
    layer_out = (
        (resid + forward_dot(act_low, full_down))
        .astype(jnp.bfloat16)
        .reshape(block_len, seq_count, width)
    )
    upstream_low = cotangent.reshape(rows_count, width)
    upstream = upstream_low.astype(jnp.float32)
    grad_act = backward_dot(upstream_low, full_down)
    grad_gate_low = (grad_act * upward * sigmoid_gate * (1.0 + gate * (1.0 - sigmoid_gate))).astype(
        jnp.bfloat16
    )
    grad_up_low = (grad_act * gate * sigmoid_gate).astype(jnp.bfloat16)
    grad_normed_ffn = backward_dot(grad_gate_low, full_gate) + backward_dot(grad_up_low, full_up)
    inward_ffn, gain_term_ffn = norm_back(
        resid, scale_ffn, full_gain_ffn.astype(jnp.float32), grad_normed_ffn
    )
    grad_resid = upstream + inward_ffn
    grad_branch = grad_resid.astype(jnp.bfloat16)
    grad_mix = backward_dot(grad_branch, full_out).astype(jnp.bfloat16)
    g_unit = unit_columns(grad_mix, seq_count, block_len)
    g_wide = jnp.concatenate([jnp.zeros_like(g_unit), g_unit], axis=1)
    q_rows, g_rows = jnp.swapaxes(q_unit, 1, 2), jnp.swapaxes(g_unit, 1, 2)
    blank = jnp.zeros_like(q_rows)
    qg = jnp.concatenate(
        [jnp.concatenate([q_rows, blank], axis=2), jnp.concatenate([blank, g_rows], axis=2)],
        axis=1,
    )
    grad_q_unit, grad_pairs = call(
        attend_back_kernel,
        [
            jax.ShapeDtypeStruct((units, HD, wide), jnp.float32),
            jax.ShapeDtypeStruct(all_pairs.shape, jnp.bfloat16),
        ],
        q_wide,
        g_wide,
        qg,
        all_pairs,
        mix_unit,
        log_total,
    )
    summed_pairs = lax.psum_scatter(grad_pairs, "ctx", scatter_dimension=0, tiled=True)
    summed_pairs = jnp.transpose(
        summed_pairs.reshape(seq_count, KVH, block_len, 2 * HD), (2, 0, 1, 3)
    )
    grad_query_low = (
        rotary(
            unit_rows(grad_q_unit, seq_count, block_len).reshape(block_len, seq_count, H, HD),
            positions,
            -1.0,
        )
        .astype(jnp.bfloat16)
        .reshape(rows_count, width)
    )
    grad_key_low = (
        rotary(summed_pairs[..., :HD].astype(jnp.float32), positions, -1.0)
        .astype(jnp.bfloat16)
        .reshape(rows_count, kv_width)
    )
    grad_value_low = summed_pairs[..., HD:].reshape(rows_count, kv_width)
    grad_normed_attn = (
        backward_dot(grad_query_low, full_query)
        + backward_dot(grad_key_low, full_key)
        + backward_dot(grad_value_low, full_value)
    )
    inward_attn, gain_term_attn = norm_back(
        inputs, scale_attn, full_gain_attn.astype(jnp.float32), grad_normed_attn
    )
    grad_tokens = (grad_resid + inward_attn).reshape(block_len, seq_count, width)

    def part(acts, grads):
        return jnp.einsum("rc,rn->cn", acts, grads, preferred_element_type=jnp.float32)

    row_shares = lax.psum_scatter(
        jnp.concatenate(
            [
                part(normed_attn, grad_query_low),
                part(normed_attn, grad_key_low),
                part(normed_attn, grad_value_low),
                part(attn_low, grad_branch),
                part(normed_ffn, grad_gate_low),
                part(normed_ffn, grad_up_low),
            ],
            axis=1,
        ).astype(jnp.bfloat16),
        "fsdp",
        scatter_dimension=0,
        tiled=True,
    )
    down_term = jnp.einsum("rc,rn->cn", act_low, upstream_low, preferred_element_type=jnp.float32)
    gain_term = jnp.stack([gain_term_attn, gain_term_ffn], axis=1)
    down_share, gain_share = (
        lax.psum_scatter(
            down_term.astype(jnp.bfloat16), "fsdp", scatter_dimension=0, tiled=True
        ).astype(jnp.float32),
        lax.psum_scatter(
            gain_term.astype(jnp.bfloat16), "fsdp", scatter_dimension=0, tiled=True
        ).astype(jnp.float32),
    )
    row_total, down_total, gain_total = (
        lax.psum(row_shares, "ctx").astype(jnp.float32),
        lax.psum(down_share.astype(jnp.bfloat16), "ctx").astype(jnp.float32),
        lax.psum(gain_share.astype(jnp.bfloat16), "ctx").astype(jnp.float32),
    )
    edges = [
        0,
        width,
        width + kv_width,
        width + 2 * kv_width,
        2 * width + 2 * kv_width,
        2 * width + 2 * kv_width + FF,
        2 * width + 2 * kv_width + 2 * FF,
    ]
    grad_query = row_total[:, edges[0] : edges[1]]
    grad_key = row_total[:, edges[1] : edges[2]]
    grad_value = row_total[:, edges[2] : edges[3]]
    grad_out = row_total[:, edges[3] : edges[4]]
    grad_gate = row_total[:, edges[4] : edges[5]]
    grad_up = row_total[:, edges[5] : edges[6]]
    return (
        layer_out,
        grad_tokens,
        grad_query,
        grad_key,
        grad_value,
        grad_out,
        grad_gate,
        grad_up,
        down_total,
        gain_total[:, 0],
        gain_total[:, 1],
    )


def solution(mesh):
    return jax.shard_map(
        on_device,
        mesh=mesh,
        in_specs=(
            P("ctx", "fsdp", None),
            P("fsdp", None),
            P("fsdp", None),
            P("fsdp", None),
            P("fsdp", None),
            P("fsdp", None),
            P("fsdp", None),
            P("fsdp", None),
            P("fsdp"),
            P("fsdp"),
            P("ctx", "fsdp", None),
        ),
        out_specs=(
            P("ctx", "fsdp", None),
            P("ctx", "fsdp", None),
            P("fsdp", None),
            P("fsdp", None),
            P("fsdp", None),
            P("fsdp", None),
            P("fsdp", None),
            P("fsdp", None),
            P("fsdp", None),
            P("fsdp"),
            P("fsdp"),
        ),
        check_vma=False,
    )
```

time: 1100 us -> 976 us (0.89)
  waiting for transfers between devices: 556 us -> 667 us
  matrix products: 193 us -> 91.8 us
  local copies, waits for them, and re-layouts: 175 us -> 98.5 us
  other arithmetic: 73.5 us -> 20.2 us
  Pallas kernels: 0 us -> 18.6 us
  loops' own time: 17.8 us -> 0 us
    dot_general x72 -> x0, matrix products: 120 us -> none  [the longest x24 28.2 us: scores_of(): jnp.einsum('bskgd,pskd->skgbp', queries, keys, preferred_element_type=jnp...]
    reduce_scatter x0 -> x1, waiting for transfers between devices: none -> 66.4 us  [on_device(): lax.psum_scatter(grad_pairs, 'ctx', scatter_dimension=0, tiled=True)]
    all_gather x1, waiting for transfers between devices: 0.02 us -> 47.2 us  [on_device(): lax.all_gather(own_weights[4], 'fsdp', axis=0, tiled=True)]
    dynamic_slice x72 -> x0, local copies, waits for them, and re-layouts: 45.8 us -> none  [over_pieces(): carry, unused = lax.scan(inner, carry, (parts, starts))]
    all_gather x1, waiting for transfers between devices: 0.01 us -> 45.2 us  [on_device(): lax.all_gather(own_weights[5], 'fsdp', axis=0, tiled=True)]
    dynamic_update_slice x8 -> x0, local copies, waits for them, and re-layouts: 45 us -> none  [back_piece(): lax.dynamic_update_slice_in_dim(grad_pairs, current + update, start, 0)]
    unnamed x13 -> x12, waiting for transfers between devices: 58 us -> 13.2 us
    add x42 -> x0, other arithmetic: 36.1 us -> none  [the longest x24 15.5 us: scores_of(): start + jnp.arange(count, dtype=jnp.int32)]
  transfers between devices with their start and end apart: 11 -> 11, of which waited for: 7 -> 10; matrix products, arithmetic and copies ran while one was open for 21% -> 15% of each run, Pallas kernels for 0% -> 1%
where the time goes in v1:
time: 976 us; the launch traced here: 967 us
  waiting for transfers between devices  667 us (68%)
  local copies, waits for them, and re-layouts  98.5 us (10%)
  matrix products  91.8 us (9%)
  blocking collectives  54.2 us (6%)
  other arithmetic  20.2 us (2%)
  Pallas kernels  18.6 us (2%)
  between operations  15.6 us (2%)
    psum x1, waiting for transfers between devices, on_device(): lax.psum(row_shares, 'ctx').astype(jnp.float32)  216 us
    reduce_scatter x1, waiting for transfers between devices, on_device(): lax.psum_scatter(jnp.concatenate([part(normed_attn, grad_query_low), part...  158 us
    reduce_scatter x1, waiting for transfers between devices, on_device(): lax.psum_scatter(grad_pairs, 'ctx', scatter_dimension=0, tiled=True)  66.4 us
    all_gather x1, waiting for transfers between devices, on_device(): lax.all_gather(own_weights[4], 'fsdp', axis=0, tiled=True)  47.2 us
    all_gather x1, waiting for transfers between devices, on_device(): all_pairs = lax.all_gather(pairs, 'ctx', axis=0)  46.1 us
    all_gather x1, waiting for transfers between devices, on_device(): lax.all_gather(own_weights[6], 'fsdp', axis=0, tiled=True)  45.2 us
    all_gather x1, waiting for transfers between devices, on_device(): lax.all_gather(own_weights[5], 'fsdp', axis=0, tiled=True)  45.2 us
    dot_general x7, matrix products, backward_dot(): jnp.einsum('rn,cn->rc', grad, weight, preferred_element_type=jnp.float32)  38 us
  transfers between devices with their start and end apart: 11, of which 10 were waited for; matrix products, arithmetic and copies ran while one was open for 15% of the time, Pallas kernels for 1%

profile of v1, /device:TPU:0, one launch (start us, length us, event | category | flops | bytes accessed | tf_op | source)
XLA Modules:
  0.0 966.6 jit_solution(7859427729409176171)
XLA Ops:
  11.7 9.1 all-reduce.7
  21.7 13.9 %all_gather.33 = bf16[1152,384]{1,0:T(8,128)(2,1)S(1)} all-gather(bf16[288,384]{1,0:T(8,128)(2,1)S(1)} %copy-done.29), channel_id=1, replica_groups=mesh['fsdp'=4,'ctx'=8] {'fsdp'}, dimensions={0}, use_global_device_ids=true | all-gather | bytes 1105920 | tf_op jit(solution)/shard_map/all_gather | solution.py:175
  38.3 9.3 all_gather.32
  58.2 5.3 copy.84
  69.1 46.1 %all-gather.9.cloned.1.call-done.kv_ref = bf16[8,12,128,128]{3,2,1,0:T(8,128)(2,1)} async-done(((bf16[1,12,128,128]{3,2,1,0:T(8,128)(2,1)}), bf16[8,12,128,128]{3,2,1,0:T(8,128)(2,1)}) %all-gather.9.cloned.1.call-update) | async-done | bytes 3145744 | tf_op jit(solution)/shard_map/all_gather | solution.py:205
  115.2 7.9 shard_map.194
  134.0 7.2 all-gather.11.cloned.1.call-done
  146.4 47.2 %all-gather.13.cloned.1.call-done = bf16[1152,3072]{1,0:T(8,128)(2,1)} async-done(((bf16[288,3072]{1,0:T(8,128)(2,1)}), bf16[1152,3072]{1,0:T(8,128)(2,1)}) %all-gather.13.cloned.1.call-update) | async-done | bytes 7077904 | tf_op jit(solution)/shard_map/all_gather | solution.py:177
  193.6 7.1 fusion.18
  200.6 45.2 %all-gather.15.cloned.1.call-done = bf16[1152,3072]{1,0:T(8,128)(2,1)} async-done(((bf16[288,3072]{1,0:T(8,128)(2,1)}), bf16[1152,3072]{1,0:T(8,128)(2,1)}) %all-gather.15.cloned.1.call-update) | async-done | bytes 7077904 | tf_op jit(solution)/shard_map/all_gather | solution.py:178
  245.8 7.1 fusion.19
  252.9 45.2 %all-gather.17.cloned.1.call-done = bf16[3072,1152]{1,0:T(8,128)(2,1)} async-done(((bf16[768,1152]{1,0:T(8,128)(2,1)}), bf16[3072,1152]{1,0:T(8,128)(2,1)}) %all-gather.17.cloned.1.call-update) | async-done | bytes 7077904 | tf_op jit(solution)/shard_map/all_gather | solution.py:179
  298.1 9.2 multiply_convert_fusion
  307.3 6.4 fusion.20
  319.1 14.3 %convolution_convert_fusion.7 = bf16[256,1152]{1,0:T(8,128)(2,1)} fusion(bf16[1152,1152]{1,0:T(8,128)(2,1)S(1)} %copy-done.15, f32[256,1152]{1,0:T(8,128)S(1)} %subtract_add_fusion.1), kind=kOutput, calls=%fused_computation.22 | convolution fusion | flops 680067072 | bytes 4423680 | tf_op jit(solution)/shard_map/rn,cn->rc/dot_general | solution.py:47
  346.7 10.7 %shard_map.195 = (f32[12,64,384]{2,1,0:T(8,128)}, bf16[8,12,128,128]{3,2,1,0:T(8,128)(2,1)}) custom-call(bf16[12,128,384]{2,1,0:T(8,128)(2,1)} %concatenate.36.clone.q_ref, bf16[12,128,384]{2,1,0:T(8,128)(2,1)} %concatenate.38.clone.g_ref, bf16[12,768,128]{2,1,0:T(8,128)(2,1)} %fusion.5.qg_ref, ...), custom_call_target="tpu_custom_call" | custom-call | tf_op jit(solution)/shard_map/pallas_call | solution.py:131
  358.5 6.6 convolution_convert_fusion
  397.2 66.4 %reduce-scatter.7.cloned.1.call-done = bf16[1,12,128,128]{3,2,1,0:T(8,128)(2,1)} async-done(((bf16[8,12,128,128]{3,2,1,0:T(8,128)(2,1)}), bf16[1,12,128,128]{3,2,1,0:T(8,128)(2,1)}) %reduce-scatter.7.cloned.1.call-update) | async-done | bytes 393232 | tf_op jit(solution)/shard_map/reduce_scatter | solution.py:265
  505.8 23.1 %reduce-scatter.11.cloned.1.call-done = bf16[768,1152]{1,0:T(8,128)(2,1)} async-done(((bf16[3072,1152]{1,0:T(8,128)(2,1)}), bf16[768,1152]{1,0:T(8,128)(2,1)}) %reduce-scatter.11.cloned.1.call-update) | async-done | bytes 1769488 | tf_op jit(solution)/shard_map/reduce_scatter | solution.py:316
  529.0 157.6 %reduce-scatter.9.cloned.1.call-done = bf16[288,9216]{1,0:T(8,128)(2,1)} async-done(((bf16[1152,9216]{1,0:T(8,128)(2,1)}), bf16[288,9216]{1,0:T(8,128)(2,1)}) %reduce-scatter.9.cloned.1.call-update) | async-done | bytes 5308432 | tf_op jit(solution)/shard_map/reduce_scatter | solution.py:297
  687.2 6.5 fusion.4
  699.7 10.1 %reduce-scatter.13.cloned.1.call-done = bf16[288,2]{1,0:T(8,128)(2,1)} async-done(((bf16[1152,2]{1,0:T(8,128)(2,1)}), bf16[288,2]{1,0:T(8,128)(2,1)}) %reduce-scatter.13.cloned.1.call-update) | async-done | bytes 1168
  710.8 21.9 %psum.23 = bf16[288,2]{0,1:T(2,128)(2,1)S(1)} all-reduce(bf16[288,2]{0,1:T(2,128)(2,1)S(1)} %copy.113), channel_id=1, replica_groups=mesh['fsdp'=4,'ctx'=8] {'ctx'}, use_global_device_ids=true, to_apply=%region_12.0 | all-reduce | flops 576 | bytes 2304 | tf_op jit(solution)/shard_map/psum | solution.py:326
  733.3 215.8 %all-reduce.10.cloned.1.call-done = (bf16[288,9216]{1,0:T(8,128)(2,1)}, bf16[768,1152]{1,0:T(8,128)(2,1)}) async-done(((bf16[288,9216]{1,0:T(8,128)(2,1)}, bf16[768,1152]{1,0:T(8,128)(2,1)}), (bf16[288,9216]{1,0:T(8,128)(2,1)}, bf16[768,1152]{1,0:T(8,128)(2,1)})) %all-reduce.10.cloned.1.call-update) | async-done | bytes 7077904 | tf_op jit(solution)/shard_map/psum | solution.py:324
  (220 shorter events, 151.8 us)
Async XLA Ops:
  7.2 13.6 %copy-start.5 = (bf16[128,2,1152]{2,1,0:T(2,128)(2,1)S(1)}, bf16[128,2,1152]{2,1,0:T(2,128)(2,1)}, u32[]{:S(2)}) copy-start(bf16[128,2,1152]{2,1,0:T(2,128)(2,1)} %param.11) | copy-start | bytes 1769476
  7.2 14.5 %copy-start.29 = (bf16[288,384]{1,0:T(8,128)(2,1)S(1)}, bf16[288,384]{1,0:T(8,128)(2,1)}, u32[]{:S(2)}) copy-start(bf16[288,384]{1,0:T(8,128)(2,1)} %param.14) | copy-start | bytes 663556
  7.2 50.9 %all-gather.7.cloned.1.call-start = ((), (), s32[]{:S(2)}) async-start(), calls=%async_computation.4 | async-start | bytes 3317760 | tf_op jit(solution)/shard_map/all_gather | solution.py:173
  8.0 107.2 %all-gather.9.cloned.1.call-start = ((), (), s32[]{:S(2)}) async-start(), calls=%async_computation.5 | async-start | bytes 3538944 | tf_op jit(solution)/shard_map/all_gather | solution.py:205
  20.8 16.3 %copy-start.27 = (f32[1152]{0:T(1024)}, f32[1152]{0:T(1024)S(1)}, u32[]{:S(2)}) copy-start(f32[1152]{0:T(1024)S(1)} %convert_element_type.118) | copy-start | bytes 13828
  21.5 15.6 %copy-start.24 = (f32[128,2]{1,0:T(8,128)}, f32[128,2]{1,0:T(8,128)S(1)}, u32[]{:S(2)}) copy-start(f32[128,2]{1,0:T(8,128)S(1)} %add_rsqrt_fusion) | copy-start | bytes 3076
  21.7 15.5 %copy-start.36 = (f32[256]{0:T(256)}, f32[256]{0:T(256)S(1)}, u32[]{:S(2)}) copy-start(f32[256]{0:T(256)S(1)} %rsqrt.27) | copy-start | bytes 3076
  54.0 87.2 %all-gather.11.cloned.1.call-start = ((), (), s32[]{:S(2)}) async-start(), calls=%async_computation.6 | async-start | bytes 3317760 | tf_op jit(solution)/shard_map/all_gather | solution.py:176
  54.7 138.9 %all-gather.13.cloned.1.call-start = ((), (), s32[]{:S(2)}) async-start(), calls=%async_computation.7 | async-start | bytes 8847360 | tf_op jit(solution)/shard_map/all_gather | solution.py:177
  55.3 190.6 %all-gather.15.cloned.1.call-start = ((), (), s32[]{:S(2)}) async-start(), calls=%async_computation.8 | async-start | bytes 8847360 | tf_op jit(solution)/shard_map/all_gather | solution.py:178
  55.9 242.3 %all-gather.17.cloned.1.call-start = ((), (), s32[]{:S(2)}) async-start(), calls=%async_computation.9 | async-start | bytes 8847360 | tf_op jit(solution)/shard_map/all_gather | solution.py:179
  56.5 407.2 %reduce-scatter.7.cloned.1.call-start = ((), (), s32[]{:S(2)}) async-start(), calls=%async_computation.10 | async-start | bytes 3538944 | tf_op jit(solution)/shard_map/reduce_scatter | solution.py:265
  58.1 5.3 copy-start.19
  307.3 6.4 copy-start.49
  307.3 6.4 copy-start.47
  307.3 6.5 copy-start.35
  307.3 6.5 copy-start.39
  307.3 6.5 copy-start.45
  357.4 171.5 %reduce-scatter.11.cloned.1.call-start = ((), (), s32[]{:S(2)}) async-start(), calls=%async_computation.12 | async-start | bytes 8847360 | tf_op jit(solution)/shard_map/reduce_scatter | solution.py:316
  365.1 321.5 %reduce-scatter.9.cloned.1.call-start = ((), (), s32[]{:S(2)}) async-start(), calls=%async_computation.11 | async-start | bytes 26542080 | tf_op jit(solution)/shard_map/reduce_scatter | solution.py:297
  379.5 5.3 copy-start.7
  488.1 4.9 copy-start.48
  498.0 211.8 %reduce-scatter.13.cloned.1.call-start = ((), (), s32[]{:S(2)}) async-start(), calls=%async_computation.13 | async-start | bytes 368640
  505.8 443.3 %all-reduce.10.cloned.1.call-start = ((), (), s32[]{:S(2)}) async-start(), calls=%async_computation.14 | async-start | bytes 14155776 | tf_op jit(solution)/shard_map/psum | solution.py:324
  (38 other events, 85.6 us)
Sparse Core Ops, SparseCore 0:
  9.6 33.1 all-gather.6
  54.1 61.0 all-gather.8
  116.7 24.4 all-gather.10
  142.6 50.9 all-gather.12
  195.0 50.8 all-gather.14
  247.3 50.8 all-gather.16
  357.6 106.0 reduce-scatter.6
  466.2 62.7 reduce-scatter.10
  531.8 154.8 reduce-scatter.8
  689.5 20.2 reduce-scatter.12
  714.4 234.6 all-reduce.9

commit v2 on v1

--- a/solution.py
+++ b/solution.py
@@ -127,6 +127,197 @@
     lax.fori_loop(0, units, unit_step, 0)
 
 
+MESH = pl.DeviceIdType.MESH
+LANES = 128
+
+
+def ring_place(ctx, fsdp, count):
+    column, side = lax.div(ctx, 2), lax.rem(ctx, 2)
+    place = column + side * (count - 1 - 2 * column)
+    odd = lax.rem(fsdp, 2)
+    return place + odd * (count - 1 - 2 * place)
+
+
+def ring_ctx(place, fsdp, count):
+    odd = lax.rem(fsdp, 2)
+    place = place + odd * (count - 1 - 2 * place)
+    late = lax.div(place, count // 2)
+    return (1 - late) * 2 * place + late * (2 * (count - 1 - place) + 1)
+
+
+def ring_neighbours(count):
+    ctx, fsdp = lax.axis_index("ctx"), lax.axis_index("fsdp")
+    place = ring_place(ctx, fsdp, count)
+    after = ring_ctx(lax.rem(place + 1, count), fsdp, count)
+    before = ring_ctx(lax.rem(place + count - 1, count), fsdp, count)
+    return place, (fsdp, after), (fsdp, before)
+
+
+class Ring:
+    def __init__(self, count, works, landings, totals, sends, arrivals):
+        self.count, self.works, self.landings, self.totals = count, works, landings, totals
+        self.sends, self.arrivals = sends, arrivals
+        self.place, self.after, self.before = ring_neighbours(count)
+        self.ticks = 2 * count - 2
+
+    def chunk(self, held, index):
+        per = held.shape[0] // self.count
+        return held.at[pl.ds(index * per, per)]
+
+    def copy(self, stream, step, index, summing):
+        source = self.chunk((self.works if summing else self.totals)[stream], index)
+        target = self.landings[stream].at[step] if summing else source
+        return pltpu.make_async_remote_copy(
+            src_ref=source,
+            dst_ref=target,
+            send_sem=self.sends.at[stream, step],
+            recv_sem=self.arrivals.at[stream, step],
+            device_id=self.after,
+            device_id_type=MESH,
+        )
+
+    def start(self, stream):
+        self.copy(stream, 0, self.place, True).start()
+
+    def tick(self, step):
+        index = lax.rem(self.place + 3 * self.count - 1 - step, self.count)
+        last = self.count - 2
+        for stream in range(len(self.works)):
+            self.copy(stream, step, index, False).wait_recv()
+
+            def add(target, stream=stream):
+                part = self.chunk(self.works[stream], index)
+                landed = self.landings[stream].at[jnp.minimum(step, last)]
+                for row in range(part.shape[0]):
+                    target[row] = (
+                        part[row].astype(jnp.float32) + landed[row].astype(jnp.float32)
+                    ).astype(part.dtype)
+
+            @pl.when(step < last)
+            def _():
+                add(self.chunk(self.works[stream], index))
+                self.copy(stream, jnp.minimum(step + 1, last), index, True).start()
+
+            @pl.when(step == last)
+            def _():
+                add(self.chunk(self.totals[stream], index))
+
+            @pl.when(jnp.logical_and(step >= last, step < self.ticks - 1))
+            def _():
+                self.copy(stream, jnp.minimum(step + 1, self.ticks - 1), index, False).start()
+
+    def finish(self):
+        def wait(step, unused):
+            for stream in range(len(self.works)):
+                self.copy(stream, step, self.place, False).wait_send()
+            return unused
+
+        lax.fori_loop(0, self.ticks, wait, 0)
+
+
+def reduce_kernel(
+    gate_ref, up_ref, down_ref, rest_ref, gate_total, up_total, down_total, rest_total,
+    gate_work, up_work, down_work, rest_work, gate_land, up_land, down_land, rest_land,
+    sends, arrivals, part_sends, part_arrivals, local_sems,
+):
+    fsdp, ctx = lax.axis_index("fsdp"), lax.axis_index("ctx")
+    group, count = lax.axis_size("fsdp"), lax.axis_size("ctx")
+    works = [gate_work, up_work, down_work, rest_work]
+    landings = [gate_land, up_land, down_land, rest_land]
+    totals = [gate_total, up_total, down_total, rest_total]
+    ring = Ring(count, works, landings, totals, sends, arrivals)
+    barrier = pltpu.get_barrier_semaphore()
+    for device in (ring.after, ring.before):
+        pl.semaphore_signal(barrier, inc=1, device_id=device, device_id_type=MESH)
+    for step in range(1, group):
+        peer = lax.rem(fsdp + step, group)
+        pl.semaphore_signal(barrier, inc=1, device_id=(peer, ctx), device_id_type=MESH)
+    pl.semaphore_wait(barrier, 1 + group)
+    per = gate_ref.shape[1]
+    copies = []
+    for which, (part, work) in enumerate(((gate_ref, gate_work), (up_ref, up_work))):
+        mine = work.at[pl.ds(fsdp * per, per)]
+        own = pltpu.make_async_copy(part.at[fsdp], mine, local_sems.at[which])
+        own.start()
+        copies.append(own)
+        for step in range(1, group):
+            peer = lax.rem(fsdp + step, group)
+            copy = pltpu.make_async_remote_copy(
+                src_ref=part.at[peer],
+                dst_ref=mine,
+                send_sem=part_sends.at[which, step - 1],
+                recv_sem=part_arrivals.at[which, step - 1],
+                device_id=(peer, ctx),
+                device_id_type=MESH,
+            )
+            copy.start()
+            copies.append(copy)
+        if work.shape[0] > per * group:
+            for row in range(per * group, work.shape[0]):
+                work[row] = jnp.zeros(work.shape[1:], work.dtype)
+    for which, (part, work) in enumerate(((down_ref, down_work), (rest_ref, rest_work))):
+        own = pltpu.make_async_copy(part, work.at[pl.ds(0, part.shape[0])], local_sems.at[2 + which])
+        own.start()
+        copies.append(own)
+        for row in range(part.shape[0], work.shape[0]):
+            work[row] = jnp.zeros(work.shape[1:], work.dtype)
+    for copy in copies:
+        copy.wait()
+    for stream in range(len(works)):
+        ring.start(stream)
+
+    def step(at, unused):
+        ring.tick(at)
+        return unused
+
+    lax.fori_loop(0, ring.ticks, step, 0)
+    ring.finish()
+
+
+def padded(blocks, count):
+    return -(-blocks // count) * count
+
+
+def reduce_gradients(gate_part, up_part, down_part, rest_part):
+    group, count = lax.axis_size("fsdp"), lax.axis_size("ctx")
+    shapes = [
+        (padded(group * gate_part.shape[1], count),) + gate_part.shape[2:],
+        (padded(group * up_part.shape[1], count),) + up_part.shape[2:],
+        (padded(down_part.shape[0], count),) + down_part.shape[1:],
+        (padded(rest_part.shape[0], count),) + rest_part.shape[1:],
+    ]
+    return pl.pallas_call(
+        reduce_kernel,
+        out_shape=[jax.ShapeDtypeStruct(shape, jnp.bfloat16) for shape in shapes],
+        in_specs=[pl.BlockSpec(memory_space=pl.ANY)] * 4,
+        out_specs=[pl.BlockSpec(memory_space=pltpu.VMEM)] * 4,
+        scratch_shapes=[pltpu.VMEM(shape, jnp.bfloat16) for shape in shapes]
+        + [
+            pltpu.VMEM((count - 1, shape[0] // count) + shape[1:], jnp.bfloat16) for shape in shapes
+        ]
+        + [
+            pltpu.SemaphoreType.DMA((4, 2 * count - 2)),
+            pltpu.SemaphoreType.DMA((4, 2 * count - 2)),
+            pltpu.SemaphoreType.DMA((2, group - 1)),
+            pltpu.SemaphoreType.DMA((2, group - 1)),
+            pltpu.SemaphoreType.DMA((4,)),
+        ],
+        compiler_params=pltpu.CompilerParams(
+            collective_id=0, has_side_effects=True, vmem_limit_bytes=56 << 20
+        ),
+    )(gate_part, up_part, down_part, rest_part)
+
+
+def lane_blocks(matrix):
+    rows, columns = matrix.shape
+    return jnp.swapaxes(matrix.reshape(rows, columns // LANES, LANES), 0, 1)
+
+
+def from_blocks(blocks, first, count):
+    part = jnp.swapaxes(blocks[first : first + count], 0, 1)
+    return part.reshape(part.shape[0], count * LANES).astype(jnp.float32)
+
+
 def call(kernel, outs, *args):
     return pl.pallas_call(
         kernel,
@@ -164,9 +355,9 @@
         full_key,
         full_value,
         full_out,
-        full_gate,
-        full_up,
-        full_down,
+        my_gate,
+        my_up,
+        my_down,
         full_gain_attn,
         full_gain_ffn,
     ) = (
@@ -174,9 +365,9 @@
         lax.all_gather(own_weights[1], "fsdp", axis=0, tiled=True),
         lax.all_gather(own_weights[2], "fsdp", axis=0, tiled=True),
         lax.all_gather(own_weights[3], "fsdp", axis=0, tiled=True),
-        lax.all_gather(own_weights[4], "fsdp", axis=0, tiled=True),
-        lax.all_gather(own_weights[5], "fsdp", axis=0, tiled=True),
-        lax.all_gather(own_weights[6], "fsdp", axis=0, tiled=True),
+        lax.all_to_all(own_weights[4], "fsdp", 1, 0, tiled=True),
+        lax.all_to_all(own_weights[5], "fsdp", 1, 0, tiled=True),
+        w_down,
         lax.all_gather(own_weights[7], "fsdp", axis=0, tiled=True),
         lax.all_gather(own_weights[8], "fsdp", axis=0, tiled=True),
     )
@@ -218,23 +409,31 @@
     resid = inputs + forward_dot(attn_low, full_out)
     scale_ffn = norm_scale(resid)
     normed_ffn = (resid * scale_ffn * full_gain_ffn.astype(jnp.float32)).astype(jnp.bfloat16)
-    gate = forward_dot(normed_ffn, full_gate)
-    upward = forward_dot(normed_ffn, full_up)
+    all_normed = lax.all_gather(normed_ffn, "fsdp", axis=0, tiled=True)
+    upstream_low = cotangent.reshape(rows_count, width)
+    upstream = upstream_low.astype(jnp.float32)
+    all_upstream = lax.all_gather(upstream_low, "fsdp", axis=0, tiled=True)
+    gate = forward_dot(all_normed, my_gate)
+    upward = forward_dot(all_normed, my_up)
     sigmoid_gate = jax.nn.sigmoid(gate)
     act_low = (gate * sigmoid_gate * upward).astype(jnp.bfloat16)
-    layer_out = (
-        (resid + forward_dot(act_low, full_down))
-        .astype(jnp.bfloat16)
-        .reshape(block_len, seq_count, width)
-    )
-    upstream_low = cotangent.reshape(rows_count, width)
-    upstream = upstream_low.astype(jnp.float32)
-    grad_act = backward_dot(upstream_low, full_down)
+    ffn_out = lax.psum_scatter(
+        forward_dot(act_low, my_down).astype(jnp.bfloat16), "fsdp", scatter_dimension=0, tiled=True
+    ).astype(jnp.float32)
+    layer_out = (resid + ffn_out).astype(jnp.bfloat16).reshape(block_len, seq_count, width)
+    grad_act = backward_dot(all_upstream, my_down)
     grad_gate_low = (grad_act * upward * sigmoid_gate * (1.0 + gate * (1.0 - sigmoid_gate))).astype(
         jnp.bfloat16
     )
     grad_up_low = (grad_act * gate * sigmoid_gate).astype(jnp.bfloat16)
-    grad_normed_ffn = backward_dot(grad_gate_low, full_gate) + backward_dot(grad_up_low, full_up)
+    grad_normed_ffn = lax.psum_scatter(
+        (backward_dot(grad_gate_low, my_gate) + backward_dot(grad_up_low, my_up)).astype(
+            jnp.bfloat16
+        ),
+        "fsdp",
+        scatter_dimension=0,
+        tiled=True,
+    ).astype(jnp.float32)
     inward_ffn, gain_term_ffn = norm_back(
         resid, scale_ffn, full_gain_ffn.astype(jnp.float32), grad_normed_ffn
     )
@@ -294,15 +493,14 @@
     def part(acts, grads):
         return jnp.einsum("rc,rn->cn", acts, grads, preferred_element_type=jnp.float32)
 
-    row_shares = lax.psum_scatter(
+    group = lax.axis_size("fsdp")
+    rest_part = lax.psum_scatter(
         jnp.concatenate(
             [
                 part(normed_attn, grad_query_low),
                 part(normed_attn, grad_key_low),
                 part(normed_attn, grad_value_low),
                 part(attn_low, grad_branch),
-                part(normed_ffn, grad_gate_low),
-                part(normed_ffn, grad_up_low),
             ],
             axis=1,
         ).astype(jnp.bfloat16),
@@ -310,36 +508,29 @@
         scatter_dimension=0,
         tiled=True,
     )
-    down_term = jnp.einsum("rc,rn->cn", act_low, upstream_low, preferred_element_type=jnp.float32)
-    gain_term = jnp.stack([gain_term_attn, gain_term_ffn], axis=1)
-    down_share, gain_share = (
-        lax.psum_scatter(
-            down_term.astype(jnp.bfloat16), "fsdp", scatter_dimension=0, tiled=True
-        ).astype(jnp.float32),
-        lax.psum_scatter(
-            gain_term.astype(jnp.bfloat16), "fsdp", scatter_dimension=0, tiled=True
-        ).astype(jnp.float32),
-    )
-    row_total, down_total, gain_total = (
-        lax.psum(row_shares, "ctx").astype(jnp.float32),
-        lax.psum(down_share.astype(jnp.bfloat16), "ctx").astype(jnp.float32),
-        lax.psum(gain_share.astype(jnp.bfloat16), "ctx").astype(jnp.float32),
-    )
-    edges = [
-        0,
-        width,
-        width + kv_width,
-        width + 2 * kv_width,
-        2 * width + 2 * kv_width,
-        2 * width + 2 * kv_width + FF,
-        2 * width + 2 * kv_width + 2 * FF,
+    gate_part = part(all_normed, grad_gate_low).astype(jnp.bfloat16)
+    up_part = part(all_normed, grad_up_low).astype(jnp.bfloat16)
+    down_part = part(act_low, all_upstream).astype(jnp.bfloat16)
+
+    def by_owner(matrix):
+        rows, columns = matrix.shape
+        split = matrix.reshape(group, rows // group, columns // LANES, LANES)
+        return jnp.swapaxes(split, 1, 2)
+
+    gate_sum, up_sum, down_sum, rest_sum = reduce_gradients(
+        by_owner(gate_part),
+        by_owner(up_part),
+        down_part.reshape(-1, 16, width),
+        lane_blocks(rest_part),
+    )
+    gains = lax.psum(jnp.stack([gain_term_attn, gain_term_ffn]), ("fsdp", "ctx"))
+    own = gain_attn.shape[0]
+    gains = lax.dynamic_slice_in_dim(gains, lax.axis_index("fsdp") * own, own, 1)
+    edges = [0, width, width + kv_width, width + 2 * kv_width, 2 * width + 2 * kv_width]
+    grad_query, grad_key, grad_value, grad_out = [
+        from_blocks(rest_sum, first // LANES, (last - first) // LANES)
+        for first, last in zip(edges[:-1], edges[1:])
     ]
-    grad_query = row_total[:, edges[0] : edges[1]]
-    grad_key = row_total[:, edges[1] : edges[2]]
-    grad_value = row_total[:, edges[2] : edges[3]]
-    grad_out = row_total[:, edges[3] : edges[4]]
-    grad_gate = row_total[:, edges[4] : edges[5]]
-    grad_up = row_total[:, edges[5] : edges[6]]
     return (
         layer_out,
         grad_tokens,
@@ -347,11 +538,11 @@
         grad_key,
         grad_value,
         grad_out,
-        grad_gate,
-        grad_up,
-        down_total,
-        gain_total[:, 0],
-        gain_total[:, 1],
+        from_blocks(gate_sum, 0, FF // LANES),
+        from_blocks(up_sum, 0, FF // LANES),
+        down_sum.reshape(-1, width)[: w_down.shape[0]].astype(jnp.float32),
+        gains[0],
+        gains[1],
     )
 
 

time: 976 us -> 828 us (0.85)
  waiting for transfers between devices: 667 us -> 270 us
  Pallas kernels: 18.6 us -> 199 us
  local copies, waits for them, and re-layouts: 98.5 us -> 126 us
  other arithmetic: 20.2 us -> 42.9 us
  matrix products: 91.8 us -> 70.6 us
  starting transfers between devices: 0.65 us -> 20.8 us
  blocking collectives: 54.2 us -> 73 us
    psum x1 -> x0, waiting for transfers between devices: 216 us -> none  [on_device(): lax.psum(row_shares, 'ctx').astype(jnp.float32)]
    pallas_call x0 -> x1, Pallas kernels: none -> 180 us  [reduce_gradients(): pl.pallas_call(reduce_kernel, out_shape=[jax.ShapeDtypeStruct(shape, jnp....]
    all_gather x3 -> x2, waiting for transfers between devices: 138 us -> 0.02 us  [the longest x1 0.02 us: on_device(): all_normed = lax.all_gather(normed_ffn, 'fsdp', axis=0, tiled=True)]
    reduce_scatter x2, waiting for transfers between devices: 181 us -> 72.5 us  [the longest x1 38.7 us: on_device(): lax.psum_scatter((backward_dot(grad_gate_low, my_gate) + backward_dot(gra...]
    all_to_all x0 -> x2, waiting for transfers between devices: none -> 56.4 us  [the longest x1 29.6 us: on_device(): lax.all_to_all(own_weights[4], 'fsdp', 1, 0, tiled=True)]
    reduce_scatter x1, waiting for transfers between devices: 66.4 us -> 90.8 us  [on_device(): lax.psum_scatter(grad_pairs, 'ctx', scatter_dimension=0, tiled=True)]
    reshape x1 -> x6, local copies, waits for them, and re-layouts: 2.67 us -> 21.7 us  [the longest x4 16.6 us: by_owner(): split = matrix.reshape(group, rows // group, columns // LANES, LANES)]
    psum x1, blocking collectives: 21.9 us -> 40.3 us  [on_device(): lax.psum(jnp.stack([gain_term_attn, gain_term_ffn]), ('fsdp', 'ctx'))]
  transfers between devices with their start and end apart: 11 -> 11, of which waited for: 10 -> 7; matrix products, arithmetic and copies ran while one was open for 15% -> 17% of each run, Pallas kernels for 1% -> 1%
where the time goes in v2:
time: 828 us; the launch traced here: 817 us
  waiting for transfers between devices  270 us (33%)
  Pallas kernels  199 us (24%)
  local copies, waits for them, and re-layouts  126 us (15%)
  blocking collectives  73 us (9%)
  matrix products  70.6 us (9%)
  other arithmetic  42.9 us (5%)
  starting transfers between devices  20.8 us (3%)
  between operations  15.1 us (2%)
    pallas_call x1, Pallas kernels, reduce_gradients(): pl.pallas_call(reduce_kernel, out_shape=[jax.ShapeDtypeStruct(shape, jnp....  180 us
    reduce_scatter x1, waiting for transfers between devices, on_device(): lax.psum_scatter(grad_pairs, 'ctx', scatter_dimension=0, tiled=True)  90.8 us
    all_gather x1, waiting for transfers between devices, on_device(): all_pairs = lax.all_gather(pairs, 'ctx', axis=0)  43 us
    psum x1, blocking collectives, on_device(): lax.psum(jnp.stack([gain_term_attn, gain_term_ffn]), ('fsdp', 'ctx'))  40.3 us
    reduce_scatter x1, waiting for transfers between devices, on_device(): lax.psum_scatter((backward_dot(grad_gate_low, my_gate) + backward_dot(gra...  38.7 us
    reduce_scatter x1, waiting for transfers between devices, on_device(): lax.psum_scatter(forward_dot(act_low, my_down).astype(jnp.bfloat16), 'fsd...  33.8 us
    unnamed x89, local copies, waits for them, and re-layouts  29.7 us
    all_to_all x1, waiting for transfers between devices, on_device(): lax.all_to_all(own_weights[4], 'fsdp', 1, 0, tiled=True)  29.6 us
  transfers between devices with their start and end apart: 11, of which 7 were waited for; matrix products, arithmetic and copies ran while one was open for 17% of the time, Pallas kernels for 1%

profile of v2, /device:TPU:0, one launch (start us, length us, event | category | flops | bytes accessed | tf_op | source)
XLA Modules:
  0.0 816.7 jit_solution(13713712588321840503)
XLA Ops:
  11.7 9.1 %all-reduce.6 = (bf16[1152]{0:T(1024)(128)(2,1)S(1)}, bf16[1152]{0:T(1024)(128)(2,1)}) all-reduce(bf16[1152]{0:T(1024)(128)(2,1)S(1)} %dynamic-update-slice, bf16[1152]{0:T(1024)(128)(2,1)S(1)} %dynamic-update-slice.1), channel_id=1, replica_groups=mesh['fsdp'=4,'ctx'=8] {'fsdp'}, use_global_device_ids=true, to_apply=%add.4 | all-reduce | flops 2304 | bytes 9216
  21.3 14.1 %all_gather.29 = bf16[1152,384]{1,0:T(8,128)(2,1)S(1)} all-gather(bf16[288,384]{1,0:T(8,128)(2,1)} %param.13), channel_id=1, replica_groups=mesh['fsdp'=4,'ctx'=8] {'fsdp'}, dimensions={0}, use_global_device_ids=true | all-gather | bytes 1105920 | tf_op jit(solution)/shard_map/all_gather | solution.py:365
  49.6 9.4 %all_gather.30 = bf16[1152,384]{1,0:T(8,128)(2,1)S(1)} all-gather(bf16[288,384]{1,0:T(8,128)(2,1)} %param.14), channel_id=1, replica_groups=mesh['fsdp'=4,'ctx'=8] {'fsdp'}, dimensions={0}, use_global_device_ids=true | all-gather | bytes 1105920 | tf_op jit(solution)/shard_map/all_gather | solution.py:366
  68.8 5.2 copy.130
  85.0 43.0 %all-gather.8.cloned.1.call-done.kv_ref = bf16[8,12,128,128]{3,2,1,0:T(8,128)(2,1)} async-done(((bf16[1,12,128,128]{3,2,1,0:T(8,128)(2,1)}), bf16[8,12,128,128]{3,2,1,0:T(8,128)(2,1)}) %all-gather.8.cloned.1.call-update) | async-done | bytes 3145744 | tf_op jit(solution)/shard_map/all_gather | solution.py:396
  128.0 7.9 shard_map.194
  148.5 5.5 all-gather.10.cloned.1.call-done
  159.3 11.7 %all-gather.14.cloned.1.call-start = ((), (), s32[]{:S(2)}) async-start(), calls=%async_computation.11 | async-start | bytes 2949120 | tf_op jit(solution)/shard_map/all_gather | solution.py:415
  183.7 29.6 %all-to-all-done = bf16[288,4,768]{2,0,1:T(8,128)(2,1)} async-done(((bf16[288,4,768]{2,0,1:T(8,128)(2,1)}), bf16[288,4,768]{2,0,1:T(8,128)(2,1)}, u32[]{:S(2)}, u32[]{:S(2)}) %all-to-all-start) | async-done | bytes 1769504 | tf_op jit(solution)/shard_map/all_to_all | solution.py:368
  217.8 6.0 fusion.19
  223.9 26.8 %all-to-all-done.1 = bf16[288,4,768]{2,0,1:T(8,128)(2,1)} async-done(((bf16[288,4,768]{2,0,1:T(8,128)(2,1)}), bf16[288,4,768]{2,0,1:T(8,128)(2,1)}, u32[]{:S(2)}, u32[]{:S(2)}) %all-to-all-start.1) | async-done | bytes 1769504 | tf_op jit(solution)/shard_map/all_to_all | solution.py:369
  250.6 6.1 fusion.20
  256.7 7.7 multiply_convert_fusion
  269.2 5.2 add_convert_fusion
  274.5 5.0 convolution_convert_fusion.2
  279.6 38.7 %reduce-scatter.9.cloned.1.call-done = bf16[256,1152]{1,0:T(8,128)(2,1)} async-done(((bf16[1024,1152]{1,0:T(8,128)(2,1)}), bf16[256,1152]{1,0:T(8,128)(2,1)}) %reduce-scatter.9.cloned.1.call-update) | async-done | bytes 589840 | tf_op jit(solution)/shard_map/reduce_scatter | solution.py:429
  320.8 33.8 %reduce-scatter.7.cloned.1.call-done = bf16[256,1152]{1,0:T(8,128)(2,1)} async-done(((bf16[1024,1152]{1,0:T(8,128)(2,1)}), bf16[256,1152]{1,0:T(8,128)(2,1)}) %reduce-scatter.7.cloned.1.call-update) | async-done | bytes 589840 | tf_op jit(solution)/shard_map/reduce_scatter | solution.py:420
  370.2 10.7 %shard_map.195 = (f32[12,64,384]{2,1,0:T(8,128)}, bf16[8,12,128,128]{3,2,1,0:T(8,128)(2,1)}) custom-call(bf16[12,128,384]{2,1,0:T(8,128)(2,1)} %concatenate.36.clone.q_ref, bf16[12,128,384]{2,1,0:T(8,128)(2,1)} %concatenate.38.clone.g_ref, bf16[12,768,128]{2,1,0:T(8,128)(2,1)} %fusion.2.qg_ref, ...), custom_call_target="tpu_custom_call" | custom-call | tf_op jit(solution)/shard_map/pallas_call | solution.py:322
  396.3 90.8 %reduce-scatter.11.cloned.1.call-done = bf16[1,12,128,128]{3,2,1,0:T(8,128)(2,1)} async-done(((bf16[8,12,128,128]{3,2,1,0:T(8,128)(2,1)}), bf16[1,12,128,128]{3,2,1,0:T(8,128)(2,1)}) %reduce-scatter.11.cloned.1.call-update) | async-done | bytes 393232 | tf_op jit(solution)/shard_map/reduce_scatter | solution.py:464
  504.4 6.3 pad_maximum_fusion
  510.7 10.3 %copy.170 = bf16[1152,3072]{1,0:T(8,128)(2,1)} copy(bf16[1152,3072]{0,1:T(8,128)(2,1)} %pad_maximum_fusion) | data formatting | bytes 14155776
  521.7 5.4 convolution_convert_fusion.4
  560.6 40.3 %psum.7 = f32[2,1152]{1,0:T(2,128)S(1)} all-reduce(f32[2,1152]{1,0:T(2,128)S(1)} %pad_maximum_fusion.1), channel_id=1, replica_groups=mesh['fsdp'=4,'ctx'=8] {'fsdp','ctx'}, use_global_device_ids=true, to_apply=%region_10.0 | all-reduce | flops 2304 | bytes 18432 | tf_op jit(solution)/shard_map/psum | solution.py:526
  609.7 180.1 %shard_map.196 = (bf16[24,288,128]{2,1,0:T(8,128)(2,1)}, bf16[24,288,128]{2,1,0:T(8,128)(2,1)}, bf16[48,16,1152]{2,1,0:T(8,128)(2,1)}, bf16[24,288,128]{2,1,0:T(8,128)(2,1)}) custom-call(bf16[4,6,288,128]{3,2,1,0:T(8,128)(2,1)} %bitcast.129, bf16[4,6,288,128]{3,2,1,0:T(8,128)(2,1)} %bitcast.128, bf16[48,16,1152]{2,1,0:T(8,128)(2,1)} %bitcast.145, ...), custom_call_target="tpu_custom_call" | custom-call | tf_op jit(solution)/shard_map/pallas_call | solution.py:289
  (202 shorter events, 193.0 us)
Async XLA Ops:
  7.2 249.5 %copy-start = (bf16[768,1152]{1,0:T(8,128)(2,1)S(1)}, bf16[768,1152]{1,0:T(8,128)(2,1)}, u32[]{:S(2)}) copy-start(bf16[768,1152]{1,0:T(8,128)(2,1)} %param.18) | copy-start | bytes 5308420
  7.2 29.7 %copy-start.7 = (bf16[128,2,1152]{2,1,0:T(2,128)(2,1)S(1)}, bf16[128,2,1152]{2,1,0:T(2,128)(2,1)}, u32[]{:S(2)}) copy-start(bf16[128,2,1152]{2,1,0:T(2,128)(2,1)} %param.11) | copy-start | bytes 1769476
  7.2 61.6 %all-gather.6.cloned.1.call-start = ((), (), s32[]{:S(2)}) async-start(), calls=%async_computation.6 | async-start | bytes 3317760 | tf_op jit(solution)/shard_map/all_gather | solution.py:364
  7.9 120.0 %all-gather.8.cloned.1.call-start = ((), (), s32[]{:S(2)}) async-start(), calls=%async_computation.7 | async-start | bytes 3538944 | tf_op jit(solution)/shard_map/all_gather | solution.py:396
  40.7 4.7 copy-start.27
  66.7 87.3 %all-gather.10.cloned.1.call-start = ((), (), s32[]{:S(2)}) async-start(), calls=%async_computation.8 | async-start | bytes 3317760 | tf_op jit(solution)/shard_map/all_gather | solution.py:367
  67.4 150.4 %all-gather.12.cloned.1.call-start = ((), (), s32[]{:S(2)}) async-start(), calls=%async_computation.9 | async-start | bytes 2949120 | tf_op jit(solution)/shard_map/all_gather | solution.py:412
  154.0 4.3 copy-start.29
  159.3 97.4 %all-gather.14.cloned.1.call-start = ((), (), s32[]{:S(2)}) async-start(), calls=%async_computation.11 | async-start | bytes 2949120 | tf_op jit(solution)/shard_map/all_gather | solution.py:415
  176.5 36.8 %all-to-all-start = ((bf16[288,4,768]{2,0,1:T(8,128)(2,1)}), bf16[288,4,768]{2,0,1:T(8,128)(2,1)}, u32[]{:S(2)}, u32[]{:S(2)}) async-start(bf16[288,4,768]{2,0,1:T(8,128)(2,1)} %bitcast.132), calls=%async_computation | async-start | bytes 3538944 | tf_op jit(solution)/shard_map/all_to_all | solution.py:368
  213.3 37.3 %all-to-all-start.1 = ((bf16[288,4,768]{2,0,1:T(8,128)(2,1)}), bf16[288,4,768]{2,0,1:T(8,128)(2,1)}, u32[]{:S(2)}, u32[]{:S(2)}) async-start(bf16[288,4,768]{2,0,1:T(8,128)(2,1)} %bitcast.131), calls=%async_computation.1 | async-start | bytes 3538944 | tf_op jit(solution)/shard_map/all_to_all | solution.py:369
  217.7 100.5 %reduce-scatter.9.cloned.1.call-start = ((), (), s32[]{:S(2)}) async-start(), calls=%async_computation.12 | async-start | bytes 2949120 | tf_op jit(solution)/shard_map/reduce_scatter | solution.py:429
  264.4 4.8 copy-start.36
  264.4 4.9 copy-start.35
  274.4 80.2 %reduce-scatter.7.cloned.1.call-start = ((), (), s32[]{:S(2)}) async-start(), calls=%async_computation.10 | async-start | bytes 2949120 | tf_op jit(solution)/shard_map/reduce_scatter | solution.py:420
  279.5 38.8 %copy-start.3 = (f32[256,1152]{1,0:T(8,128)S(1)}, f32[256,1152]{1,0:T(8,128)}, u32[]{:S(2)}) copy-start(f32[256,1152]{1,0:T(8,128)} %copy-done.2) | copy-start | bytes 3538948
  279.5 75.1 %copy-start.13 = (bf16[256,1152]{1,0:T(8,128)(2,1)S(1)}, bf16[256,1152]{1,0:T(8,128)(2,1)}, u32[]{:S(2)}) copy-start(bf16[256,1152]{1,0:T(8,128)(2,1)} %reshape.318) | copy-start | bytes 1769476
  279.5 207.6 %reduce-scatter.11.cloned.1.call-start = ((), (), s32[]{:S(2)}) async-start(), calls=%async_computation.13 | async-start | bytes 3538944 | tf_op jit(solution)/shard_map/reduce_scatter | solution.py:464
  354.6 3.7 copy-start.15
  361.2 4.5 copy-start.4
  381.0 220.7 %reduce-scatter.13.cloned.1.call-start = ((), (), s32[]{:S(2)}) async-start(), calls=%async_computation.14 | async-start | bytes 8847360
  547.0 3.5 copy-start.16
  805.4 3.7 copy-start.19
  805.4 4.6 copy-start.1
  (26 other events, 51.5 us)
Sparse Core Ops, SparseCore 0:
  9.6 33.1 all-gather.5
  66.8 61.0 all-gather.7
  129.5 24.4 all-gather.9
  159.4 57.7 all-gather.11
  218.6 35.4 all-gather.13
  274.5 43.6 reduce-scatter.8
  321.5 33.0 reduce-scatter.6
  381.1 106.0 reduce-scatter.10
  521.1 63.3 reduce-scatter.12

commit v3 on v2

--- a/solution.py
+++ b/solution.py
@@ -20,8 +20,8 @@
     half = values.shape[-1] // 2
     freqs = ROTARY_BASE ** (-2.0 * jnp.arange(half, dtype=jnp.float32) / values.shape[-1])
     angles = positions.astype(jnp.float32)[:, None] * freqs[None, :]
-    cosine = jnp.cos(angles)[:, None, None, :]
-    sine = direction * jnp.sin(angles)[:, None, None, :]
+    cosine = jnp.cos(angles)[:, None, :]
+    sine = direction * jnp.sin(angles)[:, None, :]
     first = values[..., :half]
     second = values[..., half:]
     return jnp.concatenate(
@@ -45,46 +45,6 @@
 
 def backward_dot(grad, weight):
     return jnp.einsum("rn,cn->rc", grad, weight, preferred_element_type=jnp.float32)
-
-
-def attend_kernel(q_ref, kv_ref, mix_ref, log_ref):
-    me = lax.axis_index("ctx")
-    units, deep, wide = q_ref.shape
-    keys = kv_ref.shape[2]
-
-    def unit_step(unit, unused):
-        q = q_ref[unit]
-
-        def attend(block, top, total, mixed, diagonal):
-            kv = kv_ref[block, unit]
-            scores = jnp.dot(kv, q, preferred_element_type=jnp.float32)
-            if diagonal:
-                key_at = lax.broadcasted_iota(jnp.int32, scores.shape, 0)
-                query_at = lax.rem(lax.broadcasted_iota(jnp.int32, scores.shape, 1), keys)
-                scores = jnp.where(key_at <= query_at, scores, MASKED_SCORE)
-            new_top = jnp.maximum(top, jnp.max(scores, axis=0, keepdims=True))
-            fade = jnp.exp(top - new_top)
-            weights = jnp.exp(scores - new_top)
-            total = total * fade + jnp.sum(weights, axis=0, keepdims=True)
-            added = jnp.dot(
-                kv.T, weights.astype(jnp.bfloat16), preferred_element_type=jnp.float32
-            )
-            return new_top, total, mixed * fade + added[HD:]
-
-        state = (
-            jnp.full((1, wide), MASKED_SCORE, jnp.float32),
-            jnp.zeros((1, wide), jnp.float32),
-            jnp.zeros((HD, wide), jnp.float32),
-        )
-        state = attend(me, *state, True)
-        top, total, mixed = lax.fori_loop(
-            0, me, lambda block, state: attend(block, *state, False), state
-        )
-        mix_ref[unit] = mixed / total
-        log_ref[unit] = top + jnp.log(total)
-        return unused
-
-    lax.fori_loop(0, units, unit_step, 0)
 
 
 def attend_back_kernel(q_ref, g_ref, qg_ref, kv_ref, mix_ref, log_ref, grad_q_ref, grad_kv_ref):
@@ -318,6 +278,333 @@
     return part.reshape(part.shape[0], count * LANES).astype(jnp.float32)
 
 
+class GroupGather:
+    def __init__(self, shard_of, sends, arrivals):
+        self.shard_of, self.sends, self.arrivals = shard_of, sends, arrivals
+        self.fsdp, self.ctx = lax.axis_index("fsdp"), lax.axis_index("ctx")
+        self.chips = lax.axis_size("fsdp") // 2
+        self.chip, self.core = lax.div(self.fsdp, 2), lax.rem(self.fsdp, 2)
+        self.sibling = 2 * self.chip + 1 - self.core
+
+    def copy(self, source, shard, semaphore, device):
+        return pltpu.make_async_remote_copy(
+            src_ref=source,
+            dst_ref=self.shard_of(shard),
+            send_sem=self.sends.at[semaphore],
+            recv_sem=self.arrivals.at[semaphore],
+            device_id=(device, self.ctx),
+            device_id_type=MESH,
+        )
+
+    def same_core(self, step):
+        return 2 * lax.rem(self.chip + step, self.chips) + self.core
+
+    def across(self, source):
+        return self.copy(source, self.fsdp, 0, self.sibling)
+
+    def out(self, source, step):
+        return self.copy(source, self.fsdp, step, self.same_core(step))
+
+    def onward(self, step):
+        shard = self.same_core(self.chips - step)
+        return self.copy(self.shard_of(shard), shard, self.chips - 1 + step, self.sibling)
+
+    def start(self, source):
+        for step in range(1, self.chips):
+            self.out(source, step).start()
+        self.across(source).start()
+
+    def forward(self):
+        own = self.shard_of(self.fsdp)
+        for step in range(1, self.chips):
+            self.out(own, step).wait_recv()
+            self.onward(step).start()
+
+    def sibling_here(self):
+        self.across(self.shard_of(self.fsdp)).wait_recv()
+
+    def crossed(self, step):
+        self.onward(step).wait_recv()
+
+    def sent(self):
+        own = self.shard_of(self.fsdp)
+        self.across(own).wait_send()
+        for step in range(1, self.chips):
+            self.out(own, step).wait_send()
+            self.onward(step).wait_send()
+
+    def finish(self):
+        self.forward()
+        self.sibling_here()
+        for step in range(1, self.chips):
+            self.crossed(step)
+        self.sent()
+
+
+def group_semaphores():
+    return pltpu.SemaphoreType.DMA((lax.axis_size("fsdp") - 1,))
+
+
+def greet_group(barrier):
+    fsdp, ctx, group = lax.axis_index("fsdp"), lax.axis_index("ctx"), lax.axis_size("fsdp")
+    for step in range(1, group):
+        peer = lax.rem(fsdp + step, group)
+        pl.semaphore_signal(barrier, inc=1, device_id=(peer, ctx), device_id_type=MESH)
+    return group - 1
+
+
+class Steps:
+    def __init__(self):
+        self.fsdp, self.ctx = lax.axis_index("fsdp"), lax.axis_index("ctx")
+        self.levels = lax.axis_size("ctx") // 2
+        self.level, self.side = lax.div(self.ctx, 2), lax.rem(self.ctx, 2)
+        self.peer = (self.fsdp, 2 * self.level + 1 - self.side)
+        self.above = (self.fsdp, lax.rem(self.ctx + 2, 2 * self.levels))
+        self.below = (self.fsdp, lax.rem(self.ctx + 2 * self.levels - 2, 2 * self.levels))
+        self.has_above = self.level + 1 < self.levels
+        self.has_below = self.level > 0
+
+    def greet(self, barrier):
+        pl.semaphore_signal(barrier, inc=1, device_id=self.peer, device_id_type=MESH)
+
+        @pl.when(self.has_above)
+        def _():
+            pl.semaphore_signal(barrier, inc=1, device_id=self.above, device_id_type=MESH)
+
+        @pl.when(self.has_below)
+        def _():
+            pl.semaphore_signal(barrier, inc=1, device_id=self.below, device_id_type=MESH)
+
+        return 1 + jnp.minimum(self.level, 1) + jnp.minimum(self.levels - 1 - self.level, 1)
+
+
+PARTS = 2
+
+
+def causal(keys, wide, shape):
+    key_at = lax.broadcasted_iota(jnp.int32, shape, 0)
+    query_at = lax.rem(lax.broadcasted_iota(jnp.int32, shape, 1), keys)
+    return key_at <= query_at
+
+
+def attend_kernel(
+    q_ref, kv_ref, out_ref, gate_ref, up_ref,
+    low_ref, mix_ref, log_ref, all_ref, full_out_ref, my_gate_ref, my_up_ref,
+    top_ref, total_ref, chain_sends, chain_arrivals, peer_sends, peer_arrivals,
+    out_sends, out_arrivals, part_sends, part_arrivals, local_sems,
+):
+    steps = Steps()
+    fsdp, ctx, group = steps.fsdp, steps.ctx, lax.axis_size("fsdp")
+    units, deep, wide = q_ref.shape
+    keys = kv_ref.shape[1]
+    per_part = units // PARTS
+    barrier = pltpu.get_barrier_semaphore()
+    greeted = steps.greet(barrier) + greet_group(barrier)
+    all_ref[ctx] = kv_ref[...]
+    pl.semaphore_wait(barrier, greeted)
+
+    def block_copy(level, part, side, semaphores, arrivals, arrives, device):
+        block = 2 * (steps.level - level) + side
+        held = all_ref.at[block, pl.ds(part * per_part, per_part)]
+        return pltpu.make_async_remote_copy(
+            src_ref=held,
+            dst_ref=held,
+            send_sem=semaphores.at[level, part],
+            recv_sem=arrivals.at[arrives, part],
+            device_id=device,
+            device_id_type=MESH,
+        )
+
+    def chain(level, part):
+        return block_copy(
+            level, part, steps.side, chain_sends, chain_arrivals, level + 1, steps.above
+        )
+
+    def across(level, part):
+        return block_copy(
+            level, part, steps.side, peer_sends, peer_arrivals, level, steps.peer
+        )
+
+    def pass_on(level, part):
+        @pl.when(steps.has_above)
+        def _():
+            chain(level, part).start()
+
+    for part in range(PARTS):
+        pass_on(0, part)
+
+        @pl.when(steps.side == 0)
+        def _():
+            across(0, part).start()
+
+    rows = out_ref.shape[0]
+    columns = my_gate_ref.shape[1]
+    gathered = GroupGather(
+        lambda shard: full_out_ref.at[pl.ds(shard * rows, rows)], out_sends, out_arrivals
+    )
+    gathered.start(out_ref)
+    background = []
+    own_rows = pl.ds(fsdp * rows, rows)
+    own_out = pltpu.make_async_copy(out_ref, full_out_ref.at[own_rows], local_sems.at[2])
+    own_out.start()
+    background.append(own_out)
+    for which, (source, target) in enumerate(((gate_ref, my_gate_ref), (up_ref, my_up_ref))):
+        for step in range(1, group):
+            peer = lax.rem(fsdp + step, group)
+            copy = pltpu.make_async_remote_copy(
+                src_ref=source.at[:, pl.ds(pl.multiple_of(peer * columns, LANES), columns)],
+                dst_ref=target.at[own_rows],
+                send_sem=part_sends.at[which, step - 1],
+                recv_sem=part_arrivals.at[which, step - 1],
+                device_id=(peer, ctx),
+                device_id_type=MESH,
+            )
+            copy.start()
+            background.append(copy)
+        own = pltpu.make_async_copy(
+            source.at[:, pl.ds(pl.multiple_of(fsdp * columns, LANES), columns)],
+            target.at[own_rows],
+            local_sems.at[which],
+        )
+        own.start()
+        background.append(own)
+
+    def add(unit, kv):
+        scores = jnp.dot(kv, q_ref[unit], preferred_element_type=jnp.float32)
+        top = top_ref[unit]
+        new_top = jnp.maximum(top, jnp.max(scores, axis=0, keepdims=True))
+        fade = jnp.exp(top - new_top)
+        weights = jnp.exp(scores - new_top)
+        top_ref[unit] = new_top
+        total_ref[unit] = total_ref[unit] * fade + jnp.sum(weights, axis=0, keepdims=True)
+        added = jnp.dot(kv.T, weights.astype(jnp.bfloat16), preferred_element_type=jnp.float32)
+        mix_ref[unit] = mix_ref[unit] * fade + added[HD:]
+
+    def over_units(body, first, count):
+        def two(at, unused):
+            body(first + 2 * at)
+            body(first + 2 * at + 1)
+            return unused
+
+        lax.fori_loop(0, count // 2, two, 0)
+
+    def diagonal(unit):
+        kv = kv_ref[unit]
+        scores = jnp.dot(kv, q_ref[unit], preferred_element_type=jnp.float32)
+        scores = jnp.where(causal(keys, wide, scores.shape), scores, MASKED_SCORE)
+        top = jnp.max(scores, axis=0, keepdims=True)
+        weights = jnp.exp(scores - top)
+        top_ref[unit] = top
+        total_ref[unit] = jnp.sum(weights, axis=0, keepdims=True)
+        added = jnp.dot(kv.T, weights.astype(jnp.bfloat16), preferred_element_type=jnp.float32)
+        mix_ref[unit] = added[HD:]
+
+    over_units(diagonal, 0, units)
+
+    @pl.when(steps.side == 1)
+    def _():
+        for part in range(PARTS):
+            across(0, part).wait_recv()
+            over_units(lambda unit: add(unit, all_ref[ctx - 1, unit]), part * per_part, per_part)
+
+    def level_step(level, unused):
+        for part in range(PARTS):
+            chain(level - 1, part).wait_recv()
+            pass_on(level, part)
+            across(level, part).start()
+        first = 2 * (steps.level - level)
+        for part in range(PARTS):
+            across(level, part).wait_recv()
+            over_units(
+                lambda unit: add(unit, all_ref[pl.ds(first, 2), unit].reshape(2 * keys, deep)),
+                part * per_part,
+                per_part,
+            )
+        return unused
+
+    lax.fori_loop(1, steps.level + 1, level_step, 0)
+
+    def close(unit):
+        total = total_ref[unit]
+        mix_ref[unit] = mix_ref[unit] / total
+        log_ref[unit] = top_ref[unit] + jnp.log(total)
+
+    over_units(close, 0, units)
+    groups = wide // keys
+    for sequence in range(units // KVH):
+        for pair in range(H // 2):
+            heads = []
+            for head in (2 * pair, 2 * pair + 1):
+                unit, member = sequence * KVH + head // groups, head % groups
+                heads.append(mix_ref[unit, :, member * keys : (member + 1) * keys])
+            tile = jnp.concatenate(heads, axis=0).T
+            low_ref[
+                sequence * keys : (sequence + 1) * keys, pair * 2 * HD : (pair + 1) * 2 * HD
+            ] = tile.astype(low_ref.dtype)
+    gathered.finish()
+    for copy in background:
+        copy.wait()
+
+    def sent(level, unused):
+        for part in range(PARTS):
+
+            @pl.when(steps.has_above)
+            def _():
+                chain(level, part).wait_send()
+
+            @pl.when(jnp.logical_or(level > 0, steps.side == 0))
+            def _():
+                across(level, part).wait_send()
+
+        return unused
+
+    lax.fori_loop(0, steps.level + 1, sent, 0)
+
+
+ANY = pl.BlockSpec(memory_space=pl.ANY)
+VMEM = pl.BlockSpec(memory_space=pltpu.VMEM)
+
+
+def attend(q_wide, pairs, w_out, w_gate, w_up):
+    group, count = lax.axis_size("fsdp"), lax.axis_size("ctx")
+    units, deep, wide = q_wide.shape
+    keys = pairs.shape[1]
+    rows, width = w_out.shape
+    hidden = w_gate.shape[1] // group
+    dma = pltpu.SemaphoreType.DMA
+    sequences = units // KVH
+    return pl.pallas_call(
+        attend_kernel,
+        out_shape=[
+            jax.ShapeDtypeStruct((sequences * keys, width), jnp.bfloat16),
+            jax.ShapeDtypeStruct((units, HD, wide), jnp.float32),
+            jax.ShapeDtypeStruct((units, 1, wide), jnp.float32),
+            jax.ShapeDtypeStruct((count,) + pairs.shape, jnp.bfloat16),
+            jax.ShapeDtypeStruct((group * rows, width), jnp.bfloat16),
+            jax.ShapeDtypeStruct((group * rows, hidden), jnp.bfloat16),
+            jax.ShapeDtypeStruct((group * rows, hidden), jnp.bfloat16),
+        ],
+        in_specs=[VMEM, VMEM, ANY, ANY, ANY],
+        out_specs=[VMEM, VMEM, VMEM, VMEM, ANY, ANY, ANY],
+        scratch_shapes=[
+            pltpu.VMEM((units, 1, wide), jnp.float32),
+            pltpu.VMEM((units, 1, wide), jnp.float32),
+            dma((count // 2, PARTS)),
+            dma((count // 2 + 1, PARTS)),
+            dma((count // 2, PARTS)),
+            dma((count // 2, PARTS)),
+            group_semaphores(),
+            group_semaphores(),
+            dma((2, group - 1)),
+            dma((2, group - 1)),
+            dma((3,)),
+        ],
+        compiler_params=pltpu.CompilerParams(
+            collective_id=1, has_side_effects=True, vmem_limit_bytes=56 << 20
+        ),
+    )(q_wide, pairs, w_out, w_gate, w_up)
+
+
 def call(kernel, outs, *args):
     return pl.pallas_call(
         kernel,
@@ -330,8 +617,8 @@
 
 def unit_columns(rows, seq_count, block_len):
     groups = H // KVH
-    split = rows.reshape(block_len, seq_count, KVH, groups, HD)
-    return jnp.transpose(split, (1, 2, 4, 3, 0)).reshape(
+    split = rows.reshape(seq_count, block_len, KVH, groups, HD)
+    return jnp.transpose(split, (0, 2, 4, 3, 1)).reshape(
         seq_count * KVH, HD, groups * block_len
     )
 
@@ -339,7 +626,7 @@
 def unit_rows(columns, seq_count, block_len):
     groups = H // KVH
     split = columns.reshape(seq_count, KVH, HD, groups, block_len)
-    return jnp.transpose(split, (4, 0, 1, 3, 2)).reshape(block_len * seq_count, H * HD)
+    return jnp.transpose(split, (0, 4, 1, 3, 2)).reshape(seq_count * block_len, H * HD)
 
 
 def on_device(
@@ -347,70 +634,46 @@
 ):
     block_len, seq_count, width = tokens.shape
     rows_count = block_len * seq_count
-    groups = H // KVH
     kv_width = KVH * HD
-    own_weights = (w_query, w_key, w_value, w_out, w_gate, w_up, w_down, gain_attn, gain_ffn)
-    (
-        full_query,
-        full_key,
-        full_value,
-        full_out,
-        my_gate,
-        my_up,
-        my_down,
-        full_gain_attn,
-        full_gain_ffn,
-    ) = (
-        lax.all_gather(own_weights[0], "fsdp", axis=0, tiled=True),
-        lax.all_gather(own_weights[1], "fsdp", axis=0, tiled=True),
-        lax.all_gather(own_weights[2], "fsdp", axis=0, tiled=True),
-        lax.all_gather(own_weights[3], "fsdp", axis=0, tiled=True),
-        lax.all_to_all(own_weights[4], "fsdp", 1, 0, tiled=True),
-        lax.all_to_all(own_weights[5], "fsdp", 1, 0, tiled=True),
-        w_down,
-        lax.all_gather(own_weights[7], "fsdp", axis=0, tiled=True),
-        lax.all_gather(own_weights[8], "fsdp", axis=0, tiled=True),
-    )
+    full_query, full_key, full_value = [
+        lax.all_gather(weight, "fsdp", axis=0, tiled=True) for weight in (w_query, w_key, w_value)
+    ]
+    full_gain_attn, full_gain_ffn = [
+        lax.all_gather(gain, "fsdp", axis=0, tiled=True) for gain in (gain_attn, gain_ffn)
+    ]
+    my_down = w_down
     my_start = lax.axis_index("ctx") * block_len
     positions = my_start + jnp.arange(block_len, dtype=jnp.int32)
-    inputs = tokens.astype(jnp.float32).reshape(rows_count, width)
+    inputs = jnp.swapaxes(tokens, 0, 1).reshape(rows_count, width).astype(jnp.float32)
     scale_attn = norm_scale(inputs)
     normed_attn = (inputs * scale_attn * full_gain_attn.astype(jnp.float32)).astype(jnp.bfloat16)
     query_raw = forward_dot(normed_attn, full_query)
     key_raw = forward_dot(normed_attn, full_key)
     value_raw = forward_dot(normed_attn, full_value)
     units = seq_count * KVH
-    wide = groups * block_len
+    wide = H // KVH * block_len
     queries = (
-        rotary(query_raw.reshape(block_len, seq_count, H, HD), positions, 1.0)
+        rotary(query_raw.reshape(seq_count, block_len, H, HD), positions, 1.0)
         .astype(jnp.bfloat16)
         .reshape(rows_count, width)
     )
     keys_local = rotary(
-        key_raw.reshape(block_len, seq_count, KVH, HD), positions, 1.0
+        key_raw.reshape(seq_count, block_len, KVH, HD), positions, 1.0
     ).astype(jnp.bfloat16)
-    values_local = value_raw.astype(jnp.bfloat16).reshape(block_len, seq_count, KVH, HD)
-    pairs = jnp.transpose(
-        jnp.concatenate([keys_local, values_local], axis=-1), (1, 2, 0, 3)
+    values_local = value_raw.astype(jnp.bfloat16).reshape(seq_count, block_len, KVH, HD)
+    pairs = jnp.swapaxes(
+        jnp.concatenate([keys_local, values_local], axis=-1), 1, 2
     ).reshape(units, block_len, 2 * HD)
-    all_pairs = lax.all_gather(pairs, "ctx", axis=0)
     q_unit = unit_columns(queries * jnp.bfloat16(HD ** (-0.5)), seq_count, block_len)
     q_wide = jnp.concatenate([q_unit, jnp.zeros_like(q_unit)], axis=1)
-    mix_unit, log_total = call(
-        attend_kernel,
-        [
-            jax.ShapeDtypeStruct((units, HD, wide), jnp.float32),
-            jax.ShapeDtypeStruct((units, 1, wide), jnp.float32),
-        ],
-        q_wide,
-        all_pairs,
-    )
-    attn_low = unit_rows(mix_unit.astype(jnp.bfloat16), seq_count, block_len)
+    attn_low, mix_unit, log_total, all_pairs, full_out, my_gate, my_up = attend(
+        q_wide, pairs, w_out, w_gate, w_up
+    )
     resid = inputs + forward_dot(attn_low, full_out)
     scale_ffn = norm_scale(resid)
     normed_ffn = (resid * scale_ffn * full_gain_ffn.astype(jnp.float32)).astype(jnp.bfloat16)
     all_normed = lax.all_gather(normed_ffn, "fsdp", axis=0, tiled=True)
-    upstream_low = cotangent.reshape(rows_count, width)
+    upstream_low = jnp.swapaxes(cotangent, 0, 1).reshape(rows_count, width)
     upstream = upstream_low.astype(jnp.float32)
     all_upstream = lax.all_gather(upstream_low, "fsdp", axis=0, tiled=True)
     gate = forward_dot(all_normed, my_gate)
@@ -420,7 +683,7 @@
     ffn_out = lax.psum_scatter(
         forward_dot(act_low, my_down).astype(jnp.bfloat16), "fsdp", scatter_dimension=0, tiled=True
     ).astype(jnp.float32)
-    layer_out = (resid + ffn_out).astype(jnp.bfloat16).reshape(block_len, seq_count, width)
+    layer_out = (resid + ffn_out).astype(jnp.bfloat16).reshape(seq_count, block_len, width)
     grad_act = backward_dot(all_upstream, my_down)
     grad_gate_low = (grad_act * upward * sigmoid_gate * (1.0 + gate * (1.0 - sigmoid_gate))).astype(
         jnp.bfloat16
@@ -463,11 +726,11 @@
     )
     summed_pairs = lax.psum_scatter(grad_pairs, "ctx", scatter_dimension=0, tiled=True)
     summed_pairs = jnp.transpose(
-        summed_pairs.reshape(seq_count, KVH, block_len, 2 * HD), (2, 0, 1, 3)
+        summed_pairs.reshape(seq_count, KVH, block_len, 2 * HD), (0, 2, 1, 3)
     )
     grad_query_low = (
         rotary(
-            unit_rows(grad_q_unit, seq_count, block_len).reshape(block_len, seq_count, H, HD),
+            unit_rows(grad_q_unit, seq_count, block_len).reshape(seq_count, block_len, H, HD),
             positions,
             -1.0,
         )
@@ -488,7 +751,7 @@
     inward_attn, gain_term_attn = norm_back(
         inputs, scale_attn, full_gain_attn.astype(jnp.float32), grad_normed_attn
     )
-    grad_tokens = (grad_resid + inward_attn).reshape(block_len, seq_count, width)
+    grad_tokens = (grad_resid + inward_attn).reshape(seq_count, block_len, width)
 
     def part(acts, grads):
         return jnp.einsum("rc,rn->cn", acts, grads, preferred_element_type=jnp.float32)
@@ -532,8 +795,8 @@
         for first, last in zip(edges[:-1], edges[1:])
     ]
     return (
-        layer_out,
-        grad_tokens,
+        jnp.swapaxes(layer_out, 0, 1),
+        jnp.swapaxes(grad_tokens, 0, 1),
         grad_query,
         grad_key,
         grad_value,

time: 828 us -> 713 us (0.86)
  waiting for transfers between devices: 270 us -> 199 us
  Pallas kernels: 199 us -> 250 us
  local copies, waits for them, and re-layouts: 126 us -> 80.4 us
  starting transfers between devices: 20.8 us -> 0.92 us
  other arithmetic: 42.9 us -> 28.3 us
  matrix products: 70.6 us -> 56.9 us
    pallas_call x0 -> x1, Pallas kernels: none -> 58.7 us  [attend(): pl.pallas_call(attend_kernel, out_shape=[jax.ShapeDtypeStruct((sequences...]
    all_to_all x2 -> x0, waiting for transfers between devices: 56.4 us -> none  [the longest x1 29.6 us: on_device(): lax.all_to_all(own_weights[4], 'fsdp', 1, 0, tiled=True)]
    all_gather x3 -> x1, waiting for transfers between devices: 48.4 us -> 0.01 us  [on_device(): lax.all_gather(weight, 'fsdp', axis=0, tiled=True)]
    all_gather x1, waiting for transfers between devices: 0.02 us -> 22.8 us  [on_device(): all_normed = lax.all_gather(normed_ffn, 'fsdp', axis=0, tiled=True)]
    all_gather x1, waiting for transfers between devices: 0.01 us -> 16.2 us  [on_device(): all_upstream = lax.all_gather(upstream_low, 'fsdp', axis=0, tiled=True)]
    reshape x8 -> x4, local copies, waits for them, and re-layouts: 16.5 us -> 3.54 us  [the longest x1 1.92 us: on_device(): (grad_resid + inward_attn).reshape(seq_count, block_len, width)]
    all_gather x1, starting transfers between devices: 11.7 us -> 0.04 us  [on_device(): all_upstream = lax.all_gather(upstream_low, 'fsdp', axis=0, tiled=True)]
    reduce_scatter x1, waiting for transfers between devices: 38.7 us -> 28.1 us  [on_device(): lax.psum_scatter((backward_dot(grad_gate_low, my_gate) + backward_dot(gra...]
  transfers between devices with their start and end apart: 11 -> 7, of which waited for: 7 -> 5; matrix products, arithmetic and copies ran while one was open for 17% -> 11% of each run, Pallas kernels for 1% -> 0%
where the time goes in v3:
time: 713 us; the launch traced here: 704 us
  Pallas kernels  250 us (35%)
  waiting for transfers between devices  199 us (28%)
  local copies, waits for them, and re-layouts  80.4 us (11%)
  blocking collectives  73 us (10%)
  matrix products  56.9 us (8%)
  other arithmetic  28.3 us (4%)
  between operations  15.7 us (2%)
    pallas_call x1, Pallas kernels, reduce_gradients(): pl.pallas_call(reduce_kernel, out_shape=[jax.ShapeDtypeStruct(shape, jnp....  180 us
    reduce_scatter x1, waiting for transfers between devices, on_device(): lax.psum_scatter(grad_pairs, 'ctx', scatter_dimension=0, tiled=True)  97.8 us
    pallas_call x1, Pallas kernels, attend(): pl.pallas_call(attend_kernel, out_shape=[jax.ShapeDtypeStruct((sequences...  58.7 us
    psum x1, blocking collectives, on_device(): lax.psum(jnp.stack([gain_term_attn, gain_term_ffn]), ('fsdp', 'ctx'))  40.7 us
    reduce_scatter x1, waiting for transfers between devices, on_device(): lax.psum_scatter(forward_dot(act_low, my_down).astype(jnp.bfloat16), 'fsd...  33.6 us
    reduce_scatter x1, waiting for transfers between devices, on_device(): lax.psum_scatter((backward_dot(grad_gate_low, my_gate) + backward_dot(gra...  28.1 us
    unnamed x111, local copies, waits for them, and re-layouts  27.8 us
    all_gather x2, blocking collectives, on_device(): lax.all_gather(weight, 'fsdp', axis=0, tiled=True)  23.3 us
  transfers between devices with their start and end apart: 7, of which 5 were waited for; matrix products, arithmetic and copies ran while one was open for 11% of the time, Pallas kernels for 0%

profile of v3, /device:TPU:0, one launch (start us, length us, event | category | flops | bytes accessed | tf_op | source)
XLA Modules:
  0.0 704.0 jit_solution(5324924638334629321)
XLA Ops:
  11.7 9.1 %all-reduce.6 = (bf16[1152]{0:T(1024)(128)(2,1)S(1)}, bf16[1152]{0:T(1024)(128)(2,1)}) all-reduce(bf16[1152]{0:T(1024)(128)(2,1)S(1)} %dynamic-update-slice, bf16[1152]{0:T(1024)(128)(2,1)S(1)} %dynamic-update-slice.1), channel_id=1, replica_groups=mesh['fsdp'=4,'ctx'=8] {'fsdp'}, use_global_device_ids=true, to_apply=%add.4 | all-reduce | flops 2304 | bytes 9216
  20.7 14.0 %all_gather.23 = bf16[1152,384]{1,0:T(8,128)(2,1)S(1)} all-gather(bf16[288,384]{1,0:T(8,128)(2,1)} %param.13), channel_id=1, replica_groups=mesh['fsdp'=4,'ctx'=8] {'fsdp'}, dimensions={0}, use_global_device_ids=true | all-gather | bytes 1105920 | tf_op jit(solution)/shard_map/all_gather | solution.py:639
  40.1 9.2 %all_gather.24 = bf16[1152,384]{1,0:T(8,128)(2,1)S(1)} all-gather(bf16[288,384]{1,0:T(8,128)(2,1)S(1)} %copy-done.25), channel_id=1, replica_groups=mesh['fsdp'=4,'ctx'=8] {'fsdp'}, dimensions={0}, use_global_device_ids=true | all-gather | bytes 1105920 | tf_op jit(solution)/shard_map/all_gather | solution.py:639
  55.8 5.2 copy.74
  70.1 58.7 %shard_map.194 = (bf16[256,1152]{1,0:T(8,128)(2,1)}, f32[12,64,384]{2,1,0:T(8,128)}, f32[12,1,384]{2,1,0:T(1,128)}, bf16[8,12,128,128]{3,2,1,0:T(8,128)(2,1)}, b...) custom-call(bf16[12,128,384]{2,1,0:T(8,128)(2,1)} %concatenate.36.clone.q_ref, ...), custom_call_target="tpu_custom_call" | custom-call | tf_op jit(solution)/shard_map/pallas_call | solution.py:576
  136.5 22.8 %all-gather.6.cloned.1.call-done = bf16[1024,1152]{1,0:T(8,128)(2,1)} async-done(((bf16[256,1152]{1,0:T(8,128)(2,1)}), bf16[1024,1152]{1,0:T(8,128)(2,1)}) %all-gather.6.cloned.1.call-update) | async-done | bytes 2359312 | tf_op jit(solution)/shard_map/all_gather | solution.py:675
  159.3 6.2 fusion.45
  165.5 3.9 fusion.44
  169.4 16.2 %all-gather.8.cloned.1.call-done = bf16[1024,1152]{1,0:T(8,128)(2,1)} async-done(((bf16[256,1152]{1,0:T(8,128)(2,1)}), bf16[1024,1152]{1,0:T(8,128)(2,1)}) %all-gather.8.cloned.1.call-update) | async-done | bytes 2359312 | tf_op jit(solution)/shard_map/all_gather | solution.py:678
  185.6 7.8 %multiply_convert_fusion = (bf16[1024,768]{1,0:T(8,128)(2,1)S(1)}, bf16[1024,768]{1,0:T(8,128)(2,1)S(1)}, bf16[1024,768]{1,0:T(8,128)(2,1)}) fusion(f32[1024,768]{1,0:T(8,128)} %fusion.44, f32[1024,768]{1,0:T(8,128)} %fusion.45, bf16[1024,1152]{1,0:T(8,128)(2,1)} %all-gather.8.cloned.1.call-done, bf16[768,1152]{1,0:T(8,128)(2,1)S(1)} %copy-done), kind=kOutput, calls=%fused_computation.16 | convolution fusion | flops 1824522240 | bytes 15138816 | tf_op jit(solution)/shard_map/rn,cn->rc/dot_general | solution.py:47
  195.9 3.7 add_convert_fusion
  199.7 5.0 convolution_convert_fusion.2
  204.8 28.1 %reduce-scatter.9.cloned.1.call-done = bf16[256,1152]{1,0:T(8,128)(2,1)} async-done(((bf16[1024,1152]{1,0:T(8,128)(2,1)}), bf16[256,1152]{1,0:T(8,128)(2,1)}) %reduce-scatter.9.cloned.1.call-update) | async-done | bytes 589840 | tf_op jit(solution)/shard_map/reduce_scatter | solution.py:692
  235.4 33.6 %reduce-scatter.7.cloned.1.call-done = bf16[256,1152]{1,0:T(8,128)(2,1)} async-done(((bf16[1024,1152]{1,0:T(8,128)(2,1)}), bf16[256,1152]{1,0:T(8,128)(2,1)}) %reduce-scatter.7.cloned.1.call-update) | async-done | bytes 589840 | tf_op jit(solution)/shard_map/reduce_scatter | solution.py:683
  278.0 10.7 %shard_map.195 = (f32[12,64,384]{2,1,0:T(8,128)}, bf16[8,12,128,128]{3,2,1,0:T(8,128)(2,1)}) custom-call(bf16[12,128,384]{2,1,0:T(8,128)(2,1)} %concatenate.36.clone.q_ref, bf16[12,128,384]{2,1,0:T(8,128)(2,1)} %concatenate.38.clone.g_ref, bf16[12,768,128]{2,1,0:T(8,128)(2,1)} %fusion.2.qg_ref, bf16[8,12,128,128]{3,2,1,0:T(8,128)(2,1)} %get-tuple-element.28.kv_ref, ...), custom_call_target="tpu_custom_call" | custom-call | tf_op jit(solution)/shard_map/pallas_call | solution.py:609
  297.2 97.8 %reduce-scatter.11.cloned.1.call-done = bf16[1,12,128,128]{3,2,1,0:T(8,128)(2,1)} async-done(((bf16[8,12,128,128]{3,2,1,0:T(8,128)(2,1)}), bf16[1,12,128,128]{3,2,1,0:T(8,128)(2,1)}) %reduce-scatter.11.cloned.1.call-update) | async-done | bytes 393232 | tf_op jit(solution)/shard_map/reduce_scatter | solution.py:727
  402.4 10.3 %copy.109 = bf16[1152,3072]{1,0:T(8,128)(2,1)} copy(bf16[1152,3072]{0,1:T(8,128)(2,1)} %pad_maximum_fusion) | data formatting | bytes 14155776
  413.3 5.4 convolution_convert_fusion.4
  418.7 4.9 reshape.325
  430.3 4.9 reshape.324
  438.6 3.5 convolution_convert_fusion.3
  449.0 40.7 %psum.7 = f32[2,1152]{1,0:T(2,128)S(1)} all-reduce(f32[2,1152]{1,0:T(2,128)S(1)} %pad_maximum_fusion.1), channel_id=1, replica_groups=mesh['fsdp'=4,'ctx'=8] {'fsdp','ctx'}, use_global_device_ids=true, to_apply=%region_10.0 | all-reduce | flops 2304 | bytes 18432 | tf_op jit(solution)/shard_map/psum | solution.py:789
  495.5 180.2 %shard_map.196 = (bf16[24,288,128]{2,1,0:T(8,128)(2,1)}, bf16[24,288,128]{2,1,0:T(8,128)(2,1)}, bf16[48,16,1152]{2,1,0:T(8,128)(2,1)}, bf16[24,288,128]{2,1,0:T(8,128)(2,1)}) custom-call(bf16[4,6,288,128]{3,2,1,0:T(8,128)(2,1)} %bitcast.198, bf16[4,6,288,128]{3,2,1,0:T(8,128)(2,1)} %bitcast.197, bf16[48,16,1152]{2,1,0:T(8,128)(2,1)} %bitcast.219, ...), custom_call_target="tpu_custom_call" | custom-call | tf_op jit(solution)/shard_map/pallas_call | solution.py:249
  692.3 3.6 bitcast_convert_fusion
  (205 shorter events, 103.1 us)
Async XLA Ops:
  7.2 178.4 %copy-start = (bf16[768,1152]{1,0:T(8,128)(2,1)S(1)}, bf16[768,1152]{1,0:T(8,128)(2,1)}, u32[]{:S(2)}) copy-start(bf16[768,1152]{1,0:T(8,128)(2,1)} %param.18) | copy-start | bytes 5308420
  7.2 29.1 %copy-start.2 = (bf16[128,2,1152]{2,1,0:T(2,128)(2,1)S(1)}, bf16[128,2,1152]{2,1,0:T(2,128)(2,1)}, u32[]{:S(2)}) copy-start(bf16[128,2,1152]{2,1,0:T(2,128)(2,1)} %param.11) | copy-start | bytes 1769476
  7.2 48.6 %all-gather.4.cloned.1.call-start = ((), (), s32[]{:S(2)}) async-start(), calls=%async_computation.4 | async-start | bytes 3317760 | tf_op jit(solution)/shard_map/all_gather | solution.py:639
  7.9 151.4 %all-gather.6.cloned.1.call-start = ((), (), s32[]{:S(2)}) async-start(), calls=%async_computation.5 | async-start | bytes 2949120 | tf_op jit(solution)/shard_map/all_gather | solution.py:675
  20.7 28.6 %copy-start.26 = (f32[1152]{0:T(1024)}, f32[1152]{0:T(1024)S(1)}, u32[]{:S(2)}) copy-start(f32[1152]{0:T(1024)S(1)} %convert_element_type.197) | copy-start | bytes 13828
  37.1 12.3 %copy-start.36 = (f32[256]{0:T(256)}, f32[256]{0:T(256)S(1)}, u32[]{:S(2)}) copy-start(f32[256]{0:T(256)S(1)} %get-tuple-element.91) | copy-start | bytes 3076
  38.0 23.0 %copy-start.4 = (bf16[2,128,1152]{2,1,0:T(8,128)(2,1)}, bf16[2,128,1152]{2,1,0:T(8,128)(2,1)S(1)}, u32[]{:S(2)}) copy-start(bf16[2,128,1152]{2,1,0:T(8,128)(2,1)S(1)} %fusion.13) | copy-start | bytes 1769476
  66.6 3.5 copy-start.7
  70.1 58.7 %copy-start.16 = (f32[128,2,1152]{2,0,1:T(8,128)S(1)}, f32[128,2,1152]{2,0,1:T(8,128)}, u32[]{:S(2)}) copy-start(f32[128,2,1152]{2,0,1:T(8,128)} %copy_convert_fusion) | copy-start | bytes 3538948
  128.8 4.2 copy-start.31
  134.0 51.6 %all-gather.8.cloned.1.call-start = ((), (), s32[]{:S(2)}) async-start(), calls=%async_computation.7 | async-start | bytes 2949120 | tf_op jit(solution)/shard_map/all_gather | solution.py:678
  136.0 96.9 %reduce-scatter.9.cloned.1.call-start = ((), (), s32[]{:S(2)}) async-start(), calls=%async_computation.8 | async-start | bytes 2949120 | tf_op jit(solution)/shard_map/reduce_scatter | solution.py:692
  159.3 6.2 copy-start.40
  159.3 6.2 copy-start.44
  185.5 7.8 %copy-start.45 = (bf16[1152,768]{1,0:T(8,128)(2,1)S(1)}, bf16[1152,768]{1,0:T(8,128)(2,1)}, u32[]{:S(2)}) copy-start(bf16[1152,768]{1,0:T(8,128)(2,1)} %get-tuple-element.26) | copy-start | bytes 5308420
  199.6 69.4 %reduce-scatter.7.cloned.1.call-start = ((), (), s32[]{:S(2)}) async-start(), calls=%async_computation.6 | async-start | bytes 2949120 | tf_op jit(solution)/shard_map/reduce_scatter | solution.py:683
  204.7 28.1 %copy-start.32 = (f32[1152]{0:T(1024)S(1)}, f32[1152]{0:T(1024)}, u32[]{:S(2)}) copy-start(f32[1152]{0:T(1024)} %convert_element_type.202) | copy-start | bytes 13828
  204.7 28.1 %copy-start.35 = (f32[256]{0:T(256)S(1)}, f32[256]{0:T(256)}, u32[]{:S(2)}) copy-start(f32[256]{0:T(256)} %copy-done.34) | copy-start | bytes 3076
  204.7 64.4 %copy-start.15 = (bf16[2,128,1152]{2,1,0:T(8,128)(2,1)S(1)}, bf16[2,128,1152]{2,1,0:T(8,128)(2,1)}, u32[]{:S(2)}) copy-start(bf16[2,128,1152]{2,1,0:T(8,128)(2,1)} %copy.83) | copy-start | bytes 1769476
  204.7 190.3 %reduce-scatter.11.cloned.1.call-start = ((), (), s32[]{:S(2)}) async-start(), calls=%async_computation.9 | async-start | bytes 3538944 | tf_op jit(solution)/shard_map/reduce_scatter | solution.py:727
  288.7 201.6 %reduce-scatter.13.cloned.1.call-start = ((), (), s32[]{:S(2)}) async-start(), calls=%async_computation.10 | async-start | bytes 8847360
  438.6 3.5 copy-start.21
  438.6 4.9 copy-start.20
  692.3 4.6 copy-start.1
  (33 other events, 66.0 us)
Sparse Core Ops, SparseCore 0:
  9.6 33.2 all-gather.3
  134.1 25.1 all-gather.5
  161.4 24.0 all-gather.7
  199.8 33.0 reduce-scatter.8
  236.0 33.0 reduce-scatter.6
  288.9 106.1 reduce-scatter.10
  412.8 63.5 reduce-scatter.12

commit v4 on v3

--- a/solution.py
+++ b/solution.py
@@ -273,6 +273,14 @@
     return jnp.swapaxes(matrix.reshape(rows, columns // LANES, LANES), 0, 1)
 
 
+def from_parts(parts, rows, columns):
+    group = lax.axis_size("fsdp")
+    wide = columns // group // LANES
+    split = parts.reshape(group, -1, 16, LANES)[:, : wide * (rows // 16)]
+    split = split.reshape(group, wide, rows // 16, 16, LANES)
+    return jnp.transpose(split, (2, 3, 0, 1, 4)).reshape(rows, columns).astype(jnp.float32)
+
+
 def from_blocks(blocks, first, count):
     part = jnp.swapaxes(blocks[first : first + count], 0, 1)
     return part.reshape(part.shape[0], count * LANES).astype(jnp.float32)
@@ -388,10 +396,10 @@
 
 
 def attend_kernel(
-    q_ref, kv_ref, out_ref, gate_ref, up_ref,
-    low_ref, mix_ref, log_ref, all_ref, full_out_ref, my_gate_ref, my_up_ref,
+    q_ref, kv_ref, out_ref, gate_ref, up_ref, g_ref,
+    low_ref, mix_ref, log_ref, all_ref, full_out_ref, my_gate_ref, my_up_ref, all_g_ref,
     top_ref, total_ref, chain_sends, chain_arrivals, peer_sends, peer_arrivals,
-    out_sends, out_arrivals, part_sends, part_arrivals, local_sems,
+    out_sends, out_arrivals, g_sends, g_arrivals, part_sends, part_arrivals, local_sems,
 ):
     steps = Steps()
     fsdp, ctx, group = steps.fsdp, steps.ctx, lax.axis_size("fsdp")
@@ -443,7 +451,11 @@
         lambda shard: full_out_ref.at[pl.ds(shard * rows, rows)], out_sends, out_arrivals
     )
     gathered.start(out_ref)
-    background = []
+    gathered_g = GroupGather(lambda shard: all_g_ref.at[shard], g_sends, g_arrivals)
+    gathered_g.start(g_ref)
+    own_g = pltpu.make_async_copy(g_ref, all_g_ref.at[fsdp], local_sems.at[3])
+    own_g.start()
+    background = [own_g]
     own_rows = pl.ds(fsdp * rows, rows)
     own_out = pltpu.make_async_copy(out_ref, full_out_ref.at[own_rows], local_sems.at[2])
     own_out.start()
@@ -542,6 +554,7 @@
                 sequence * keys : (sequence + 1) * keys, pair * 2 * HD : (pair + 1) * 2 * HD
             ] = tile.astype(low_ref.dtype)
     gathered.finish()
+    gathered_g.finish()
     for copy in background:
         copy.wait()
 
@@ -565,7 +578,7 @@
 VMEM = pl.BlockSpec(memory_space=pltpu.VMEM)
 
 
-def attend(q_wide, pairs, w_out, w_gate, w_up):
+def attend(q_wide, pairs, w_out, w_gate, w_up, g_rows):
     group, count = lax.axis_size("fsdp"), lax.axis_size("ctx")
     units, deep, wide = q_wide.shape
     keys = pairs.shape[1]
@@ -583,9 +596,10 @@
             jax.ShapeDtypeStruct((group * rows, width), jnp.bfloat16),
             jax.ShapeDtypeStruct((group * rows, hidden), jnp.bfloat16),
             jax.ShapeDtypeStruct((group * rows, hidden), jnp.bfloat16),
+            jax.ShapeDtypeStruct((group,) + g_rows.shape, jnp.bfloat16),
         ],
-        in_specs=[VMEM, VMEM, ANY, ANY, ANY],
-        out_specs=[VMEM, VMEM, VMEM, VMEM, ANY, ANY, ANY],
+        in_specs=[VMEM, VMEM, ANY, ANY, ANY, ANY],
+        out_specs=[VMEM, VMEM, VMEM, VMEM, ANY, ANY, ANY, ANY],
         scratch_shapes=[
             pltpu.VMEM((units, 1, wide), jnp.float32),
             pltpu.VMEM((units, 1, wide), jnp.float32),
@@ -593,16 +607,328 @@
             dma((count // 2 + 1, PARTS)),
             dma((count // 2, PARTS)),
             dma((count // 2, PARTS)),
-            group_semaphores(),
-            group_semaphores(),
+            *[group_semaphores()] * 4,
             dma((2, group - 1)),
             dma((2, group - 1)),
-            dma((3,)),
+            dma((4,)),
         ],
         compiler_params=pltpu.CompilerParams(
             collective_id=1, has_side_effects=True, vmem_limit_bytes=56 << 20
         ),
-    )(q_wide, pairs, w_out, w_gate, w_up)
+    )(q_wide, pairs, w_out, w_gate, w_up, g_rows)
+
+
+class GroupScatter:
+    def __init__(self, give_sib, got_sib, give_cross, got_cross, far, got_far, sends, arrivals):
+        self.give_sib, self.got_sib = give_sib, got_sib
+        self.give_cross, self.got_cross = give_cross, got_cross
+        self.far, self.got_far = far, got_far
+        self.sends, self.arrivals = sends, arrivals
+        self.fsdp, self.ctx = lax.axis_index("fsdp"), lax.axis_index("ctx")
+        self.chips = lax.axis_size("fsdp") // 2
+        self.chip, self.core = lax.div(self.fsdp, 2), lax.rem(self.fsdp, 2)
+        self.sibling = 2 * self.chip + 1 - self.core
+
+    def copy(self, source, target, semaphore, device):
+        return pltpu.make_async_remote_copy(
+            src_ref=source,
+            dst_ref=target,
+            send_sem=self.sends.at[semaphore],
+            recv_sem=self.arrivals.at[semaphore],
+            device_id=(device, self.ctx),
+            device_id_type=MESH,
+        )
+
+    def to_sibling(self):
+        return self.copy(self.give_sib, self.got_sib, 0, self.sibling)
+
+    def to_cross(self, step):
+        return self.copy(
+            self.give_cross.at[step - 1], self.got_cross.at[step - 1], step, self.sibling
+        )
+
+    def to_far(self, step):
+        chip = lax.rem(self.chip + self.chips - step, self.chips)
+        return self.copy(
+            self.far.at[step - 1],
+            self.got_far.at[step - 1],
+            self.chips - 1 + step,
+            2 * chip + self.core,
+        )
+
+    def add_cross(self, step):
+        self.to_cross(step).wait_recv()
+        held = self.far.at[step - 1]
+        held[...] = (
+            held[...].astype(jnp.float32) + self.got_cross[step - 1].astype(jnp.float32)
+        ).astype(held.dtype)
+        self.to_far(step).start()
+
+    def total(self, own):
+        self.to_sibling().wait_recv()
+        value = own + self.got_sib[...].astype(jnp.float32)
+        for step in range(1, self.chips):
+            self.to_far(step).wait_recv()
+            value = value + self.got_far[step - 1].astype(jnp.float32)
+        return value
+
+    def sent(self):
+        self.to_sibling().wait_send()
+        for step in range(1, self.chips):
+            self.to_cross(step).wait_send()
+            self.to_far(step).wait_send()
+
+
+def scatter_scratch(rows, width):
+    far = lax.axis_size("fsdp") // 2 - 1
+    one, many = (rows, width), (far, rows, width)
+    return [pltpu.VMEM(shape, jnp.bfloat16) for shape in (one, one, many, many, many, many)]
+
+
+def dot_columns(left, right):
+    return lax.dot_general(
+        left, right, (((1,), (1,)), ((), ())), preferred_element_type=jnp.float32
+    )
+
+
+def tiles(count, body):
+    def step(at, unused):
+        body(at)
+        return unused
+
+    lax.fori_loop(0, count, step, 0)
+
+
+def lane_tile(at, size):
+    return pl.ds(pl.multiple_of(at * size, LANES), size)
+
+
+def width_tile(width):
+    return 384 if width % 384 == 0 else width
+
+
+def hidden_tile(hidden):
+    return 256 if hidden % 256 == 0 else 128
+
+
+def transpose_into(target, source):
+    rows, columns = source.shape
+
+    def body(at):
+        part = source[:, lane_tile(at, LANES)]
+        target[pl.ds(pl.multiple_of(at * LANES, LANES), LANES), :] = part.T
+
+    tiles(columns // LANES, body)
+
+
+def ffn_kernel(
+    x_ref, low_ref, out_ref, gate_ref, up_ref, down_ref, all_g_ref, gain_ref,
+    layer_ref, resid_grad_ref, branch_ref, g_wide_ref, gate_part_ref, up_part_ref, down_part_ref,
+    gain_grad_ref,
+    all_n_ref, turned_n, turned_act, act_ref, gate_grad, up_grad, resid_ref, layer_own, grad_own,
+    *rest,
+):
+    down_scratch, grad_scratch = rest[:6], rest[6:12]
+    n_sends, n_arrivals, down_sends, down_arrivals, grad_sends, grad_arrivals = rest[12:]
+    group = lax.axis_size("fsdp")
+    rows, width = x_ref.shape
+    hidden = gate_ref.shape[1]
+    barrier = pltpu.get_barrier_semaphore()
+    greeted = greet_group(barrier)
+    step_in, step_out = hidden_tile(hidden), width_tile(width)
+
+    def branch(at):
+        columns = lane_tile(at, step_out)
+        resid_ref[:, columns] = x_ref[:, columns].astype(jnp.float32) + forward_dot(
+            low_ref[...], out_ref[:, columns]
+        )
+
+    tiles(width // step_out, branch)
+    gain = gain_ref[...]
+    scale = norm_scale(resid_ref[...])
+    gathered = GroupGather(lambda shard: all_n_ref.at[shard], n_sends, n_arrivals)
+    fsdp, chips = gathered.fsdp, gathered.chips
+    all_n_ref[fsdp] = (resid_ref[...] * scale * gain).astype(jnp.bfloat16)
+    pl.semaphore_wait(barrier, greeted)
+    gathered.start(all_n_ref.at[fsdp])
+    layer_sum = GroupScatter(*down_scratch, down_sends, down_arrivals)
+    grad_sum = GroupScatter(*grad_scratch, grad_sends, grad_arrivals)
+
+    def hidden_part(shard):
+        def body(at):
+            columns = lane_tile(at, step_in)
+            normed = all_n_ref[shard]
+            gate = forward_dot(normed, gate_ref[:, columns])
+            upward = forward_dot(normed, up_ref[:, columns])
+            grad_act = dot_columns(
+                all_g_ref[shard], down_ref[pl.ds(pl.multiple_of(at * step_in, LANES), step_in), :]
+            )
+            sigmoid = jax.nn.sigmoid(gate)
+            silu = gate * sigmoid
+            act_ref[shard, :, columns] = (silu * upward).astype(jnp.bfloat16)
+            gate_grad[shard, :, columns] = (
+                grad_act * upward * (sigmoid * (1.0 + gate * (1.0 - sigmoid)))
+            ).astype(jnp.bfloat16)
+            up_grad[shard, :, columns] = (grad_act * silu).astype(jnp.bfloat16)
+
+        tiles(hidden // step_in, body)
+
+    def grad_part(shard, target):
+        def body(at):
+            columns = pl.ds(pl.multiple_of(at * step_out, LANES), step_out)
+            target[:, columns] = (
+                dot_columns(gate_grad[shard], gate_ref[columns, :])
+                + dot_columns(up_grad[shard], up_ref[columns, :])
+            ).astype(target.dtype)
+
+        tiles(width // step_out, body)
+
+    def layer_part(shard, target):
+        def body(at):
+            columns = lane_tile(at, step_out)
+            target[:, columns] = forward_dot(act_ref[shard], down_ref[:, columns]).astype(
+                target.dtype
+            )
+
+        tiles(width // step_out, body)
+
+    hidden_part(fsdp)
+    gathered.sibling_here()
+    sibling = gathered.sibling
+    hidden_part(sibling)
+    grad_part(sibling, grad_sum.give_sib)
+    grad_sum.to_sibling().start()
+    layer_part(sibling, layer_sum.give_sib)
+    layer_sum.to_sibling().start()
+    gathered.forward()
+    grad_part(fsdp, grad_own)
+    layer_part(fsdp, layer_own)
+    for step in range(1, chips):
+        ours = gathered.same_core(chips - step)
+        theirs = ours + sibling - fsdp
+        gathered.crossed(step)
+        hidden_part(theirs)
+        grad_part(theirs, grad_sum.give_cross.at[step - 1])
+        grad_sum.to_cross(step).start()
+        hidden_part(ours)
+        grad_part(ours, grad_sum.far.at[step - 1])
+        grad_sum.add_cross(step)
+        layer_part(theirs, layer_sum.give_cross.at[step - 1])
+        layer_sum.to_cross(step).start()
+        layer_part(ours, layer_sum.far.at[step - 1])
+        layer_sum.add_cross(step)
+
+    for shard in range(group):
+        span = slice(shard * rows, (shard + 1) * rows)
+        transpose_into(turned_n.at[:, span], all_n_ref.at[shard])
+        transpose_into(turned_act.at[:, span], act_ref.at[shard])
+
+    def down_tile(at):
+        columns = lane_tile(at, step_out)
+        down_part_ref[:, columns] = forward_dot(
+            turned_act[...], all_g_ref[:, :, columns].reshape(group * rows, step_out)
+        ).astype(jnp.bfloat16)
+
+    tiles(width // step_out, down_tile)
+    own = width // group
+    row_blocks = own // 16
+    for source, target in ((gate_grad, gate_part_ref), (up_grad, up_part_ref)):
+
+        def weight_tile(at):
+            columns = lane_tile(at, step_in)
+            part = forward_dot(
+                turned_n[...], source[:, :, columns].reshape(group * rows, step_in)
+            ).astype(jnp.bfloat16)
+            for block in range(step_in // LANES):
+                first = (at * (step_in // LANES) + block) * row_blocks
+                for owner in range(group):
+                    target[owner, pl.ds(first, row_blocks)] = part[
+                        owner * own : (owner + 1) * own, block * LANES : (block + 1) * LANES
+                    ].reshape(row_blocks, 16, LANES)
+
+        tiles(hidden // step_in, weight_tile)
+        filled = hidden // LANES * row_blocks
+        for spare in range(filled, target.shape[1]):
+            for owner in range(group):
+                target[owner, spare] = jnp.zeros(target.shape[2:], target.dtype)
+
+    upstream = grad_sum.total(grad_own[...])
+    resid = resid_ref[...]
+    scaled = upstream * gain
+    grad_resid = (
+        all_g_ref[fsdp].astype(jnp.float32)
+        + scale * scaled
+        - resid * scale**3 * jnp.mean(scaled * resid, axis=-1, keepdims=True)
+    )
+    gain_grad_ref[...] = jnp.sum(upstream * resid * scale, axis=0, keepdims=True)
+    resid_grad_ref[...] = grad_resid
+    branch_ref[...] = grad_resid.astype(jnp.bfloat16)
+    units, _, wide = g_wide_ref.shape
+    sequences = units // KVH
+    keys = rows // sequences
+    groups = wide // keys
+    g_wide_ref[:, :HD, :] = jnp.zeros((units, HD, wide), g_wide_ref.dtype)
+    for pair in range(H // 2):
+        columns = slice(pair * 2 * HD, (pair + 1) * 2 * HD)
+        mixed = dot_columns(branch_ref[...], out_ref[columns, :]).astype(jnp.bfloat16)
+        for sequence in range(sequences):
+            turned = mixed[sequence * keys : (sequence + 1) * keys].T
+            for half in range(2):
+                head = 2 * pair + half
+                unit, member = sequence * KVH + head // groups, head % groups
+                g_wide_ref[unit, HD:, member * keys : (member + 1) * keys] = turned[
+                    half * HD : (half + 1) * HD
+                ]
+    layer_ref[...] = (resid + layer_sum.total(layer_own[...])).astype(jnp.bfloat16)
+    gathered.sent()
+    grad_sum.sent()
+    layer_sum.sent()
+
+
+def spread(blocks, count):
+    return -(-blocks // count) * count
+
+
+def feed_forward(x, low, full_out, my_gate, my_up, my_down, all_g, gain, units, wide):
+    group, count = lax.axis_size("fsdp"), lax.axis_size("ctx")
+    rows, width = x.shape
+    hidden = my_gate.shape[1]
+    blocks = spread(hidden // LANES * (width // group // 16), count)
+    chips = group // 2
+    dma = pltpu.SemaphoreType.DMA((2 * chips - 1,))
+    bf16 = jnp.bfloat16
+    return pl.pallas_call(
+        ffn_kernel,
+        out_shape=[
+            jax.ShapeDtypeStruct((rows, width), bf16),
+            jax.ShapeDtypeStruct((rows, width), jnp.float32),
+            jax.ShapeDtypeStruct((rows, width), bf16),
+            jax.ShapeDtypeStruct((units, 2 * HD, wide), bf16),
+            jax.ShapeDtypeStruct((group, blocks, 16, LANES), bf16),
+            jax.ShapeDtypeStruct((group, blocks, 16, LANES), bf16),
+            jax.ShapeDtypeStruct((hidden, width), bf16),
+            jax.ShapeDtypeStruct((1, width), jnp.float32),
+        ],
+        in_specs=[VMEM] * 8,
+        out_specs=[VMEM] * 8,
+        scratch_shapes=[
+            pltpu.VMEM((group, rows, width), bf16),
+            pltpu.VMEM((width, group * rows), bf16),
+            pltpu.VMEM((hidden, group * rows), bf16),
+            pltpu.VMEM((group, rows, hidden), bf16),
+            pltpu.VMEM((group, rows, hidden), bf16),
+            pltpu.VMEM((group, rows, hidden), bf16),
+            pltpu.VMEM((rows, width), jnp.float32),
+            pltpu.VMEM((rows, width), jnp.float32),
+            pltpu.VMEM((rows, width), jnp.float32),
+            *scatter_scratch(rows, width),
+            *scatter_scratch(rows, width),
+            *[dma] * 6,
+        ],
+        compiler_params=pltpu.CompilerParams(
+            collective_id=2, has_side_effects=True, vmem_limit_bytes=60 << 20
+        ),
+    )(x, low, full_out, my_gate, my_up, my_down, all_g, gain)
 
 
 def call(kernel, outs, *args):
@@ -644,7 +970,9 @@
     my_down = w_down
     my_start = lax.axis_index("ctx") * block_len
     positions = my_start + jnp.arange(block_len, dtype=jnp.int32)
-    inputs = jnp.swapaxes(tokens, 0, 1).reshape(rows_count, width).astype(jnp.float32)
+    x_rows = jnp.swapaxes(tokens, 0, 1).reshape(rows_count, width)
+    g_rows = jnp.swapaxes(cotangent, 0, 1).reshape(rows_count, width)
+    inputs = x_rows.astype(jnp.float32)
     scale_attn = norm_scale(inputs)
     normed_attn = (inputs * scale_attn * full_gain_attn.astype(jnp.float32)).astype(jnp.bfloat16)
     query_raw = forward_dot(normed_attn, full_query)
@@ -666,51 +994,24 @@
     ).reshape(units, block_len, 2 * HD)
     q_unit = unit_columns(queries * jnp.bfloat16(HD ** (-0.5)), seq_count, block_len)
     q_wide = jnp.concatenate([q_unit, jnp.zeros_like(q_unit)], axis=1)
-    attn_low, mix_unit, log_total, all_pairs, full_out, my_gate, my_up = attend(
-        q_wide, pairs, w_out, w_gate, w_up
-    )
-    resid = inputs + forward_dot(attn_low, full_out)
-    scale_ffn = norm_scale(resid)
-    normed_ffn = (resid * scale_ffn * full_gain_ffn.astype(jnp.float32)).astype(jnp.bfloat16)
-    all_normed = lax.all_gather(normed_ffn, "fsdp", axis=0, tiled=True)
-    upstream_low = jnp.swapaxes(cotangent, 0, 1).reshape(rows_count, width)
-    upstream = upstream_low.astype(jnp.float32)
-    all_upstream = lax.all_gather(upstream_low, "fsdp", axis=0, tiled=True)
-    gate = forward_dot(all_normed, my_gate)
-    upward = forward_dot(all_normed, my_up)
-    sigmoid_gate = jax.nn.sigmoid(gate)
-    act_low = (gate * sigmoid_gate * upward).astype(jnp.bfloat16)
-    ffn_out = lax.psum_scatter(
-        forward_dot(act_low, my_down).astype(jnp.bfloat16), "fsdp", scatter_dimension=0, tiled=True
-    ).astype(jnp.float32)
-    layer_out = (resid + ffn_out).astype(jnp.bfloat16).reshape(seq_count, block_len, width)
-    grad_act = backward_dot(all_upstream, my_down)
-    grad_gate_low = (grad_act * upward * sigmoid_gate * (1.0 + gate * (1.0 - sigmoid_gate))).astype(
-        jnp.bfloat16
-    )
-    grad_up_low = (grad_act * gate * sigmoid_gate).astype(jnp.bfloat16)
-    grad_normed_ffn = lax.psum_scatter(
-        (backward_dot(grad_gate_low, my_gate) + backward_dot(grad_up_low, my_up)).astype(
-            jnp.bfloat16
-        ),
-        "fsdp",
-        scatter_dimension=0,
-        tiled=True,
-    ).astype(jnp.float32)
-    inward_ffn, gain_term_ffn = norm_back(
-        resid, scale_ffn, full_gain_ffn.astype(jnp.float32), grad_normed_ffn
-    )
-    grad_resid = upstream + inward_ffn
-    grad_branch = grad_resid.astype(jnp.bfloat16)
-    grad_mix = backward_dot(grad_branch, full_out).astype(jnp.bfloat16)
-    g_unit = unit_columns(grad_mix, seq_count, block_len)
-    g_wide = jnp.concatenate([jnp.zeros_like(g_unit), g_unit], axis=1)
-    q_rows, g_rows = jnp.swapaxes(q_unit, 1, 2), jnp.swapaxes(g_unit, 1, 2)
-    blank = jnp.zeros_like(q_rows)
-    qg = jnp.concatenate(
-        [jnp.concatenate([q_rows, blank], axis=2), jnp.concatenate([blank, g_rows], axis=2)],
-        axis=1,
-    )
+    attn_low, mix_unit, log_total, all_pairs, full_out, my_gate, my_up, all_g = attend(
+        q_wide, pairs, w_out, w_gate, w_up, g_rows
+    )
+    layer_out, grad_resid, grad_branch, g_wide, gate_part, up_part, down_part, gain_term_ffn = (
+        feed_forward(
+            x_rows,
+            attn_low,
+            full_out,
+            my_gate,
+            my_up,
+            w_down,
+            all_g,
+            full_gain_ffn.astype(jnp.float32)[None],
+            units,
+            wide,
+        )
+    )
+    qg = jnp.concatenate([jnp.swapaxes(q_wide, 1, 2), jnp.swapaxes(g_wide, 1, 2)], axis=1)
     grad_q_unit, grad_pairs = call(
         attend_back_kernel,
         [
@@ -751,6 +1052,7 @@
     inward_attn, gain_term_attn = norm_back(
         inputs, scale_attn, full_gain_attn.astype(jnp.float32), grad_normed_attn
     )
+    layer_out = layer_out.reshape(seq_count, block_len, width)
     grad_tokens = (grad_resid + inward_attn).reshape(seq_count, block_len, width)
 
     def part(acts, grads):
@@ -771,22 +1073,13 @@
         scatter_dimension=0,
         tiled=True,
     )
-    gate_part = part(all_normed, grad_gate_low).astype(jnp.bfloat16)
-    up_part = part(all_normed, grad_up_low).astype(jnp.bfloat16)
-    down_part = part(act_low, all_upstream).astype(jnp.bfloat16)
-
-    def by_owner(matrix):
-        rows, columns = matrix.shape
-        split = matrix.reshape(group, rows // group, columns // LANES, LANES)
-        return jnp.swapaxes(split, 1, 2)
-
     gate_sum, up_sum, down_sum, rest_sum = reduce_gradients(
-        by_owner(gate_part),
-        by_owner(up_part),
+        gate_part,
+        up_part,
         down_part.reshape(-1, 16, width),
         lane_blocks(rest_part),
     )
-    gains = lax.psum(jnp.stack([gain_term_attn, gain_term_ffn]), ("fsdp", "ctx"))
+    gains = lax.psum(jnp.stack([gain_term_attn, gain_term_ffn[0]]), ("fsdp", "ctx"))
     own = gain_attn.shape[0]
     gains = lax.dynamic_slice_in_dim(gains, lax.axis_index("fsdp") * own, own, 1)
     edges = [0, width, width + kv_width, width + 2 * kv_width, 2 * width + 2 * kv_width]
@@ -801,8 +1094,8 @@
         grad_key,
         grad_value,
         grad_out,
-        from_blocks(gate_sum, 0, FF // LANES),
-        from_blocks(up_sum, 0, FF // LANES),
+        from_parts(gate_sum, gain_attn.shape[0], FF),
+        from_parts(up_sum, gain_attn.shape[0], FF),
         down_sum.reshape(-1, width)[: w_down.shape[0]].astype(jnp.float32),
         gains[0],
         gains[1],

time: 713 us -> 639 us (0.90)
  waiting for transfers between devices: 199 us -> 113 us
  Pallas kernels: 250 us -> 329 us
  matrix products: 56.9 us -> 8.6 us
  other arithmetic: 28.3 us -> 19.2 us
  local copies, waits for them, and re-layouts: 80.4 us -> 73.1 us
    pallas_call x0 -> x1, Pallas kernels: none -> 63 us  [feed_forward(): pl.pallas_call(ffn_kernel, out_shape=[jax.ShapeDtypeStruct((rows, width),...]
    reduce_scatter x2 -> x0, waiting for transfers between devices: 61.7 us -> none  [the longest x1 33.6 us: on_device(): lax.psum_scatter(forward_dot(act_low, my_down).astype(jnp.bfloat16), 'fsd...]
    all_gather x2 -> x0, waiting for transfers between devices: 39 us -> none  [the longest x1 22.8 us: on_device(): all_normed = lax.all_gather(normed_ffn, 'fsdp', axis=0, tiled=True)]
    dot_general x7 -> x3, matrix products: 21.8 us -> 1.96 us  [forward_dot(): return jnp.dot(left, right, preferred_element_type=jnp.float32)]
    convert_element_type x1 -> x4, local copies, waits for them, and re-layouts: 0.25 us -> 18.6 us  [from_parts(): jnp.transpose(split, (2, 3, 0, 1, 4)).reshape(rows, columns)]
    reshape x6 -> x1, local copies, waits for them, and re-layouts: 18.1 us -> 2.79 us  [on_device(): layer_out = layer_out.reshape(seq_count, block_len, width)]
    dot_general x7 -> x3, matrix products: 17.2 us -> 2.37 us  [backward_dot(): jnp.einsum('rn,cn->rc', grad, weight, preferred_element_type=jnp.float32)]
    dot_general x7 -> x4, matrix products: 18 us -> 4.27 us  [part(): jnp.einsum('rc,rn->cn', acts, grads, preferred_element_type=jnp.float32)]
  transfers between devices with their start and end apart: 7 -> 3, of which waited for: 5 -> 2; matrix products, arithmetic and copies ran while one was open for 11% -> 4% of each run, Pallas kernels for 0% -> 0%
where the time goes in v4:
time: 639 us; the launch traced here: 632 us
  Pallas kernels  329 us (51%)
  waiting for transfers between devices  113 us (18%)
  local copies, waits for them, and re-layouts  73.1 us (11%)
  blocking collectives  72.9 us (11%)
  other arithmetic  19.2 us (3%)
  between operations  15.4 us (2%)
  matrix products  8.6 us (1%)
    pallas_call x1, Pallas kernels, reduce_gradients(): pl.pallas_call(reduce_kernel, out_shape=[jax.ShapeDtypeStruct(shape, jnp....  184 us
    reduce_scatter x1, waiting for transfers between devices, on_device(): lax.psum_scatter(grad_pairs, 'ctx', scatter_dimension=0, tiled=True)  99.4 us
    pallas_call x1, Pallas kernels, attend(): pl.pallas_call(attend_kernel, out_shape=[jax.ShapeDtypeStruct((sequences...  71.9 us
    pallas_call x1, Pallas kernels, feed_forward(): pl.pallas_call(ffn_kernel, out_shape=[jax.ShapeDtypeStruct((rows, width),...  63 us
    psum x1, blocking collectives, on_device(): lax.psum(jnp.stack([gain_term_attn, gain_term_ffn[0]]), ('fsdp', 'ctx'))  40.5 us
    unnamed x75, local copies, waits for them, and re-layouts  26 us
    all_gather x2, blocking collectives, on_device(): lax.all_gather(weight, 'fsdp', axis=0, tiled=True)  23.3 us
    convert_element_type x4, local copies, waits for them, and re-layouts, from_parts(): jnp.transpose(split, (2, 3, 0, 1, 4)).reshape(rows, columns)  18.6 us
  transfers between devices with their start and end apart: 3, of which 2 were waited for; matrix products, arithmetic and copies ran while one was open for 4% of the time, Pallas kernels for 0%

profile of v4, /device:TPU:0, one launch (start us, length us, event | category | flops | bytes accessed | tf_op | source)
XLA Modules:
  0.0 631.6 jit_solution(8807133303930324401)
XLA Ops:
  11.6 9.1 %all-reduce.3 = (bf16[1152]{0:T(1024)(128)(2,1)}, bf16[1152]{0:T(1024)(128)(2,1)S(1)}) all-reduce(bf16[1152]{0:T(1024)(128)(2,1)S(1)} %dynamic-update-slice.1, bf16[1152]{0:T(1024)(128)(2,1)S(1)} %dynamic-update-slice), channel_id=1, replica_groups=mesh['fsdp'=4,'ctx'=8] {'fsdp'}, use_global_device_ids=true, to_apply=%add.2 | all-reduce | flops 2304 | bytes 9216
  21.3 14.1 %all_gather.17 = bf16[1152,384]{1,0:T(8,128)(2,1)S(1)} all-gather(bf16[288,384]{1,0:T(8,128)(2,1)} %param.13), channel_id=1, replica_groups=mesh['fsdp'=4,'ctx'=8] {'fsdp'}, dimensions={0}, use_global_device_ids=true | all-gather | bytes 1105920 | tf_op jit(solution)/shard_map/all_gather | solution.py:965
  39.1 9.3 %all_gather.18 = bf16[1152,384]{1,0:T(8,128)(2,1)S(1)} all-gather(bf16[288,384]{1,0:T(8,128)(2,1)S(1)} %copy-done.20), channel_id=1, replica_groups=mesh['fsdp'=4,'ctx'=8] {'fsdp'}, dimensions={0}, use_global_device_ids=true | all-gather | bytes 1105920 | tf_op jit(solution)/shard_map/all_gather | solution.py:965
  53.1 4.1 copy.98
  61.4 71.9 %shard_map.194 = (bf16[256,1152]{1,0:T(8,128)(2,1)}, f32[12,64,384]{2,1,0:T(8,128)}, f32[12,1,384]{2,1,0:T(1,128)}, bf16[8,12,128,128]{3,2,1,0:T(8,128)(2,1)}, b...) custom-call(bf16[12,128,384]{2,1,0:T(8,128)(2,1)} %concatenate.27.cl, ...), custom_call_target="tpu_custom_call" | custom-call | tf_op jit(solution)/shard_map/pallas_call | solution.py:589
  133.3 63.0 %shard_map.195 = (bf16[256,1152]{1,0:T(8,128)(2,1)}, f32[256,1152]{1,0:T(8,128)}, bf16[256,1152]{1,0:T(8,128)(2,1)}, bf16[12,128,384]{2,1,0:T(8,128)(2,1)}, bf16...) custom-call(bf16[256,1152]{1,0:T(8,128)(2,1)} %bitcast.134, ...), custom_call_target="tpu_custom_call" | custom-call | tf_op jit(solution)/shard_map/pallas_call | solution.py:900
  199.6 10.7 %shard_map.196 = (f32[12,64,384]{2,1,0:T(8,128)}, bf16[8,12,128,128]{3,2,1,0:T(8,128)(2,1)}) custom-call(bf16[12,128,384]{2,1,0:T(8,128)(2,1)} %concatenate.27.clone.q_ref, bf16[12,128,384]{2,1,0:T(8,128)(2,1)} %get-tuple-element.40.g_ref, bf16[12,768,128]{2,1,0:T(8,128)(2,1)} %pad_maximum_fusion.1.qg_ref, ...), custom_call_target="tpu_custom_call" | custom-call | tf_op jit(solution)/shard_map/pallas_call | solution.py:935
  215.0 2.4 convolution_convert_fusion
  217.5 99.4 %reduce-scatter.5.cloned.1.call-done = bf16[1,12,128,128]{3,2,1,0:T(8,128)(2,1)} async-done(((bf16[8,12,128,128]{3,2,1,0:T(8,128)(2,1)}), bf16[1,12,128,128]{3,2,1,0:T(8,128)(2,1)}) %reduce-scatter.5.cloned.1.call-update) | async-done | bytes 393232 | tf_op jit(solution)/shard_map/reduce_scatter | solution.py:1028
  322.0 3.5 pad_maximum_fusion
  325.5 10.3 %copy.129 = bf16[1152,3072]{1,0:T(8,128)(2,1)} copy(bf16[1152,3072]{0,1:T(8,128)(2,1)} %pad_maximum_fusion) | data formatting | bytes 14155776
  336.5 2.8 copy.170
  343.8 1.9 copy.169
  345.7 40.5 %psum.7 = f32[2,1152]{1,0:T(2,128)S(1)} all-reduce(f32[2,1152]{1,0:T(2,128)S(1)} %pad_maximum_fusion.2), channel_id=1, replica_groups=mesh['fsdp'=4,'ctx'=8] {'fsdp','ctx'}, use_global_device_ids=true, to_apply=%region_5.0 | all-reduce | flops 2304 | bytes 18432 | tf_op jit(solution)/shard_map/psum | solution.py:1082
  386.9 12.6 %reduce-scatter.7.cloned.1.call-done = bf16[288,3072]{1,0:T(8,128)(2,1)} async-done(((bf16[1152,3072]{1,0:T(8,128)(2,1)}), bf16[288,3072]{1,0:T(8,128)(2,1)}) %reduce-scatter.7.cloned.1.call-update) | async-done | bytes 1769488
  399.6 2.9 copy.130
  402.4 2.4 copy.117
  404.8 183.6 %shard_map.197 = (bf16[448,16,128]{2,1,0:T(8,128)(2,1)}, bf16[448,16,128]{2,1,0:T(8,128)(2,1)}, bf16[48,16,1152]{2,1,0:T(8,128)(2,1)}, bf16[24,288,128]{2,1,0:T(8,128)(2,1)}) custom-call(bf16[4,112,16,128]{3,2,1,0:T(8,128)(2,1)} %get-tuple-element.46.gate_ref, bf16[4,112,16,128]{3,2,1,0:T(8,128)(2,1)} %get-tuple-element.47.up_ref, ...), custom_call_target="tpu_custom_call" | custom-call | tf_op jit(solution)/shard_map/pallas_call | solution.py:249
  590.2 2.8 convert_bitcast_fusion.2
  593.7 4.3 copy.122
  598.0 5.0 reshape.313
  605.2 4.3 copy.123
  609.5 5.0 reshape.314
  620.1 3.6 bitcast_convert_fusion
  (138 shorter events, 46.8 us)
Async XLA Ops:
  7.2 29.1 %copy-start.5 = (bf16[128,2,1152]{2,1,0:T(2,128)(2,1)S(1)}, bf16[128,2,1152]{2,1,0:T(2,128)(2,1)}, u32[]{:S(2)}) copy-start(bf16[128,2,1152]{2,1,0:T(2,128)(2,1)} %param.11) | copy-start | bytes 1769476
  7.2 45.9 %all-gather.2.cloned.1.call-start = ((), (), s32[]{:S(2)}) async-start(), calls=%async_computation.2 | async-start | bytes 3317760 | tf_op jit(solution)/shard_map/all_gather | solution.py:965
  7.9 308.9 %reduce-scatter.5.cloned.1.call-start = ((), (), s32[]{:S(2)}) async-start(), calls=%async_computation.3 | async-start | bytes 3538944 | tf_op jit(solution)/shard_map/reduce_scatter | solution.py:1028
  36.3 12.0 %copy-start.1 = (bf16[128,2,1152]{2,0,1:T(8,128)(2,1)}, bf16[128,2,1152]{2,0,1:T(8,128)(2,1)S(1)}, u32[]{:S(2)}) copy-start(bf16[128,2,1152]{2,0,1:T(8,128)(2,1)S(1)} %copy.97) | copy-start | bytes 1769476
  36.6 11.8 %copy-start.28 = (f32[256]{0:T(256)}, f32[256]{0:T(256)S(1)}, u32[]{:S(2)}) copy-start(f32[256]{0:T(256)S(1)} %get-tuple-element.111) | copy-start | bytes 3076
  37.4 1.5 copy-start.22
  37.4 1.7 copy-start.20
  38.3 10.9 %copy-start.24 = (f32[1152]{0:T(1024)S(1)}, f32[1152]{0:T(1024)}, u32[]{:S(2)}) copy-start(f32[1152]{0:T(1024)} %convert_element_type.145) | copy-start | bytes 13828
  49.3 2.4 copy-start.19
  49.8 2.7 copy-start.31
  210.3 189.2 %reduce-scatter.7.cloned.1.call-start = ((), (), s32[]{:S(2)}) async-start(), calls=%async_computation.4 | async-start | bytes 8847360
  213.6 1.4 copy-start.10
  320.2 1.8 copy-start
  335.8 3.5 copy-start.9
  335.8 3.5 copy-start.11
  339.2 1.3 copy-start.4
  339.3 1.4 copy-start.14
  340.6 1.4 copy-start.8
  340.6 1.4 copy-start.25
  340.6 1.4 copy-start.29
  342.1 1.3 copy-start.16
  343.8 1.9 copy-start.30
  590.2 2.8 copy-start.15
  620.1 3.6 copy-start.12
  (11 other events, 10.6 us)
Sparse Core Ops, SparseCore 0:
  9.6 33.1 all-gather.1
  210.4 106.3 reduce-scatter.4
  335.9 63.5 reduce-scatter.6

commit v5 on v4

--- a/solution.py
+++ b/solution.py
@@ -33,58 +33,8 @@
     return lax.rsqrt(jnp.mean(rows * rows, axis=-1, keepdims=True) + EPSILON)
 
 
-def norm_back(rows, scale, gain, upstream):
-    scaled = upstream * gain
-    inward = scale * scaled - rows * scale**3 * jnp.mean(scaled * rows, axis=-1, keepdims=True)
-    return (inward, jnp.sum(upstream * rows * scale, axis=0))
-
-
 def forward_dot(left, right):
     return jnp.dot(left, right, preferred_element_type=jnp.float32)
-
-
-def backward_dot(grad, weight):
-    return jnp.einsum("rn,cn->rc", grad, weight, preferred_element_type=jnp.float32)
-
-
-def attend_back_kernel(q_ref, g_ref, qg_ref, kv_ref, mix_ref, log_ref, grad_q_ref, grad_kv_ref):
-    me = lax.axis_index("ctx")
-    units, deep, wide = q_ref.shape
-    blocks, _, keys, _ = kv_ref.shape
-
-    def clear(block, unused):
-        grad_kv_ref[block] = jnp.zeros(grad_kv_ref.shape[1:], grad_kv_ref.dtype)
-        return unused
-
-    lax.fori_loop(me + 1, blocks, clear, 0)
-
-    def unit_step(unit, unused):
-        q, g, qg, log_total = q_ref[unit], g_ref[unit], qg_ref[unit], log_ref[unit]
-        delta = jnp.sum(g[HD:].astype(jnp.float32) * mix_ref[unit], axis=0, keepdims=True)
-
-        def back(block, grad_q, diagonal):
-            kv = kv_ref[block, unit]
-            scores = jnp.dot(kv, q, preferred_element_type=jnp.float32)
-            probs = jnp.exp(scores - log_total)
-            if diagonal:
-                key_at = lax.broadcasted_iota(jnp.int32, scores.shape, 0)
-                query_at = lax.rem(lax.broadcasted_iota(jnp.int32, scores.shape, 1), keys)
-                probs = jnp.where(key_at <= query_at, probs, 0.0)
-            grad_probs = jnp.dot(kv, g, preferred_element_type=jnp.float32)
-            grad_scores = (probs * (grad_probs - delta)).astype(jnp.bfloat16)
-            both = jnp.concatenate([grad_scores, probs.astype(jnp.bfloat16)], axis=1)
-            grad_kv_ref[block, unit] = jnp.dot(
-                both, qg, preferred_element_type=jnp.float32
-            ).astype(grad_kv_ref.dtype)
-            added = jnp.dot(kv.T, grad_scores, preferred_element_type=jnp.float32)
-            return grad_q + added[:HD]
-
-        grad_q = back(me, jnp.zeros((HD, wide), jnp.float32), True)
-        grad_q = lax.fori_loop(0, me, lambda block, held: back(block, held, False), grad_q)
-        grad_q_ref[unit] = grad_q * HD ** (-0.5)
-        return unused
-
-    lax.fori_loop(0, units, unit_step, 0)
 
 
 MESH = pl.DeviceIdType.MESH
@@ -103,187 +53,6 @@
     place = place + odd * (count - 1 - 2 * place)
     late = lax.div(place, count // 2)
     return (1 - late) * 2 * place + late * (2 * (count - 1 - place) + 1)
-
-
-def ring_neighbours(count):
-    ctx, fsdp = lax.axis_index("ctx"), lax.axis_index("fsdp")
-    place = ring_place(ctx, fsdp, count)
-    after = ring_ctx(lax.rem(place + 1, count), fsdp, count)
-    before = ring_ctx(lax.rem(place + count - 1, count), fsdp, count)
-    return place, (fsdp, after), (fsdp, before)
-
-
-class Ring:
-    def __init__(self, count, works, landings, totals, sends, arrivals):
-        self.count, self.works, self.landings, self.totals = count, works, landings, totals
-        self.sends, self.arrivals = sends, arrivals
-        self.place, self.after, self.before = ring_neighbours(count)
-        self.ticks = 2 * count - 2
-
-    def chunk(self, held, index):
-        per = held.shape[0] // self.count
-        return held.at[pl.ds(index * per, per)]
-
-    def copy(self, stream, step, index, summing):
-        source = self.chunk((self.works if summing else self.totals)[stream], index)
-        target = self.landings[stream].at[step] if summing else source
-        return pltpu.make_async_remote_copy(
-            src_ref=source,
-            dst_ref=target,
-            send_sem=self.sends.at[stream, step],
-            recv_sem=self.arrivals.at[stream, step],
-            device_id=self.after,
-            device_id_type=MESH,
-        )
-
-    def start(self, stream):
-        self.copy(stream, 0, self.place, True).start()
-
-    def tick(self, step):
-        index = lax.rem(self.place + 3 * self.count - 1 - step, self.count)
-        last = self.count - 2
-        for stream in range(len(self.works)):
-            self.copy(stream, step, index, False).wait_recv()
-
-            def add(target, stream=stream):
-                part = self.chunk(self.works[stream], index)
-                landed = self.landings[stream].at[jnp.minimum(step, last)]
-                for row in range(part.shape[0]):
-                    target[row] = (
-                        part[row].astype(jnp.float32) + landed[row].astype(jnp.float32)
-                    ).astype(part.dtype)
-
-            @pl.when(step < last)
-            def _():
-                add(self.chunk(self.works[stream], index))
-                self.copy(stream, jnp.minimum(step + 1, last), index, True).start()
-
-            @pl.when(step == last)
-            def _():
-                add(self.chunk(self.totals[stream], index))
-
-            @pl.when(jnp.logical_and(step >= last, step < self.ticks - 1))
-            def _():
-                self.copy(stream, jnp.minimum(step + 1, self.ticks - 1), index, False).start()
-
-    def finish(self):
-        def wait(step, unused):
-            for stream in range(len(self.works)):
-                self.copy(stream, step, self.place, False).wait_send()
-            return unused
-
-        lax.fori_loop(0, self.ticks, wait, 0)
-
-
-def reduce_kernel(
-    gate_ref, up_ref, down_ref, rest_ref, gate_total, up_total, down_total, rest_total,
-    gate_work, up_work, down_work, rest_work, gate_land, up_land, down_land, rest_land,
-    sends, arrivals, part_sends, part_arrivals, local_sems,
-):
-    fsdp, ctx = lax.axis_index("fsdp"), lax.axis_index("ctx")
-    group, count = lax.axis_size("fsdp"), lax.axis_size("ctx")
-    works = [gate_work, up_work, down_work, rest_work]
-    landings = [gate_land, up_land, down_land, rest_land]
-    totals = [gate_total, up_total, down_total, rest_total]
-    ring = Ring(count, works, landings, totals, sends, arrivals)
-    barrier = pltpu.get_barrier_semaphore()
-    for device in (ring.after, ring.before):
-        pl.semaphore_signal(barrier, inc=1, device_id=device, device_id_type=MESH)
-    for step in range(1, group):
-        peer = lax.rem(fsdp + step, group)
-        pl.semaphore_signal(barrier, inc=1, device_id=(peer, ctx), device_id_type=MESH)
-    pl.semaphore_wait(barrier, 1 + group)
-    per = gate_ref.shape[1]
-    copies = []
-    for which, (part, work) in enumerate(((gate_ref, gate_work), (up_ref, up_work))):
-        mine = work.at[pl.ds(fsdp * per, per)]
-        own = pltpu.make_async_copy(part.at[fsdp], mine, local_sems.at[which])
-        own.start()
-        copies.append(own)
-        for step in range(1, group):
-            peer = lax.rem(fsdp + step, group)
-            copy = pltpu.make_async_remote_copy(
-                src_ref=part.at[peer],
-                dst_ref=mine,
-                send_sem=part_sends.at[which, step - 1],
-                recv_sem=part_arrivals.at[which, step - 1],
-                device_id=(peer, ctx),
-                device_id_type=MESH,
-            )
-            copy.start()
-            copies.append(copy)
-        if work.shape[0] > per * group:
-            for row in range(per * group, work.shape[0]):
-                work[row] = jnp.zeros(work.shape[1:], work.dtype)
-    for which, (part, work) in enumerate(((down_ref, down_work), (rest_ref, rest_work))):
-        own = pltpu.make_async_copy(part, work.at[pl.ds(0, part.shape[0])], local_sems.at[2 + which])
-        own.start()
-        copies.append(own)
-        for row in range(part.shape[0], work.shape[0]):
-            work[row] = jnp.zeros(work.shape[1:], work.dtype)
-    for copy in copies:
-        copy.wait()
-    for stream in range(len(works)):
-        ring.start(stream)
-
-    def step(at, unused):
-        ring.tick(at)
-        return unused
-
-    lax.fori_loop(0, ring.ticks, step, 0)
-    ring.finish()
-
-
-def padded(blocks, count):
-    return -(-blocks // count) * count
-
-
-def reduce_gradients(gate_part, up_part, down_part, rest_part):
-    group, count = lax.axis_size("fsdp"), lax.axis_size("ctx")
-    shapes = [
-        (padded(group * gate_part.shape[1], count),) + gate_part.shape[2:],
-        (padded(group * up_part.shape[1], count),) + up_part.shape[2:],
-        (padded(down_part.shape[0], count),) + down_part.shape[1:],
-        (padded(rest_part.shape[0], count),) + rest_part.shape[1:],
-    ]
-    return pl.pallas_call(
-        reduce_kernel,
-        out_shape=[jax.ShapeDtypeStruct(shape, jnp.bfloat16) for shape in shapes],
-        in_specs=[pl.BlockSpec(memory_space=pl.ANY)] * 4,
-        out_specs=[pl.BlockSpec(memory_space=pltpu.VMEM)] * 4,
-        scratch_shapes=[pltpu.VMEM(shape, jnp.bfloat16) for shape in shapes]
-        + [
-            pltpu.VMEM((count - 1, shape[0] // count) + shape[1:], jnp.bfloat16) for shape in shapes
-        ]
-        + [
-            pltpu.SemaphoreType.DMA((4, 2 * count - 2)),
-            pltpu.SemaphoreType.DMA((4, 2 * count - 2)),
-            pltpu.SemaphoreType.DMA((2, group - 1)),
-            pltpu.SemaphoreType.DMA((2, group - 1)),
-            pltpu.SemaphoreType.DMA((4,)),
-        ],
-        compiler_params=pltpu.CompilerParams(
-            collective_id=0, has_side_effects=True, vmem_limit_bytes=56 << 20
-        ),
-    )(gate_part, up_part, down_part, rest_part)
-
-
-def lane_blocks(matrix):
-    rows, columns = matrix.shape
-    return jnp.swapaxes(matrix.reshape(rows, columns // LANES, LANES), 0, 1)
-
-
-def from_parts(parts, rows, columns):
-    group = lax.axis_size("fsdp")
-    wide = columns // group // LANES
-    split = parts.reshape(group, -1, 16, LANES)[:, : wide * (rows // 16)]
-    split = split.reshape(group, wide, rows // 16, 16, LANES)
-    return jnp.transpose(split, (2, 3, 0, 1, 4)).reshape(rows, columns).astype(jnp.float32)
-
-
-def from_blocks(blocks, first, count):
-    part = jnp.swapaxes(blocks[first : first + count], 0, 1)
-    return part.reshape(part.shape[0], count * LANES).astype(jnp.float32)
 
 
 class GroupGather:
@@ -397,7 +166,7 @@
 
 def attend_kernel(
     q_ref, kv_ref, out_ref, gate_ref, up_ref, g_ref,
-    low_ref, mix_ref, log_ref, all_ref, full_out_ref, my_gate_ref, my_up_ref, all_g_ref,
+    low_ref, low_t_ref, mix_ref, log_ref, all_ref, full_out_ref, my_gate_ref, my_up_ref, all_g_ref,
     top_ref, total_ref, chain_sends, chain_arrivals, peer_sends, peer_arrivals,
     out_sends, out_arrivals, g_sends, g_arrivals, part_sends, part_arrivals, local_sems,
 ):
@@ -549,10 +318,11 @@
             for head in (2 * pair, 2 * pair + 1):
                 unit, member = sequence * KVH + head // groups, head % groups
                 heads.append(mix_ref[unit, :, member * keys : (member + 1) * keys])
-            tile = jnp.concatenate(heads, axis=0).T
-            low_ref[
-                sequence * keys : (sequence + 1) * keys, pair * 2 * HD : (pair + 1) * 2 * HD
-            ] = tile.astype(low_ref.dtype)
+            tile = jnp.concatenate(heads, axis=0).astype(low_ref.dtype)
+            span = slice(sequence * keys, (sequence + 1) * keys)
+            columns = slice(pair * 2 * HD, (pair + 1) * 2 * HD)
+            low_t_ref[columns, span] = tile
+            low_ref[span, columns] = tile.T
     gathered.finish()
     gathered_g.finish()
     for copy in background:
@@ -590,6 +360,7 @@
         attend_kernel,
         out_shape=[
             jax.ShapeDtypeStruct((sequences * keys, width), jnp.bfloat16),
+            jax.ShapeDtypeStruct((width, sequences * keys), jnp.bfloat16),
             jax.ShapeDtypeStruct((units, HD, wide), jnp.float32),
             jax.ShapeDtypeStruct((units, 1, wide), jnp.float32),
             jax.ShapeDtypeStruct((count,) + pairs.shape, jnp.bfloat16),
@@ -599,7 +370,7 @@
             jax.ShapeDtypeStruct((group,) + g_rows.shape, jnp.bfloat16),
         ],
         in_specs=[VMEM, VMEM, ANY, ANY, ANY, ANY],
-        out_specs=[VMEM, VMEM, VMEM, VMEM, ANY, ANY, ANY, ANY],
+        out_specs=[VMEM] * 5 + [ANY] * 4,
         scratch_shapes=[
             pltpu.VMEM((units, 1, wide), jnp.float32),
             pltpu.VMEM((units, 1, wide), jnp.float32),
@@ -931,14 +702,607 @@
     )(x, low, full_out, my_gate, my_up, my_down, all_g, gain)
 
 
-def call(kernel, outs, *args):
+class Ring:
+    def __init__(self, work, landing, total, semaphores, forward, exchange=False):
+        self.fsdp, self.ctx = lax.axis_index("fsdp"), lax.axis_index("ctx")
+        self.group, self.count = lax.axis_size("fsdp"), lax.axis_size("ctx")
+        self.work, self.landing, self.total = work, landing, total
+        self.sends, self.arrivals = semaphores[:2]
+        self.part_sends, self.part_arrivals, self.own_sem = semaphores[2:] if exchange else (None,) * 3
+        self.exchange = exchange
+        side = 0 if forward else 1
+        self.place = ring_place(self.ctx, side, self.count)
+        self.after = (self.fsdp, ring_ctx(lax.rem(self.place + 1, self.count), side, self.count))
+        self.ticks = 2 * self.count - 2 + int(exchange)
+
+    def chunk(self, held, index):
+        if self.exchange:
+            return held.at[index]
+        per = held.shape[0] // self.count
+        return held.at[pl.ds(index * per, per)]
+
+    def summing(self, step, index):
+        return self.copy(self.chunk(self.work, index), self.landing.at[step], step)
+
+    def handing(self, step, index):
+        held = self.chunk(self.total, index)
+        return self.copy(held, held, step)
+
+    def copy(self, source, target, step):
+        return pltpu.make_async_remote_copy(
+            src_ref=source,
+            dst_ref=target,
+            send_sem=self.sends.at[step],
+            recv_sem=self.arrivals.at[step],
+            device_id=self.after,
+            device_id_type=MESH,
+        )
+
+    def part(self, index, step):
+        peer = lax.rem(self.fsdp + step, self.group)
+        return pltpu.make_async_remote_copy(
+            src_ref=self.work.at[index, peer],
+            dst_ref=self.total.at[index, self.fsdp],
+            send_sem=self.part_sends.at[step - 1],
+            recv_sem=self.part_arrivals.at[step - 1],
+            device_id=(peer, self.ctx),
+            device_id_type=MESH,
+        )
+
+    def own_part(self, index):
+        return pltpu.make_async_copy(
+            self.work.at[index, self.fsdp], self.total.at[index, self.fsdp], self.own_sem
+        )
+
+    def start(self):
+        self.summing(0, self.place).start()
+
+    def tick(self, at):
+        last = self.count - 2
+        gap = int(self.exchange)
+        step = at - gap * jnp.where(at > last, 1, 0) if self.exchange else at
+        index = lax.rem(self.place + 3 * self.count - 1 - step, self.count)
+
+        def add(target):
+            part, landed = self.chunk(self.work, index), self.landing.at[jnp.minimum(at, last)]
+            for row in range(part.shape[0]):
+                target[row] = (
+                    part[row].astype(jnp.float32) + landed[row].astype(jnp.float32)
+                ).astype(part.dtype)
+
+        @pl.when(at <= last)
+        def _():
+            self.summing(jnp.minimum(at, last), index).wait_recv()
+
+        @pl.when(at < last)
+        def _():
+            add(self.chunk(self.work, index))
+            self.summing(jnp.minimum(at + 1, last), index).start()
+
+        if self.exchange:
+
+            @pl.when(at == last)
+            def _():
+                add(self.chunk(self.work, index))
+                for peer in range(1, self.group):
+                    self.part(index, peer).start()
+                self.own_part(index).start()
+
+            @pl.when(at == last + 1)
+            def _():
+                done = lax.rem(self.place + 1, self.count)
+                self.own_part(done).wait()
+                for peer in range(1, self.group):
+                    self.part(done, peer).wait_recv()
+                self.handing(last + 1, done).start()
+
+        else:
+
+            @pl.when(at == last)
+            def _():
+                add(self.chunk(self.total, index))
+                self.handing(last + 1, index).start()
+
+        @pl.when(at > last + gap)
+        def _():
+            here = jnp.maximum(step, last + 1)
+            self.handing(here, index).wait_recv()
+
+            @pl.when(here < 2 * self.count - 3)
+            def _():
+                self.handing(jnp.minimum(here + 1, 2 * self.count - 3), index).start()
+
+    def finish(self):
+        def wait(step, unused):
+            self.handing(step, self.place).wait_send()
+            return unused
+
+        lax.fori_loop(0, 2 * self.count - 2, wait, 0)
+        if self.exchange:
+            for peer in range(1, self.group):
+                self.part(lax.rem(self.place + 1, self.count), peer).wait_send()
+
+
+def ring_scratch(chunk, exchange=False):
+    count = lax.axis_size("ctx")
+    work = (count,) + chunk if exchange else (count * chunk[0],) + chunk[1:]
+    return [pltpu.VMEM(work, jnp.bfloat16), pltpu.VMEM((count - 1,) + chunk, jnp.bfloat16)]
+
+
+def ring_total(chunk, exchange=False):
+    count = lax.axis_size("ctx")
+    work = (count,) + chunk if exchange else (count * chunk[0],) + chunk[1:]
+    return jax.ShapeDtypeStruct(work, jnp.bfloat16)
+
+
+def ring_semaphores(exchange=False):
+    dma, steps = pltpu.SemaphoreType.DMA, 2 * lax.axis_size("ctx") - 2
+    parts = lax.axis_size("fsdp") - 1
+    return [dma((steps,))] * 2 + ([dma((parts,))] * 2 + [dma] if exchange else [])
+
+
+def back_kernel(
+    q_ref, g_ref, pairs_ref, mix_ref, log_ref, gate_ref, up_ref, down_ref, gain_grad_ref,
+    branch_ref, low_t_ref, normed_t_ref, w_query_ref, w_key_ref, w_value_ref, x_ref, gain_ref,
+    resid_grad_ref, cos_ref, sin_ref,
+    tokens_ref, gate_total, up_total, down_a_total, down_b_total, rest_a_total, rest_b_total,
+    peer_got, chain_got,
+    kv_ref, stage_ref, final_ref, qg_ref, delta_ref, grad_q_ref,
+    gate_work, gate_land, up_work, up_land, down_a_work, down_a_land, down_b_work, down_b_land,
+    rest_a_work, rest_a_land, rest_b_work, rest_b_land,
+    low_all, normed_all, branch_all, query_all, pair_all, upstream_ref, gain_give, gain_got,
+    *semaphores,
+):
+    steps = Steps()
+    fsdp, ctx, group, count = steps.fsdp, steps.ctx, lax.axis_size("fsdp"), lax.axis_size("ctx")
+    units, deep, wide = q_ref.shape
+    keys = pairs_ref.shape[2]
+    rows, width = x_ref.shape
+    own = width // group
+    taken = iter(semaphores)
+
+    def take(number):
+        return [next(taken) for _ in range(number)]
+
+    gate_ring = Ring(gate_work, gate_land, gate_total, take(5), True, True)
+    up_ring = Ring(up_work, up_land, up_total, take(5), False, True)
+    down_a = Ring(down_a_work, down_a_land, down_a_total, take(2), True)
+    down_b = Ring(down_b_work, down_b_land, down_b_total, take(2), False)
+    rest_a = Ring(rest_a_work, rest_a_land, rest_a_total, take(2), True)
+    rest_b = Ring(rest_b_work, rest_b_land, rest_b_total, take(2), False)
+    first_rings = (gate_ring, up_ring, down_a, down_b)
+    peer_sends, peer_arrivals, chain_sends, chain_arrivals = take(4)
+    branch_gather = GroupGather(lambda shard: branch_all.at[shard], *take(2))
+    query_gather = GroupGather(lambda shard: query_all.at[shard], *take(2))
+    pair_gather = GroupGather(lambda shard: pair_all.at[shard], *take(2))
+    low_sends, low_arrivals, normed_sends, normed_arrivals, gain_sends, gain_arrivals = take(6)
+    local_sems, stage_sems = take(2)
+
+    barrier = pltpu.get_barrier_semaphore()
+    greeted = steps.greet(barrier) + greet_group(barrier) + 2
+    for device in (gate_ring.after, up_ring.after):
+        pl.semaphore_signal(barrier, inc=1, device_id=device, device_id_type=MESH)
+
+    loads = []
+
+    def load(source, target):
+        copy = pltpu.make_async_copy(source, target, local_sems.at[len(loads)])
+        copy.start()
+        loads.append(copy)
+
+    load(pairs_ref, kv_ref)
+    load(branch_ref, branch_all.at[fsdp])
+    load(low_t_ref.at[pl.ds(fsdp * own, own)], low_all.at[:, lane_tile(fsdp, rows)])
+    load(normed_t_ref.at[pl.ds(fsdp * own, own)], normed_all.at[:, lane_tile(fsdp, rows)])
+    for which in range(2):
+        target = (down_a_work, down_b_work)[which]
+        load(down_ref.at[which], target)
+    n = gate_work.shape[2]
+    chunk_loads = []
+    for which, (source, target) in enumerate(((gate_ref, gate_work), (up_ref, up_work))):
+        for chunk in range(count):
+            copy = pltpu.make_async_copy(
+                source.at[:, pl.ds(chunk * n, n)],
+                target.at[chunk],
+                local_sems.at[len(loads) + which * count + chunk],
+            )
+            copy.start()
+            chunk_loads.append(copy)
+
+    def prepare(unit):
+        q, g = q_ref[unit], g_ref[unit]
+        qg_ref[unit, :wide] = q.T
+        qg_ref[unit, wide:] = g.T
+        delta_ref[unit] = jnp.sum(
+            g[HD:].astype(jnp.float32) * mix_ref[unit], axis=0, keepdims=True
+        )
+        grad_q_ref[unit] = jnp.zeros((HD, wide), jnp.float32)
+
+    tiles(units, prepare)
+
+    for copy in loads + chunk_loads:
+        copy.wait()
+    pl.semaphore_wait(barrier, greeted)
+    for ring in first_rings:
+        ring.start()
+    branch_gather.start(branch_ref)
+
+    def slices(source, target, sends, arrivals, step):
+        peer = lax.rem(fsdp + step, group)
+        return pltpu.make_async_remote_copy(
+            src_ref=source.at[pl.ds(peer * own, own)],
+            dst_ref=target.at[:, lane_tile(fsdp, rows)],
+            send_sem=sends.at[step - 1],
+            recv_sem=arrivals.at[step - 1],
+            device_id=(peer, ctx),
+            device_id_type=MESH,
+        )
+
+    turned = [
+        slices(*ends, step)
+        for ends in (
+            (low_t_ref, low_all, low_sends, low_arrivals),
+            (normed_t_ref, normed_all, normed_sends, normed_arrivals),
+        )
+        for step in range(1, group)
+    ]
+    for copy in turned:
+        copy.start()
+
+    def tick(at):
+        for ring in first_rings:
+            if ring.exchange:
+                ring.tick(at)
+            else:
+
+                @pl.when(at < ring.ticks)
+                def _():
+                    ring.tick(jnp.minimum(at, ring.ticks - 1))
+
+    def back(unit, first, blocks, diagonal):
+        kv = kv_ref[pl.ds(first, blocks), unit].reshape(blocks * keys, deep)
+        scores = jnp.dot(kv, q_ref[unit], preferred_element_type=jnp.float32)
+        probs = jnp.exp(scores - log_ref[unit])
+        if diagonal:
+            probs = jnp.where(causal(keys, wide, scores.shape), probs, 0.0)
+        grad_probs = jnp.dot(kv, g_ref[unit], preferred_element_type=jnp.float32)
+        grad_scores = (probs * (grad_probs - delta_ref[unit])).astype(jnp.bfloat16)
+        both = jnp.concatenate([grad_scores, probs.astype(jnp.bfloat16)], axis=1)
+        grad_kv = jnp.dot(both, qg_ref[unit], preferred_element_type=jnp.float32)
+        added = jnp.dot(kv.T, grad_scores, preferred_element_type=jnp.float32)
+        grad_q_ref[unit] = grad_q_ref[unit] + added[:HD]
+        kv_ref[pl.ds(first, blocks), unit] = grad_kv.astype(kv_ref.dtype).reshape(
+            blocks, keys, deep
+        )
+
+    def over_units(body):
+        def two(at):
+            body(2 * at)
+            body(2 * at + 1)
+
+        tiles(units // 2, two)
+
+    def across(pair):
+        return pltpu.make_async_remote_copy(
+            src_ref=kv_ref.at[2 * pair + 1 - steps.side],
+            dst_ref=peer_got.at[pair],
+            send_sem=peer_sends.at[pair],
+            recv_sem=peer_arrivals.at[pair],
+            device_id=steps.peer,
+            device_id_type=MESH,
+        )
+
+    def down_chain(pair):
+        return pltpu.make_async_remote_copy(
+            src_ref=kv_ref.at[2 * pair + steps.side],
+            dst_ref=chain_got.at[pair],
+            send_sem=chain_sends.at[pair],
+            recv_sem=chain_arrivals.at[pair],
+            device_id=steps.below,
+            device_id_type=MESH,
+        )
+
+    def combine(time):
+        pair = time - steps.levels + steps.level
+
+        @pl.when(jnp.logical_and(pair >= 0, pair <= steps.level))
+        def _():
+            for slot, expected, arrival, source in (
+                (0, jnp.logical_or(pair < steps.level, steps.side == 0), across, peer_got),
+                (1, steps.has_above, down_chain, chain_got),
+            ):
+
+                @pl.when(expected)
+                def _():
+                    arrival(pair).wait_recv()
+                    copy = pltpu.make_async_copy(
+                        source.at[pair], stage_ref.at[slot], stage_sems.at[slot]
+                    )
+                    copy.start()
+                    copy.wait()
+
+                @pl.when(jnp.logical_not(expected))
+                def _():
+                    stage_ref[slot] = jnp.zeros(stage_ref.shape[1:], stage_ref.dtype)
+
+            def add(unit):
+                final_ref[unit] = (
+                    kv_ref[2 * pair + steps.side, unit].astype(jnp.float32)
+                    + stage_ref[0, unit].astype(jnp.float32)
+                    + stage_ref[1, unit].astype(jnp.float32)
+                )
+
+            tiles(units, add)
+
+            @pl.when(pair < steps.level)
+            def _():
+                kv_ref[2 * pair + steps.side] = final_ref[...].astype(kv_ref.dtype)
+                down_chain(pair).start()
+
+    def slot(pair):
+        @pl.when(pair < steps.level)
+        def _():
+            over_units(lambda unit: back(unit, 2 * pair, 2, False))
+            across(pair).start()
+
+        @pl.when(pair == steps.level)
+        def _():
+            over_units(lambda unit: back(unit, ctx, 1, True))
+
+            @pl.when(steps.side == 1)
+            def _():
+                over_units(lambda unit: back(unit, ctx - 1, 1, False))
+                across(steps.level).start()
+
+        tick(pair)
+        combine(pair)
+
+    tiles(steps.levels, slot)
+    done = steps.levels
+    cosine, sine = cos_ref[...], sin_ref[...]
+
+    def unturn(columns):
+        first, second = columns[: HD // 2], columns[HD // 2 :]
+        return jnp.concatenate(
+            [first * cosine + second * sine, second * cosine - first * sine], axis=0
+        )
+
+    sequences = units // KVH
+    groups = wide // keys
+    for sequence in range(sequences):
+        span = slice(sequence * keys, (sequence + 1) * keys)
+        for pair in range(H // 2):
+            heads = []
+            for head in (2 * pair, 2 * pair + 1):
+                unit, member = sequence * KVH + head // groups, head % groups
+                part = grad_q_ref[unit, :, member * keys : (member + 1) * keys]
+                heads.append(unturn(part * HD ** (-0.5)))
+            query_all[fsdp, span, pair * 2 * HD : (pair + 1) * 2 * HD] = (
+                jnp.concatenate(heads, axis=0).astype(jnp.bfloat16).T
+            )
+    query_gather.start(query_all.at[fsdp])
+    tick(done)
+    combine(steps.levels)
+    kv_width = KVH * HD
+    for sequence in range(sequences):
+        span = slice(sequence * keys, (sequence + 1) * keys)
+        for pair in range(KVH // 2):
+            turned_keys, turned_values = [], []
+            for unit in (sequence * KVH + 2 * pair, sequence * KVH + 2 * pair + 1):
+                part = final_ref[unit].T
+                turned_keys.append(unturn(part[:HD]))
+                turned_values.append(part[HD:])
+            for start, parts in ((0, turned_keys), (kv_width, turned_values)):
+                pair_all[fsdp, span, start + pair * 2 * HD : start + (pair + 1) * 2 * HD] = (
+                    jnp.concatenate(parts, axis=0).astype(jnp.bfloat16).T
+                )
+    pair_gather.start(pair_all.at[fsdp])
+    branch_gather.forward()
+    query_gather.forward()
+
+    step_out = width_tile(width)
+
+    def upstream_tile(at):
+        columns = pl.ds(pl.multiple_of(at * step_out, LANES), step_out)
+        upstream_ref[:, columns] = (
+            dot_columns(query_all[fsdp], w_query_ref[columns, :])
+            + dot_columns(pair_all[fsdp, :, :kv_width], w_key_ref[columns, :])
+            + dot_columns(pair_all[fsdp, :, kv_width:], w_value_ref[columns, :])
+        )
+
+    tiles(width // step_out, upstream_tile)
+    inputs = x_ref[...].astype(jnp.float32)
+    scale = norm_scale(inputs)
+    upstream = upstream_ref[...]
+    scaled = upstream * gain_ref[...]
+    tokens_ref[...] = (
+        resid_grad_ref[...]
+        + scale * scaled
+        - inputs * scale**3 * jnp.mean(scaled * inputs, axis=-1, keepdims=True)
+    )
+    gain_attn = jnp.sum(upstream * inputs * scale, axis=0, keepdims=True)
+    lanes = width // LANES
+    gain_give[...] = jnp.zeros(gain_give.shape, jnp.float32)
+    for block in range(lanes):
+        columns = slice(block * LANES, (block + 1) * LANES)
+        gain_give[block : block + 1, :] = gain_attn[:, columns]
+        gain_give[lanes + block : lanes + block + 1, :] = gain_grad_ref[:, columns]
+
+    def gain_copy(step):
+        peer = lax.rem(fsdp + step, group)
+        return pltpu.make_async_remote_copy(
+            src_ref=gain_give,
+            dst_ref=gain_got.at[step - 1],
+            send_sem=gain_sends.at[step - 1],
+            recv_sem=gain_arrivals.at[step - 1],
+            device_id=(peer, ctx),
+            device_id_type=MESH,
+        )
+
+    for step in range(1, group):
+        gain_copy(step).start()
+    tick(done + 1)
+    for copy in turned:
+        copy.wait_recv()
+    for gather in (branch_gather, query_gather):
+        gather.sibling_here()
+        for step in range(1, gather.chips):
+            gather.crossed(step)
+    row_blocks = own // 16
+
+    def weight_grad(left, right, columns, target, first):
+        span = 384 if columns % 384 == 0 else LANES
+
+        def body(at):
+            part = forward_dot(
+                left[...], right[:, :, lane_tile(at, span)].reshape(group * rows, span)
+            ).astype(jnp.bfloat16)
+            for block in range(span // LANES):
+                begin = first + (at * (span // LANES) + block) * row_blocks
+                target[pl.ds(begin, row_blocks)] = part[
+                    :, block * LANES : (block + 1) * LANES
+                ].reshape(row_blocks, 16, LANES)
+
+        tiles(columns // span, body)
+
+    weight_grad(low_all, branch_all, width, rest_b_work, 0)
+    weight_grad(normed_all, query_all, width, rest_a_work, 0)
+    tick(done + 2)
+    pair_gather.forward()
+    pair_gather.sibling_here()
+    for step in range(1, pair_gather.chips):
+        pair_gather.crossed(step)
+    blocks = width // LANES * row_blocks
+    key_blocks = kv_width // LANES * row_blocks
+    weight_grad(normed_all, pair_all.at[:, :, :kv_width], kv_width, rest_a_work, blocks)
+    weight_grad(normed_all, pair_all.at[:, :, kv_width:], kv_width, rest_b_work, blocks)
+    gains = gain_give[...]
+    for step in range(1, group):
+        gain_copy(step).wait_recv()
+        gains = gains + gain_got[step - 1]
+    filled = blocks + key_blocks
+    gain_tiles = gains.shape[0] // 16
+    rest_a_work[filled : filled + gain_tiles] = gains.astype(jnp.bfloat16).reshape(
+        gain_tiles, 16, LANES
+    )
+    for spare in range(filled + gain_tiles, rest_a_work.shape[0]):
+        rest_a_work[spare] = jnp.zeros((16, LANES), jnp.bfloat16)
+    for spare in range(filled, rest_b_work.shape[0]):
+        rest_b_work[spare] = jnp.zeros((16, LANES), jnp.bfloat16)
+    rest_a.start()
+    rest_b.start()
+    begun = done + 3
+    left = gate_ring.ticks - begun
+
+    def last_ticks(at, unused):
+        @pl.when(at < left)
+        def _():
+            tick(jnp.minimum(begun + at, gate_ring.ticks - 1))
+
+        for ring in (rest_a, rest_b):
+            ring.tick(at)
+        return unused
+
+    lax.fori_loop(0, rest_a.ticks, last_ticks, 0)
+
+    def more_ticks(at, unused):
+        tick(begun + at)
+        return unused
+
+    lax.fori_loop(rest_a.ticks, max(left, rest_a.ticks), more_ticks, 0)
+    for ring in first_rings + (rest_a, rest_b):
+        ring.finish()
+    for copy in turned:
+        copy.wait_send()
+    for gather in (branch_gather, query_gather, pair_gather):
+        gather.sent()
+    for step in range(1, group):
+        gain_copy(step).wait_send()
+
+    def sent(pair):
+        @pl.when(jnp.logical_or(pair < steps.level, steps.side == 1))
+        def _():
+            across(pair).wait_send()
+
+        @pl.when(pair < steps.level)
+        def _():
+            down_chain(pair).wait_send()
+
+    tiles(steps.level + 1, sent)
+
+
+def layer_back(
+    q_wide, g_wide, all_pairs, mix, log_total, gate_part, up_part, down_part, gain_grad, branch,
+    low_t, normed_t, w_query, w_key, w_value, x, gain, resid_grad, cosine, sine,
+):
+    group, count = lax.axis_size("fsdp"), lax.axis_size("ctx")
+    units, deep, wide = q_wide.shape
+    keys = all_pairs.shape[2]
+    rows, width = x.shape
+    own, kv_width = width // group, w_key.shape[1]
+    bf16, f32 = jnp.bfloat16, jnp.float32
+    dma = pltpu.SemaphoreType.DMA
+    wide_chunk = (group, gate_part.shape[1] // count, 16, LANES)
+    down_chunk = (down_part.shape[1] // count,) + down_part.shape[2:]
+    gain_rows = spread(2 * (width // LANES), 16)
+    tiles_held = (width + kv_width) // LANES * (own // 16)
+    a_chunk = (spread(tiles_held + gain_rows // 16, count) // count, 16, LANES)
+    b_chunk = (spread(tiles_held, count) // count, 16, LANES)
+    levels = count // 2
     return pl.pallas_call(
-        kernel,
-        out_shape=outs,
-        in_specs=[pl.BlockSpec(memory_space=pltpu.VMEM)] * len(args),
-        out_specs=[pl.BlockSpec(memory_space=pltpu.VMEM)] * len(outs),
-        compiler_params=pltpu.CompilerParams(vmem_limit_bytes=56 << 20),
-    )(*args)
+        back_kernel,
+        out_shape=[
+            jax.ShapeDtypeStruct((rows, width), f32),
+            ring_total(wide_chunk, True),
+            ring_total(wide_chunk, True),
+            ring_total(down_chunk),
+            ring_total(down_chunk),
+            ring_total(a_chunk),
+            ring_total(b_chunk),
+            *[jax.ShapeDtypeStruct((levels, units, keys, deep), bf16)] * 2,
+        ],
+        in_specs=[VMEM, VMEM, ANY, VMEM, VMEM, ANY, ANY, ANY, VMEM, ANY, ANY, ANY] + [VMEM] * 8,
+        out_specs=[VMEM] * 7 + [ANY] * 2,
+        scratch_shapes=[
+            pltpu.VMEM(all_pairs.shape, bf16),
+            pltpu.VMEM((2, units, keys, deep), bf16),
+            pltpu.VMEM((units, keys, deep), f32),
+            pltpu.VMEM((units, 2 * wide, deep), bf16),
+            pltpu.VMEM((units, 1, wide), f32),
+            pltpu.VMEM((units, HD, wide), f32),
+            *ring_scratch(wide_chunk, True),
+            *ring_scratch(wide_chunk, True),
+            *ring_scratch(down_chunk),
+            *ring_scratch(down_chunk),
+            *ring_scratch(a_chunk),
+            *ring_scratch(b_chunk),
+            pltpu.VMEM((own, group * rows), bf16),
+            pltpu.VMEM((own, group * rows), bf16),
+            pltpu.VMEM((group, rows, width), bf16),
+            pltpu.VMEM((group, rows, width), bf16),
+            pltpu.VMEM((group, rows, 2 * kv_width), bf16),
+            pltpu.VMEM((rows, width), f32),
+            pltpu.VMEM((gain_rows, LANES), f32),
+            pltpu.VMEM((group - 1, gain_rows, LANES), f32),
+            *ring_semaphores(True),
+            *ring_semaphores(True),
+            *ring_semaphores(),
+            *ring_semaphores(),
+            *ring_semaphores(),
+            *ring_semaphores(),
+            *[dma((levels,))] * 4,
+            *[group_semaphores()] * 6,
+            *[dma((group - 1,))] * 6,
+            dma((6 + 2 * count,)),
+            dma((2,)),
+        ],
+        compiler_params=pltpu.CompilerParams(
+            collective_id=3, has_side_effects=True, vmem_limit_bytes=62 << 20
+        ),
+    )(
+        q_wide, g_wide, all_pairs, mix, log_total, gate_part, up_part, down_part, gain_grad, branch,
+        low_t, normed_t, w_query, w_key, w_value, x, gain, resid_grad, cosine, sine,
+    )
 
 
 def unit_columns(rows, seq_count, block_len):
@@ -949,10 +1313,18 @@
     )
 
 
-def unit_rows(columns, seq_count, block_len):
-    groups = H // KVH
-    split = columns.reshape(seq_count, KVH, HD, groups, block_len)
-    return jnp.transpose(split, (0, 4, 1, 3, 2)).reshape(seq_count * block_len, H * HD)
+def from_tiles(held, rows):
+    blocks = held.shape[0] * 16 // rows
+    split = held.reshape(blocks, rows, LANES)
+    return jnp.swapaxes(split, 0, 1).reshape(rows, blocks * LANES).astype(jnp.float32)
+
+
+def from_parts(total, rows, columns):
+    count, group, n = total.shape[:3]
+    wide = columns // group // LANES
+    split = jnp.swapaxes(total, 0, 1).reshape(group, count * n, 16, LANES)
+    split = split[:, : wide * (rows // 16)].reshape(group, wide, rows, LANES)
+    return jnp.transpose(split, (2, 0, 1, 3)).reshape(rows, columns).astype(jnp.float32)
 
 
 def on_device(
@@ -994,7 +1366,7 @@
     ).reshape(units, block_len, 2 * HD)
     q_unit = unit_columns(queries * jnp.bfloat16(HD ** (-0.5)), seq_count, block_len)
     q_wide = jnp.concatenate([q_unit, jnp.zeros_like(q_unit)], axis=1)
-    attn_low, mix_unit, log_total, all_pairs, full_out, my_gate, my_up, all_g = attend(
+    (attn_low, low_t, mix_unit, log_total, all_pairs, full_out, my_gate, my_up, all_g) = attend(
         q_wide, pairs, w_out, w_gate, w_up, g_rows
     )
     layer_out, grad_resid, grad_branch, g_wide, gate_part, up_part, down_part, gain_term_ffn = (
@@ -1011,92 +1383,51 @@
             wide,
         )
     )
-    qg = jnp.concatenate([jnp.swapaxes(q_wide, 1, 2), jnp.swapaxes(g_wide, 1, 2)], axis=1)
-    grad_q_unit, grad_pairs = call(
-        attend_back_kernel,
-        [
-            jax.ShapeDtypeStruct((units, HD, wide), jnp.float32),
-            jax.ShapeDtypeStruct(all_pairs.shape, jnp.bfloat16),
-        ],
+    count = lax.axis_size("ctx")
+    down_blocks = down_part.reshape(-1, 16, width)
+    spare = spread(down_blocks.shape[0], 2 * count) - down_blocks.shape[0]
+    down_blocks = jnp.pad(down_blocks, ((0, spare), (0, 0), (0, 0)))
+    freqs = ROTARY_BASE ** (-2.0 * jnp.arange(HD // 2, dtype=jnp.float32) / HD)
+    angles = freqs[:, None] * positions.astype(jnp.float32)[None, :]
+    grad_tokens, gate_total, up_total, down_a, down_b, rest_a, rest_b, _, _ = layer_back(
         q_wide,
         g_wide,
-        qg,
         all_pairs,
         mix_unit,
         log_total,
-    )
-    summed_pairs = lax.psum_scatter(grad_pairs, "ctx", scatter_dimension=0, tiled=True)
-    summed_pairs = jnp.transpose(
-        summed_pairs.reshape(seq_count, KVH, block_len, 2 * HD), (0, 2, 1, 3)
-    )
-    grad_query_low = (
-        rotary(
-            unit_rows(grad_q_unit, seq_count, block_len).reshape(seq_count, block_len, H, HD),
-            positions,
-            -1.0,
-        )
-        .astype(jnp.bfloat16)
-        .reshape(rows_count, width)
-    )
-    grad_key_low = (
-        rotary(summed_pairs[..., :HD].astype(jnp.float32), positions, -1.0)
-        .astype(jnp.bfloat16)
-        .reshape(rows_count, kv_width)
-    )
-    grad_value_low = summed_pairs[..., HD:].reshape(rows_count, kv_width)
-    grad_normed_attn = (
-        backward_dot(grad_query_low, full_query)
-        + backward_dot(grad_key_low, full_key)
-        + backward_dot(grad_value_low, full_value)
-    )
-    inward_attn, gain_term_attn = norm_back(
-        inputs, scale_attn, full_gain_attn.astype(jnp.float32), grad_normed_attn
-    )
-    layer_out = layer_out.reshape(seq_count, block_len, width)
-    grad_tokens = (grad_resid + inward_attn).reshape(seq_count, block_len, width)
-
-    def part(acts, grads):
-        return jnp.einsum("rc,rn->cn", acts, grads, preferred_element_type=jnp.float32)
-
-    group = lax.axis_size("fsdp")
-    rest_part = lax.psum_scatter(
-        jnp.concatenate(
-            [
-                part(normed_attn, grad_query_low),
-                part(normed_attn, grad_key_low),
-                part(normed_attn, grad_value_low),
-                part(attn_low, grad_branch),
-            ],
-            axis=1,
-        ).astype(jnp.bfloat16),
-        "fsdp",
-        scatter_dimension=0,
-        tiled=True,
-    )
-    gate_sum, up_sum, down_sum, rest_sum = reduce_gradients(
         gate_part,
         up_part,
-        down_part.reshape(-1, 16, width),
-        lane_blocks(rest_part),
+        down_blocks.reshape(2, -1, 16, width),
+        gain_term_ffn,
+        grad_branch,
+        low_t,
+        normed_attn.T,
+        full_query,
+        full_key,
+        full_value,
+        x_rows,
+        full_gain_attn.astype(jnp.float32)[None],
+        grad_resid,
+        jnp.cos(angles),
+        jnp.sin(angles),
     )
-    gains = lax.psum(jnp.stack([gain_term_attn, gain_term_ffn[0]]), ("fsdp", "ctx"))
     own = gain_attn.shape[0]
+    down_rows = jnp.concatenate([down_a, down_b]).reshape(-1, width)[: w_down.shape[0]]
+    blocks = width // LANES * (own // 16)
+    filled = blocks + kv_width // LANES * (own // 16)
+    gains = rest_a[filled:].reshape(-1, LANES)[: 2 * (width // LANES)].reshape(2, width)
     gains = lax.dynamic_slice_in_dim(gains, lax.axis_index("fsdp") * own, own, 1)
-    edges = [0, width, width + kv_width, width + 2 * kv_width, 2 * width + 2 * kv_width]
-    grad_query, grad_key, grad_value, grad_out = [
-        from_blocks(rest_sum, first // LANES, (last - first) // LANES)
-        for first, last in zip(edges[:-1], edges[1:])
-    ]
+    gains = gains.astype(jnp.float32)
     return (
-        jnp.swapaxes(layer_out, 0, 1),
-        jnp.swapaxes(grad_tokens, 0, 1),
-        grad_query,
-        grad_key,
-        grad_value,
-        grad_out,
-        from_parts(gate_sum, gain_attn.shape[0], FF),
-        from_parts(up_sum, gain_attn.shape[0], FF),
-        down_sum.reshape(-1, width)[: w_down.shape[0]].astype(jnp.float32),
+        jnp.swapaxes(layer_out.reshape(seq_count, block_len, width), 0, 1),
+        jnp.swapaxes(grad_tokens.reshape(seq_count, block_len, width), 0, 1),
+        from_tiles(rest_a[:blocks], own),
+        from_tiles(rest_a[blocks:filled], own),
+        from_tiles(rest_b[blocks:filled], own),
+        from_tiles(rest_b[:blocks], own),
+        from_parts(gate_total, own, FF),
+        from_parts(up_total, own, FF),
+        down_rows.astype(jnp.float32),
         gains[0],
         gains[1],
     )

time: 639 us -> 454 us (0.71)
  waiting for transfers between devices: 113 us -> 0.68 us
  blocking collectives: 72.9 us -> 31.7 us
  local copies, waits for them, and re-layouts: 73.1 us -> 55.4 us
  other arithmetic: 19.2 us -> 5.69 us
  matrix products: 8.6 us -> 2.18 us
    reduce_scatter x1 -> x0, waiting for transfers between devices: 99.4 us -> none  [on_device(): lax.psum_scatter(grad_pairs, 'ctx', scatter_dimension=0, tiled=True)]
    psum x1 -> x0, blocking collectives: 40.5 us -> none  [on_device(): lax.psum(jnp.stack([gain_term_attn, gain_term_ffn[0]]), ('fsdp', 'ctx'))]
    unnamed x75 -> x42, local copies, waits for them, and re-layouts: 26 us -> 8.27 us
    unnamed x4 -> x1, waiting for transfers between devices: 13.3 us -> 0.68 us
    dot_general x7 -> x0, matrix products: 6.64 us -> none  [the longest x4 4.27 us: part(): jnp.einsum('rc,rn->cn', acts, grads, preferred_element_type=jnp.float32)]
    pallas_call x2 -> x1, Pallas kernels: 194 us -> 200 us  [layer_back(): pl.pallas_call(back_kernel, out_shape=[jax.ShapeDtypeStruct((rows, width)...]
  transfers between devices with their start and end apart: 3 -> 1, of which waited for: 2 -> 0; matrix products, arithmetic and copies ran while one was open for 4% -> 3% of each run, Pallas kernels for 0% -> 0%
where the time goes in v5:
time: 454 us; the launch traced here: 446 us
  Pallas kernels  335 us (74%)
  local copies, waits for them, and re-layouts  55.4 us (12%)
  blocking collectives  31.7 us (7%)
  between operations  15.4 us (3%)
  other arithmetic  5.69 us (1%)
    pallas_call x1, Pallas kernels, layer_back(): pl.pallas_call(back_kernel, out_shape=[jax.ShapeDtypeStruct((rows, width)...  200 us
    pallas_call x1, Pallas kernels, attend(): pl.pallas_call(attend_kernel, out_shape=[jax.ShapeDtypeStruct((sequences...  72.3 us
    pallas_call x1, Pallas kernels, feed_forward(): pl.pallas_call(ffn_kernel, out_shape=[jax.ShapeDtypeStruct((rows, width),...  63 us
    all_gather x2, blocking collectives, on_device(): lax.all_gather(weight, 'fsdp', axis=0, tiled=True)  23.2 us
    convert_element_type x4, local copies, waits for them, and re-layouts, from_parts(): jnp.transpose(split, (2, 0, 1, 3)).reshape(rows, columns)  19 us
  transfers between devices with their start and end apart: 1, of which 0 were waited for; matrix products, arithmetic and copies ran while one was open for 3% of the time, Pallas kernels for 0%

profile of v5, /device:TPU:0, one launch (start us, length us, event | category | flops | bytes accessed | tf_op | source)
XLA Modules:
  0.0 446.5 jit_solution(17539574009073576898)
XLA Ops:
  7.9 1.2 dynamic-slice
  11.6 8.5 %all-reduce.3 = (bf16[1152]{0:T(1024)(128)(2,1)S(1)}, bf16[1152]{0:T(1024)(128)(2,1)S(1)}) all-reduce(bf16[1152]{0:T(1024)(128)(2,1)S(1)} %dynamic-update-slice.1, bf16[1152]{0:T(1024)(128)(2,1)S(1)} %dynamic-update-slice), channel_id=1, replica_groups=mesh['fsdp'=4,'ctx'=8] {'fsdp'}, use_global_device_ids=true, to_apply=%add.2 | all-reduce | flops 2304 | bytes 9216
  20.7 1.1 copy.89
  22.1 13.9 %all_gather.18.w_value_ref = bf16[1152,384]{1,0:T(8,128)(2,1)S(1)} all-gather(bf16[288,384]{1,0:T(8,128)(2,1)S(1)} %copy-done.15), channel_id=1, replica_groups=mesh['fsdp'=4,'ctx'=8] {'fsdp'}, dimensions={0}, use_global_device_ids=true | all-gather | bytes 1105920 | tf_op jit(solution)/shard_map/all_gather | solution.py:1337
  37.7 9.3 %all_gather.17.w_key_ref = bf16[1152,384]{1,0:T(8,128)(2,1)S(1)} all-gather(bf16[288,384]{1,0:T(8,128)(2,1)S(1)} %copy-done.16), channel_id=1, replica_groups=mesh['fsdp'=4,'ctx'=8] {'fsdp'}, dimensions={0}, use_global_device_ids=true | all-gather | bytes 1105920 | tf_op jit(solution)/shard_map/all_gather | solution.py:1337
  54.0 4.2 copy.92
  60.7 1.2 concatenate.17.q_ref
  61.8 72.3 %shard_map.194 = (bf16[256,1152]{1,0:T(8,128)(2,1)}, bf16[1152,256]{1,0:T(8,128)(2,1)}, f32[12,64,384]{2,1,0:T(8,128)}, f32[12,1,384]{2,1,0:T(1,128)}, bf16[8,12...) custom-call(bf16[12,128,384]{2,1,0:T(8,128)(2,1)} %concatenate.17.q_, ...), custom_call_target="tpu_custom_call" | custom-call | tf_op jit(solution)/shard_map/pallas_call | solution.py:359
  134.1 63.0 %shard_map.195 = (bf16[256,1152]{1,0:T(8,128)(2,1)}, f32[256,1152]{1,0:T(8,128)}, bf16[256,1152]{1,0:T(8,128)(2,1)}, bf16[12,128,384]{2,1,0:T(8,128)(2,1)}, bf16...) custom-call(bf16[256,1152]{1,0:T(8,128)(2,1)} %bitcast.102, ...), custom_call_target="tpu_custom_call" | custom-call | tf_op jit(solution)/shard_map/pallas_call | solution.py:671
  197.1 200.1 %shard_map.196 = (f32[256,1152]{1,0:T(8,128)}, bf16[8,4,14,16,128]{4,3,2,1,0:T(8,128)(2,1)}, bf16[8,4,14,16,128]{4,3,2,1,0:T(8,128)(2,1)}, bf16[24,16,1152]{2,1,...) custom-call(bf16[12,128,384]{2,1,0:T(8,128)(2,1)} %concatenate.17.q_, ...), custom_call_target="tpu_custom_call" | custom-call | tf_op jit(solution)/shard_map/pallas_call | solution.py:1252
  397.2 1.3 slice.46
  400.5 1.4 slice.52
  401.9 1.4 copy.133
  403.3 1.9 copy.131
  405.9 1.6 copy.111
  407.5 1.1 copy.105
  408.6 1.2 copy.104
  410.4 1.6 copy.112
  412.0 1.8 copy.107
  414.6 4.3 copy.108
  418.8 5.3 %reshape.239 = f32[288,3072]{1,0:T(8,128)} reshape(f32[288,4,6,128]{3,2,1,0:T(8,128)} %copy.108) | data formatting | bytes 7077888 | tf_op jit(solution)/shard_map/convert_element_type | solution.py:1327
  425.2 4.3 copy.110
  429.5 5.1 %reshape.240 = f32[288,3072]{1,0:T(8,128)} reshape(f32[288,4,6,128]{3,2,1,0:T(8,128)} %copy.110) | data formatting | bytes 7077888 | tf_op jit(solution)/shard_map/convert_element_type | solution.py:1327
  434.8 2.2 bitcast_convert_fusion
  (88 shorter events, 21.9 us)
Async XLA Ops:
  7.2 14.7 %copy-start.4 = (bf16[128,2,1152]{2,1,0:T(2,128)(2,1)S(1)}, bf16[128,2,1152]{2,1,0:T(2,128)(2,1)}, u32[]{:S(2)}) copy-start(bf16[128,2,1152]{2,1,0:T(2,128)(2,1)} %param.11) | copy-start | bytes 1769476
  7.2 14.9 %copy-start.15 = (bf16[288,384]{1,0:T(8,128)(2,1)S(1)}, bf16[288,384]{1,0:T(8,128)(2,1)}, u32[]{:S(2)}) copy-start(bf16[288,384]{1,0:T(8,128)(2,1)} %param.14) | copy-start | bytes 663556
  7.2 46.8 %all-gather.2.cloned.1.call-start = ((), (), s32[]{:S(2)}) async-start(), calls=%async_computation | async-start | bytes 3317760 | tf_op jit(solution)/shard_map/all_gather | solution.py:1337
  21.9 30.1 %copy-start = (bf16[128,2,1152]{2,0,1:T(8,128)(2,1)}, bf16[128,2,1152]{2,0,1:T(8,128)(2,1)S(1)}, u32[]{:S(2)}) copy-start(bf16[128,2,1152]{2,0,1:T(8,128)(2,1)S(1)} %copy.89) | copy-start | bytes 1769476
  36.0 0.9 copy-start.2
  36.0 1.7 copy-start.16
  47.0 1.6 copy-start.1
  48.6 1.9 copy-start.13
  54.0 4.2 copy-start.5
  397.2 2.3 copy-start.12
  397.2 4.7 %copy-start.14 = (bf16[256,1152]{1,0:T(8,128)(2,1)S(1)}, bf16[256,1152]{1,0:T(8,128)(2,1)}, u32[]{:S(2)}) copy-start(bf16[256,1152]{1,0:T(8,128)(2,1)} %get-tuple-element.40) | copy-start | bytes 1769476
  399.5 3.8 copy-start.9
  407.4 2.4 copy-start.3
  418.8 5.4 %copy-start.8 = (bf16[8,4,14,16,128]{4,3,2,1,0:T(8,128)(2,1)S(1)}, bf16[8,4,14,16,128]{4,3,2,1,0:T(8,128)(2,1)}, u32[]{:S(2)}) copy-start(bf16[8,4,14,16,128]{4,3,2,1,0:T(8,128)(2,1)} %get-tuple-element.56) | copy-start | bytes 5505028
  429.5 5.1 %copy-start.10 = (bf16[24,16,1152]{2,1,0:T(8,128)(2,1)S(1)}, bf16[24,16,1152]{2,1,0:T(8,128)(2,1)}, u32[]{:S(2)}) copy-start(bf16[24,16,1152]{2,1,0:T(8,128)(2,1)} %get-tuple-element.57) | copy-start | bytes 2654212
  429.5 5.1 %copy-start.11 = (bf16[24,16,1152]{2,1,0:T(8,128)(2,1)S(1)}, bf16[24,16,1152]{2,1,0:T(8,128)(2,1)}, u32[]{:S(2)}) copy-start(bf16[24,16,1152]{2,1,0:T(8,128)(2,1)} %get-tuple-element.58) | copy-start | bytes 2654212
  434.8 3.6 copy-start.6
  434.8 3.6 copy-start.7
Sparse Core Ops, SparseCore 0:
  9.6 33.1 all-gather.1

commit v6 on v5

--- a/solution.py
+++ b/solution.py
@@ -845,11 +845,11 @@
     q_ref, g_ref, pairs_ref, mix_ref, log_ref, gate_ref, up_ref, down_ref, gain_grad_ref,
     branch_ref, low_t_ref, normed_t_ref, w_query_ref, w_key_ref, w_value_ref, x_ref, gain_ref,
     resid_grad_ref, cos_ref, sin_ref,
-    tokens_ref, gate_total, up_total, down_a_total, down_b_total, rest_a_total, rest_b_total,
-    peer_got, chain_got,
+    tokens_ref, gate_total, up_total, down_a_total, down_b_total, out_total, rest_a_total,
+    rest_b_total, peer_got, chain_got,
     kv_ref, stage_ref, final_ref, qg_ref, delta_ref, grad_q_ref,
     gate_work, gate_land, up_work, up_land, down_a_work, down_a_land, down_b_work, down_b_land,
-    rest_a_work, rest_a_land, rest_b_work, rest_b_land,
+    out_work, out_land, rest_a_work, rest_a_land, rest_b_work, rest_b_land,
     low_all, normed_all, branch_all, query_all, pair_all, upstream_ref, gain_give, gain_got,
     *semaphores,
 ):
@@ -868,6 +868,7 @@
     up_ring = Ring(up_work, up_land, up_total, take(5), False, True)
     down_a = Ring(down_a_work, down_a_land, down_a_total, take(2), True)
     down_b = Ring(down_b_work, down_b_land, down_b_total, take(2), False)
+    out_ring = Ring(out_work, out_land, out_total, take(2), True)
     rest_a = Ring(rest_a_work, rest_a_land, rest_a_total, take(2), True)
     rest_b = Ring(rest_b_work, rest_b_land, rest_b_total, take(2), False)
     first_rings = (gate_ring, up_ring, down_a, down_b)
@@ -890,37 +891,19 @@
         copy.start()
         loads.append(copy)
 
+    n = gate_work.shape[2]
+    for source, target in ((gate_ref, gate_work), (up_ref, up_work)):
+        for chunk in range(count):
+            load(source.at[:, pl.ds(chunk * n, n)], target.at[chunk])
+    first = down_a_work.shape[0]
+    load(down_ref.at[pl.ds(0, first)], down_a_work)
+    load(down_ref.at[pl.ds(first, down_b_work.shape[0])], down_b_work)
+    ring_loads = len(loads)
     load(pairs_ref, kv_ref)
     load(branch_ref, branch_all.at[fsdp])
     load(low_t_ref.at[pl.ds(fsdp * own, own)], low_all.at[:, lane_tile(fsdp, rows)])
     load(normed_t_ref.at[pl.ds(fsdp * own, own)], normed_all.at[:, lane_tile(fsdp, rows)])
-    for which in range(2):
-        target = (down_a_work, down_b_work)[which]
-        load(down_ref.at[which], target)
-    n = gate_work.shape[2]
-    chunk_loads = []
-    for which, (source, target) in enumerate(((gate_ref, gate_work), (up_ref, up_work))):
-        for chunk in range(count):
-            copy = pltpu.make_async_copy(
-                source.at[:, pl.ds(chunk * n, n)],
-                target.at[chunk],
-                local_sems.at[len(loads) + which * count + chunk],
-            )
-            copy.start()
-            chunk_loads.append(copy)
-
-    def prepare(unit):
-        q, g = q_ref[unit], g_ref[unit]
-        qg_ref[unit, :wide] = q.T
-        qg_ref[unit, wide:] = g.T
-        delta_ref[unit] = jnp.sum(
-            g[HD:].astype(jnp.float32) * mix_ref[unit], axis=0, keepdims=True
-        )
-        grad_q_ref[unit] = jnp.zeros((HD, wide), jnp.float32)
-
-    tiles(units, prepare)
-
-    for copy in loads + chunk_loads:
+    for copy in loads[:ring_loads]:
         copy.wait()
     pl.semaphore_wait(barrier, greeted)
     for ring in first_rings:
@@ -949,15 +932,30 @@
     for copy in turned:
         copy.start()
 
-    def tick(at):
-        for ring in first_rings:
-            if ring.exchange:
-                ring.tick(at)
-            else:
-
-                @pl.when(at < ring.ticks)
-                def _():
-                    ring.tick(jnp.minimum(at, ring.ticks - 1))
+    def prepare(unit):
+        q, g = q_ref[unit], g_ref[unit]
+        qg_ref[unit, :wide] = q.T
+        qg_ref[unit, wide:] = g.T
+        delta_ref[unit] = jnp.sum(
+            g[HD:].astype(jnp.float32) * mix_ref[unit], axis=0, keepdims=True
+        )
+        grad_q_ref[unit] = jnp.zeros((HD, wide), jnp.float32)
+
+    tiles(units, prepare)
+    for copy in loads[ring_loads:]:
+        copy.wait()
+
+    def tick(ring, at):
+        @pl.when(at < ring.ticks)
+        def _():
+            ring.tick(jnp.minimum(at, ring.ticks - 1))
+
+    def pump(at):
+        for turn, ring in enumerate(first_rings):
+
+            @pl.when(lax.rem(at, len(first_rings)) == turn)
+            def _():
+                tick(ring, lax.div(at, len(first_rings)))
 
     def back(unit, first, blocks, diagonal):
         kv = kv_ref[pl.ds(first, blocks), unit].reshape(blocks * keys, deep)
@@ -975,13 +973,6 @@
             blocks, keys, deep
         )
 
-    def over_units(body):
-        def two(at):
-            body(2 * at)
-            body(2 * at + 1)
-
-        tiles(units // 2, two)
-
     def across(pair):
         return pltpu.make_async_remote_copy(
             src_ref=kv_ref.at[2 * pair + 1 - steps.side],
@@ -1039,26 +1030,56 @@
                 kv_ref[2 * pair + steps.side] = final_ref[...].astype(kv_ref.dtype)
                 down_chain(pair).start()
 
+    turns = units // 2
+
     def slot(pair):
-        @pl.when(pair < steps.level)
+        def turn(at):
+            @pl.when(pair < steps.level)
+            def _():
+                for unit in (2 * at, 2 * at + 1):
+                    back(unit, 2 * pair, 2, False)
+
+            @pl.when(pair == steps.level)
+            def _():
+                for unit in (2 * at, 2 * at + 1):
+                    back(unit, ctx, 1, True)
+
+            @pl.when(jnp.logical_and(pair == steps.level, steps.side == 1))
+            def _():
+                for unit in (2 * at, 2 * at + 1):
+                    back(unit, ctx - 1, 1, False)
+
+            pump(pair * turns + at)
+
+        tiles(turns, turn)
+
+        @pl.when(jnp.logical_or(pair < steps.level, (pair == steps.level) & (steps.side == 1)))
         def _():
-            over_units(lambda unit: back(unit, 2 * pair, 2, False))
             across(pair).start()
 
-        @pl.when(pair == steps.level)
-        def _():
-            over_units(lambda unit: back(unit, ctx, 1, True))
-
-            @pl.when(steps.side == 1)
-            def _():
-                over_units(lambda unit: back(unit, ctx - 1, 1, False))
-                across(steps.level).start()
-
-        tick(pair)
         combine(pair)
 
     tiles(steps.levels, slot)
-    done = steps.levels
+    pumped = [steps.levels * turns]
+
+    def pump_next(times=1):
+        def body(at, unused, begin=pumped[0]):
+            pump(begin + at)
+            return unused
+
+        lax.fori_loop(0, times, body, 0)
+        pumped[0] += times
+
+    def pumping(times, body):
+        begin = pumped[0]
+
+        def step(at):
+            body(at)
+            pump(begin + at)
+
+        tiles(times, step)
+        pumped[0] += times
+
     cosine, sine = cos_ref[...], sin_ref[...]
 
     def unturn(columns):
@@ -1080,8 +1101,8 @@
             query_all[fsdp, span, pair * 2 * HD : (pair + 1) * 2 * HD] = (
                 jnp.concatenate(heads, axis=0).astype(jnp.bfloat16).T
             )
+        pump_next()
     query_gather.start(query_all.at[fsdp])
-    tick(done)
     combine(steps.levels)
     kv_width = KVH * HD
     for sequence in range(sequences):
@@ -1098,6 +1119,7 @@
                 )
     pair_gather.start(pair_all.at[fsdp])
     branch_gather.forward()
+    pump_next(2)
     query_gather.forward()
 
     step_out = width_tile(width)
@@ -1110,7 +1132,7 @@
             + dot_columns(pair_all[fsdp, :, kv_width:], w_value_ref[columns, :])
         )
 
-    tiles(width // step_out, upstream_tile)
+    pumping(width // step_out, upstream_tile)
     inputs = x_ref[...].astype(jnp.float32)
     scale = norm_scale(inputs)
     upstream = upstream_ref[...]
@@ -1141,7 +1163,7 @@
 
     for step in range(1, group):
         gain_copy(step).start()
-    tick(done + 1)
+    pump_next()
     for copy in turned:
         copy.wait_recv()
     for gather in (branch_gather, query_gather):
@@ -1150,67 +1172,65 @@
             gather.crossed(step)
     row_blocks = own // 16
 
-    def weight_grad(left, right, columns, target, first):
-        span = 384 if columns % 384 == 0 else LANES
+    def weight_grad(left, right, begin, end, target, first):
+        span = LANES * next(n for n in (3, 2, 1) if (end - begin) % (n * LANES) == 0)
 
         def body(at):
+            columns = pl.ds(pl.multiple_of(begin + at * span, LANES), span)
             part = forward_dot(
-                left[...], right[:, :, lane_tile(at, span)].reshape(group * rows, span)
+                left[...], right[:, :, columns].reshape(group * rows, span)
             ).astype(jnp.bfloat16)
             for block in range(span // LANES):
-                begin = first + (at * (span // LANES) + block) * row_blocks
-                target[pl.ds(begin, row_blocks)] = part[
+                here = first + (at * (span // LANES) + block) * row_blocks
+                target[pl.ds(here, row_blocks)] = part[
                     :, block * LANES : (block + 1) * LANES
                 ].reshape(row_blocks, 16, LANES)
 
-        tiles(columns // span, body)
-
-    weight_grad(low_all, branch_all, width, rest_b_work, 0)
-    weight_grad(normed_all, query_all, width, rest_a_work, 0)
-    tick(done + 2)
+        pumping((end - begin) // span, body)
+        return first + (end - begin) // LANES * row_blocks
+
+    def clear_from(target, first):
+        for spare in range(first, target.shape[0]):
+            target[spare] = jnp.zeros((16, LANES), jnp.bfloat16)
+
+    clear_from(out_work, weight_grad(low_all, branch_all, 0, width, out_work, 0))
+    out_ring.start()
+    split = query_split(width)
+    filled_a = weight_grad(normed_all, query_all, 0, split, rest_a_work, 0)
+    filled_b = weight_grad(normed_all, query_all, split, width, rest_b_work, 0)
     pair_gather.forward()
+    pump_next()
     pair_gather.sibling_here()
     for step in range(1, pair_gather.chips):
         pair_gather.crossed(step)
-    blocks = width // LANES * row_blocks
-    key_blocks = kv_width // LANES * row_blocks
-    weight_grad(normed_all, pair_all.at[:, :, :kv_width], kv_width, rest_a_work, blocks)
-    weight_grad(normed_all, pair_all.at[:, :, kv_width:], kv_width, rest_b_work, blocks)
+    filled_b = weight_grad(normed_all, pair_all, 0, 2 * kv_width, rest_b_work, filled_b)
     gains = gain_give[...]
     for step in range(1, group):
         gain_copy(step).wait_recv()
         gains = gains + gain_got[step - 1]
-    filled = blocks + key_blocks
     gain_tiles = gains.shape[0] // 16
-    rest_a_work[filled : filled + gain_tiles] = gains.astype(jnp.bfloat16).reshape(
+    rest_a_work[filled_a : filled_a + gain_tiles] = gains.astype(jnp.bfloat16).reshape(
         gain_tiles, 16, LANES
     )
-    for spare in range(filled + gain_tiles, rest_a_work.shape[0]):
-        rest_a_work[spare] = jnp.zeros((16, LANES), jnp.bfloat16)
-    for spare in range(filled, rest_b_work.shape[0]):
-        rest_b_work[spare] = jnp.zeros((16, LANES), jnp.bfloat16)
+    clear_from(rest_a_work, filled_a + gain_tiles)
+    clear_from(rest_b_work, filled_b)
     rest_a.start()
     rest_b.start()
-    begun = done + 3
-    left = gate_ring.ticks - begun
+    begun = pumped[0]
+    half = len(first_rings) // 2
+    total_pumps = gate_ring.ticks * len(first_rings)
 
     def last_ticks(at, unused):
-        @pl.when(at < left)
-        def _():
-            tick(jnp.minimum(begun + at, gate_ring.ticks - 1))
-
-        for ring in (rest_a, rest_b):
-            ring.tick(at)
+        for turn in range(half):
+            pump(jnp.minimum(begun + half * at + turn, total_pumps))
+        tick(out_ring, at)
+        tick(rest_a, at)
+        tick(rest_b, at)
         return unused
 
-    lax.fori_loop(0, rest_a.ticks, last_ticks, 0)
-
-    def more_ticks(at, unused):
-        tick(begun + at)
-        return unused
-
-    lax.fori_loop(rest_a.ticks, max(left, rest_a.ticks), more_ticks, 0)
-    for ring in first_rings + (rest_a, rest_b):
+    rounds = max(out_ring.ticks, -(-(total_pumps - begun) // half))
+    lax.fori_loop(0, rounds, last_ticks, 0)
+    for ring in first_rings + (out_ring, rest_a, rest_b):
         ring.finish()
     for copy in turned:
         copy.wait_send()
@@ -1229,6 +1249,16 @@
             down_chain(pair).wait_send()
 
     tiles(steps.level + 1, sent)
+
+
+def query_split(width):
+    return width // LANES * 7 // 9 * LANES
+
+
+def down_split(blocks, count):
+    each = -(-blocks // count)
+    first = max(1, each // 3)
+    return first, max(1, each - first)
 
 
 def layer_back(
@@ -1243,11 +1273,17 @@
     bf16, f32 = jnp.bfloat16, jnp.float32
     dma = pltpu.SemaphoreType.DMA
     wide_chunk = (group, gate_part.shape[1] // count, 16, LANES)
-    down_chunk = (down_part.shape[1] // count,) + down_part.shape[2:]
+    down_chunks = [(per,) + down_part.shape[1:] for per in down_split(down_part.shape[0], count)]
     gain_rows = spread(2 * (width // LANES), 16)
-    tiles_held = (width + kv_width) // LANES * (own // 16)
-    a_chunk = (spread(tiles_held + gain_rows // 16, count) // count, 16, LANES)
-    b_chunk = (spread(tiles_held, count) // count, 16, LANES)
+    split, row_blocks = query_split(width), own // 16
+    out_chunk, a_chunk, b_chunk = [
+        (spread(held, count) // count, 16, LANES)
+        for held in (
+            width // LANES * row_blocks,
+            split // LANES * row_blocks + gain_rows // 16,
+            (width - split + 2 * kv_width) // LANES * row_blocks,
+        )
+    ]
     levels = count // 2
     return pl.pallas_call(
         back_kernel,
@@ -1255,14 +1291,15 @@
             jax.ShapeDtypeStruct((rows, width), f32),
             ring_total(wide_chunk, True),
             ring_total(wide_chunk, True),
-            ring_total(down_chunk),
-            ring_total(down_chunk),
+            ring_total(down_chunks[0]),
+            ring_total(down_chunks[1]),
+            ring_total(out_chunk),
             ring_total(a_chunk),
             ring_total(b_chunk),
             *[jax.ShapeDtypeStruct((levels, units, keys, deep), bf16)] * 2,
         ],
         in_specs=[VMEM, VMEM, ANY, VMEM, VMEM, ANY, ANY, ANY, VMEM, ANY, ANY, ANY] + [VMEM] * 8,
-        out_specs=[VMEM] * 7 + [ANY] * 2,
+        out_specs=[VMEM] * 8 + [ANY] * 2,
         scratch_shapes=[
             pltpu.VMEM(all_pairs.shape, bf16),
             pltpu.VMEM((2, units, keys, deep), bf16),
@@ -1272,8 +1309,9 @@
             pltpu.VMEM((units, HD, wide), f32),
             *ring_scratch(wide_chunk, True),
             *ring_scratch(wide_chunk, True),
-            *ring_scratch(down_chunk),
-            *ring_scratch(down_chunk),
+            *ring_scratch(down_chunks[0]),
+            *ring_scratch(down_chunks[1]),
+            *ring_scratch(out_chunk),
             *ring_scratch(a_chunk),
             *ring_scratch(b_chunk),
             pltpu.VMEM((own, group * rows), bf16),
@@ -1286,10 +1324,7 @@
             pltpu.VMEM((group - 1, gain_rows, LANES), f32),
             *ring_semaphores(True),
             *ring_semaphores(True),
-            *ring_semaphores(),
-            *ring_semaphores(),
-            *ring_semaphores(),
-            *ring_semaphores(),
+            *[kind for _ in range(5) for kind in ring_semaphores()],
             *[dma((levels,))] * 4,
             *[group_semaphores()] * 6,
             *[dma((group - 1,))] * 6,
@@ -1313,18 +1348,69 @@
     )
 
 
-def from_tiles(held, rows):
-    blocks = held.shape[0] * 16 // rows
-    split = held.reshape(blocks, rows, LANES)
-    return jnp.swapaxes(split, 0, 1).reshape(rows, blocks * LANES).astype(jnp.float32)
-
-
-def from_parts(total, rows, columns):
-    count, group, n = total.shape[:3]
-    wide = columns // group // LANES
-    split = jnp.swapaxes(total, 0, 1).reshape(group, count * n, 16, LANES)
-    split = split[:, : wide * (rows // 16)].reshape(group, wide, rows, LANES)
-    return jnp.transpose(split, (2, 0, 1, 3)).reshape(rows, columns).astype(jnp.float32)
+def finish_kernel(
+    gate_ref, up_ref, down_a_ref, down_b_ref, out_ref, rest_a_ref, rest_b_ref,
+    query_grad, key_grad, value_grad, out_grad, gate_grad, up_grad, down_grad,
+):
+    rows = gate_grad.shape[0]
+    row_blocks = rows // 16
+    for source, target in ((gate_ref, gate_grad), (up_ref, up_grad)):
+        held = source[...].reshape((-1,) + source.shape[3:])
+        for block in range(target.shape[1] // LANES):
+            target[:, block * LANES : (block + 1) * LANES] = (
+                held[block * row_blocks : (block + 1) * row_blocks]
+                .reshape(rows, LANES)
+                .astype(jnp.float32)
+            )
+
+    @pl.when(pl.program_id(0) == 0)
+    def _():
+        def unpack(source, first, target, begin, end):
+            for block in range(begin, end):
+                here = first + (block - begin) * row_blocks
+                target[:, block * LANES : (block + 1) * LANES] = (
+                    source[here : here + row_blocks].reshape(rows, LANES).astype(jnp.float32)
+                )
+            return first + (end - begin) * row_blocks
+
+        width, kv_width = query_grad.shape[1], key_grad.shape[1]
+        split = query_split(width) // LANES
+        unpack(out_ref, 0, out_grad, 0, width // LANES)
+        unpack(rest_a_ref, 0, query_grad, 0, split)
+        at = unpack(rest_b_ref, 0, query_grad, split, width // LANES)
+        at = unpack(rest_b_ref, at, key_grad, 0, kv_width // LANES)
+        unpack(rest_b_ref, at, value_grad, 0, kv_width // LANES)
+        blocks = down_grad.shape[0] // 16
+        first = min(down_a_ref.shape[0], blocks)
+        for begin, end, source in ((0, first, down_a_ref), (first, blocks, down_b_ref)):
+            if end > begin:
+                down_grad[begin * 16 : end * 16, :] = (
+                    source[: end - begin]
+                    .reshape((end - begin) * 16, down_grad.shape[1])
+                    .astype(jnp.float32)
+                )
+
+
+def finish(gate, up, down_a, down_b, out, rest_a, rest_b, own, width, kv_width, hidden):
+    count, group, n = gate.shape[:3]
+
+    def whole(array):
+        return pl.BlockSpec(array.shape, lambda part, rank=len(array.shape): (0,) * rank)
+
+    wide = pl.BlockSpec((count, 1, n, 16, LANES), lambda part: (0, part, 0, 0, 0))
+    outs = [
+        jax.ShapeDtypeStruct((own, columns), jnp.float32)
+        for columns in (width, kv_width, kv_width, width, FF, FF)
+    ] + [jax.ShapeDtypeStruct((hidden, width), jnp.float32)]
+    slice_spec = pl.BlockSpec((own, FF // group), lambda part: (0, part))
+    return pl.pallas_call(
+        finish_kernel,
+        grid=(group,),
+        out_shape=outs,
+        in_specs=[wide, wide] + [whole(a) for a in (down_a, down_b, out, rest_a, rest_b)],
+        out_specs=[whole(a) for a in outs[:4]] + [slice_spec, slice_spec, whole(outs[6])],
+        compiler_params=pltpu.CompilerParams(vmem_limit_bytes=60 << 20),
+    )(gate, up, down_a, down_b, out, rest_a, rest_b)
 
 
 def on_device(
@@ -1385,11 +1471,11 @@
     )
     count = lax.axis_size("ctx")
     down_blocks = down_part.reshape(-1, 16, width)
-    spare = spread(down_blocks.shape[0], 2 * count) - down_blocks.shape[0]
+    spare = count * sum(down_split(down_blocks.shape[0], count)) - down_blocks.shape[0]
     down_blocks = jnp.pad(down_blocks, ((0, spare), (0, 0), (0, 0)))
     freqs = ROTARY_BASE ** (-2.0 * jnp.arange(HD // 2, dtype=jnp.float32) / HD)
     angles = freqs[:, None] * positions.astype(jnp.float32)[None, :]
-    grad_tokens, gate_total, up_total, down_a, down_b, rest_a, rest_b, _, _ = layer_back(
+    grad_tokens, gate_total, up_total, down_a, down_b, out_sum, rest_a, rest_b, _, _ = layer_back(
         q_wide,
         g_wide,
         all_pairs,
@@ -1397,7 +1483,7 @@
         log_total,
         gate_part,
         up_part,
-        down_blocks.reshape(2, -1, 16, width),
+        down_blocks,
         gain_term_ffn,
         grad_branch,
         low_t,
@@ -1412,22 +1498,18 @@
         jnp.sin(angles),
     )
     own = gain_attn.shape[0]
-    down_rows = jnp.concatenate([down_a, down_b]).reshape(-1, width)[: w_down.shape[0]]
-    blocks = width // LANES * (own // 16)
-    filled = blocks + kv_width // LANES * (own // 16)
+    filled = query_split(width) // LANES * (own // 16)
     gains = rest_a[filled:].reshape(-1, LANES)[: 2 * (width // LANES)].reshape(2, width)
     gains = lax.dynamic_slice_in_dim(gains, lax.axis_index("fsdp") * own, own, 1)
     gains = gains.astype(jnp.float32)
+    grads = finish(
+        gate_total, up_total, down_a, down_b, out_sum, rest_a, rest_b,
+        own, width, kv_width, w_down.shape[0],
+    )
     return (
         jnp.swapaxes(layer_out.reshape(seq_count, block_len, width), 0, 1),
         jnp.swapaxes(grad_tokens.reshape(seq_count, block_len, width), 0, 1),
-        from_tiles(rest_a[:blocks], own),
-        from_tiles(rest_a[blocks:filled], own),
-        from_tiles(rest_b[blocks:filled], own),
-        from_tiles(rest_b[:blocks], own),
-        from_parts(gate_total, own, FF),
-        from_parts(up_total, own, FF),
-        down_rows.astype(jnp.float32),
+        *grads,
         gains[0],
         gains[1],
     )

time: 454 us -> 434 us (0.956); the launches traced: 446 us -> 434 us
  local copies, waits for them, and re-layouts: 55.4 us -> 24.1 us
  Pallas kernels: 335 us -> 358 us
    convert_element_type x9 -> x0, local copies, waits for them, and re-layouts: 23.3 us -> none  [the longest x4 19 us: from_parts(): jnp.transpose(split, (2, 0, 1, 3)).reshape(rows, columns)]
    pallas_call x1, Pallas kernels: 200 us -> 214 us  [layer_back(): pl.pallas_call(back_kernel, out_shape=[jax.ShapeDtypeStruct((rows, width)...]
    pallas_call x0 -> x1, Pallas kernels: none -> 9.22 us  [finish(): pl.pallas_call(finish_kernel, grid=(group,), out_shape=outs, in_specs=[wi...]
where the time goes in v6:
time: 434 us
  Pallas kernels  358 us (82%)
  blocking collectives  31.7 us (7%)
  local copies, waits for them, and re-layouts  24.1 us (6%)
  between operations  15 us (3%)
    pallas_call x1, Pallas kernels, layer_back(): pl.pallas_call(back_kernel, out_shape=[jax.ShapeDtypeStruct((rows, width)...  214 us
    pallas_call x1, Pallas kernels, attend(): pl.pallas_call(attend_kernel, out_shape=[jax.ShapeDtypeStruct((sequences...  71.9 us
    pallas_call x1, Pallas kernels, feed_forward(): pl.pallas_call(ffn_kernel, out_shape=[jax.ShapeDtypeStruct((rows, width),...  62.9 us
    all_gather x2, blocking collectives, on_device(): lax.all_gather(weight, 'fsdp', axis=0, tiled=True)  23.2 us
    pallas_call x1, Pallas kernels, finish(): pl.pallas_call(finish_kernel, grid=(group,), out_shape=outs, in_specs=[wi...  9.22 us
  transfers between devices with their start and end apart: 1, of which 0 were waited for; matrix products, arithmetic and copies ran while one was open for 3% of the time, Pallas kernels for 0%

profile of v6, /device:TPU:0, one launch (start us, length us, event | category | flops | bytes accessed | tf_op | source)
XLA Modules:
  0.0 433.6 jit_solution(15944313304967213160)
XLA Ops:
  7.2 0.7 all-gather.2.cloned.1.call-update
  7.9 1.2 dynamic-slice
  9.8 0.9 dynamic-update-slice
  10.7 0.9 dynamic-update-slice.1
  11.6 8.5 %all-reduce.3 = (bf16[1152]{0:T(1024)(128)(2,1)S(1)}, bf16[1152]{0:T(1024)(128)(2,1)S(1)}) all-reduce(bf16[1152]{0:T(1024)(128)(2,1)S(1)} %dynamic-update-slice, bf16[1152]{0:T(1024)(128)(2,1)S(1)} %dynamic-update-slice.1), channel_id=1, replica_groups=mesh['fsdp'=4,'ctx'=8] {'fsdp'}, use_global_device_ids=true, to_apply=%add.1 | all-reduce | flops 2304 | bytes 9216
  20.7 1.1 copy.65
  22.1 13.9 %all_gather.18.w_value_ref = bf16[1152,384]{1,0:T(8,128)(2,1)S(1)} all-gather(bf16[288,384]{1,0:T(8,128)(2,1)S(1)} %copy-done.6), channel_id=1, replica_groups=mesh['fsdp'=4,'ctx'=8] {'fsdp'}, dimensions={0}, use_global_device_ids=true | all-gather | bytes 1105920 | tf_op jit(solution)/shard_map/all_gather | solution.py:1423
  36.0 0.9 copy-done.2
  37.9 9.2 %all_gather.17.w_key_ref = bf16[1152,384]{1,0:T(8,128)(2,1)S(1)} all-gather(bf16[288,384]{1,0:T(8,128)(2,1)S(1)} %copy-done.7), channel_id=1, replica_groups=mesh['fsdp'=4,'ctx'=8] {'fsdp'}, dimensions={0}, use_global_device_ids=true | all-gather | bytes 1105920 | tf_op jit(solution)/shard_map/all_gather | solution.py:1423
  47.1 0.9 copy.70
  49.6 1.0 copy.74
  50.6 0.9 copy.75
  52.3 1.1 copy.77.normed_t_ref
  53.4 0.8 multiply_sine_fusion
  54.1 4.2 copy.68
  58.3 1.1 fusion.6
  60.8 1.2 concatenate.14.q_ref
  62.0 71.9 %shard_map.194 = (bf16[256,1152]{1,0:T(8,128)(2,1)}, bf16[1152,256]{1,0:T(8,128)(2,1)}, f32[12,64,384]{2,1,0:T(8,128)}, f32[12,1,384]{2,1,0:T(1,128)}, bf16[8,12...) custom-call(bf16[12,128,384]{2,1,0:T(8,128)(2,1)} %concatenate.14.q_, ...), custom_call_target="tpu_custom_call" | custom-call | tf_op jit(solution)/shard_map/pallas_call | solution.py:359
  133.9 62.9 %shard_map.195 = (bf16[256,1152]{1,0:T(8,128)(2,1)}, f32[256,1152]{1,0:T(8,128)}, bf16[256,1152]{1,0:T(8,128)(2,1)}, bf16[12,128,384]{2,1,0:T(8,128)(2,1)}, bf16...) custom-call(bf16[256,1152]{1,0:T(8,128)(2,1)} %bitcast.53, ...), custom_call_target="tpu_custom_call" | custom-call | tf_op jit(solution)/shard_map/pallas_call | solution.py:671
  196.8 2.5 copy.95
  199.3 213.6 %shard_map.196 = (f32[256,1152]{1,0:T(8,128)}, bf16[8,4,14,16,128]{4,3,2,1,0:T(8,128)(2,1)}, bf16[8,4,14,16,128]{4,3,2,1,0:T(8,128)(2,1)}, bf16[16,16,1152]{2,1,...) custom-call(bf16[12,128,384]{2,1,0:T(8,128)(2,1)} %concatenate.14.q_, ...), custom_call_target="tpu_custom_call" | custom-call | tf_op jit(solution)/shard_map/pallas_call | solution.py:1288
  412.9 3.2 copy.93
  416.1 0.7 slice.28
  417.5 9.2 %shard_map.197 = (f32[288,1152]{1,0:T(8,128)}, f32[288,384]{1,0:T(8,128)}, f32[288,384]{1,0:T(8,128)}, f32[288,1152]{1,0:T(8,128)}, f32[288,3072]{1,0:T(8,128)},...) custom-call(bf16[8,4,14,16,128]{4,3,2,1,0:T(8,128)(2,1)} %get-tuple-element.61.gate_ref, ...), custom_call_target="tpu_custom_call" | custom-call | tf_op jit(solution)/shard_map/pallas_call | solution.py:1406
  (44 shorter events, 6.2 us)
Async XLA Ops:
  7.2 14.7 %copy-start.3 = (bf16[128,2,1152]{2,1,0:T(2,128)(2,1)S(1)}, bf16[128,2,1152]{2,1,0:T(2,128)(2,1)}, u32[]{:S(2)}) copy-start(bf16[128,2,1152]{2,1,0:T(2,128)(2,1)} %param.11) | copy-start | bytes 1769476
  7.2 14.9 %copy-start.6 = (bf16[288,384]{1,0:T(8,128)(2,1)S(1)}, bf16[288,384]{1,0:T(8,128)(2,1)}, u32[]{:S(2)}) copy-start(bf16[288,384]{1,0:T(8,128)(2,1)} %param.14) | copy-start | bytes 663556
  7.2 46.9 %all-gather.2.cloned.1.call-start = ((), (), s32[]{:S(2)}) async-start(), calls=%async_computation | async-start | bytes 3317760 | tf_op jit(solution)/shard_map/all_gather | solution.py:1423
  21.9 30.3 %copy-start = (bf16[128,2,1152]{2,0,1:T(8,128)(2,1)}, bf16[128,2,1152]{2,0,1:T(8,128)(2,1)S(1)}, u32[]{:S(2)}) copy-start(bf16[128,2,1152]{2,0,1:T(8,128)(2,1)S(1)} %copy.65) | copy-start | bytes 1769476
  36.0 0.9 copy-start.2
  36.9 0.9 copy-start.7
  47.1 1.6 copy-start.1
  48.7 1.9 copy-start.5
  54.1 4.2 copy-start.4
Sparse Core Ops, SparseCore 0:
  9.6 33.1 all-gather.1

commit v7 on v6

--- a/solution.py
+++ b/solution.py
@@ -389,6 +389,218 @@
     )(q_wide, pairs, w_out, w_gate, w_up, g_rows)
 
 
+class Ring:
+    def __init__(self, work, landing, total, semaphores, forward, exchange=False):
+        self.fsdp, self.ctx = lax.axis_index("fsdp"), lax.axis_index("ctx")
+        self.group, self.count = lax.axis_size("fsdp"), lax.axis_size("ctx")
+        self.work, self.landing, self.total = work, landing, total
+        self.sends, self.arrivals = semaphores[:2]
+        self.part_sends, self.part_arrivals, self.own_sem = semaphores[2:] if exchange else (None,) * 3
+        self.exchange = exchange
+        side = 0 if forward else 1
+        self.place = ring_place(self.ctx, side, self.count)
+        self.after = (self.fsdp, ring_ctx(lax.rem(self.place + 1, self.count), side, self.count))
+        self.ticks = 2 * self.count - 2 + int(exchange)
+
+    def chunk(self, held, index):
+        if self.exchange:
+            return held.at[index]
+        per = held.shape[0] // self.count
+        return held.at[pl.ds(index * per, per)]
+
+    def summing(self, step, index):
+        return self.copy(self.chunk(self.work, index), self.landing.at[step], step)
+
+    def handing(self, step, index):
+        held = self.chunk(self.total, index)
+        return self.copy(held, held, step)
+
+    def copy(self, source, target, step):
+        return pltpu.make_async_remote_copy(
+            src_ref=source,
+            dst_ref=target,
+            send_sem=self.sends.at[step],
+            recv_sem=self.arrivals.at[step],
+            device_id=self.after,
+            device_id_type=MESH,
+        )
+
+    def part(self, index, step):
+        peer = lax.rem(self.fsdp + step, self.group)
+        return pltpu.make_async_remote_copy(
+            src_ref=self.work.at[index, peer],
+            dst_ref=self.total.at[index, self.fsdp],
+            send_sem=self.part_sends.at[step - 1],
+            recv_sem=self.part_arrivals.at[step - 1],
+            device_id=(peer, self.ctx),
+            device_id_type=MESH,
+        )
+
+    def own_part(self, index):
+        return pltpu.make_async_copy(
+            self.work.at[index, self.fsdp], self.total.at[index, self.fsdp], self.own_sem
+        )
+
+    def start(self):
+        self.summing(0, self.place).start()
+
+    def tick(self, at):
+        last = self.count - 2
+        gap = int(self.exchange)
+        step = at - gap * jnp.where(at > last, 1, 0) if self.exchange else at
+        index = lax.rem(self.place + 3 * self.count - 1 - step, self.count)
+
+        def add(target):
+            part, landed = self.chunk(self.work, index), self.landing.at[jnp.minimum(at, last)]
+            for row in range(part.shape[0]):
+                target[row] = (
+                    part[row].astype(jnp.float32) + landed[row].astype(jnp.float32)
+                ).astype(part.dtype)
+
+        @pl.when(at <= last)
+        def _():
+            self.summing(jnp.minimum(at, last), index).wait_recv()
+
+        @pl.when(at < last)
+        def _():
+            add(self.chunk(self.work, index))
+            self.summing(jnp.minimum(at + 1, last), index).start()
+
+        if self.exchange:
+
+            @pl.when(at == last)
+            def _():
+                add(self.chunk(self.work, index))
+                for peer in range(1, self.group):
+                    self.part(index, peer).start()
+                self.own_part(index).start()
+
+            @pl.when(at == last + 1)
+            def _():
+                done = lax.rem(self.place + 1, self.count)
+                self.own_part(done).wait()
+                for peer in range(1, self.group):
+                    self.part(done, peer).wait_recv()
+                self.handing(last + 1, done).start()
+
+        else:
+
+            @pl.when(at == last)
+            def _():
+                add(self.chunk(self.total, index))
+                self.handing(last + 1, index).start()
+
+        @pl.when(at > last + gap)
+        def _():
+            here = jnp.maximum(step, last + 1)
+            self.handing(here, index).wait_recv()
+
+            @pl.when(here < 2 * self.count - 3)
+            def _():
+                self.handing(jnp.minimum(here + 1, 2 * self.count - 3), index).start()
+
+    def finish(self):
+        def wait(step, unused):
+            self.handing(step, self.place).wait_send()
+            return unused
+
+        lax.fori_loop(0, 2 * self.count - 2, wait, 0)
+        if self.exchange:
+            for peer in range(1, self.group):
+                self.part(lax.rem(self.place + 1, self.count), peer).wait_send()
+
+
+class SumRing(Ring):
+    def __init__(self, *args):
+        super().__init__(*args)
+        self.ticks = self.count - 1
+
+    def tick(self, at):
+        last = self.count - 2
+        index = lax.rem(self.place + 2 * self.count - 1 - at, self.count)
+        self.summing(at, index).wait_recv()
+        work, landed = self.chunk(self.work, index), self.landing.at[at]
+
+        def add(target):
+            for row in range(work.shape[0]):
+                target[row] = (
+                    work[row].astype(jnp.float32) + landed[row].astype(jnp.float32)
+                ).astype(work.dtype)
+
+        @pl.when(at < last)
+        def _():
+            add(work)
+            self.summing(jnp.minimum(at + 1, last), index).start()
+
+        @pl.when(at == last)
+        def _():
+            add(self.total)
+
+    def finish(self):
+        def wait(step, unused):
+            self.summing(step, self.place).wait_send()
+            return unused
+
+        lax.fori_loop(0, self.ticks, wait, 0)
+
+
+class SpreadRing(Ring):
+    def __init__(self, total, semaphores, forward):
+        super().__init__(None, None, total, semaphores, forward)
+        self.ticks = self.count - 1
+        self.first = lax.rem(self.place + 1, self.count)
+
+    def start(self):
+        self.handing(0, self.first).start()
+
+    def tick(self, at):
+        index = lax.rem(self.place + self.count - at, self.count)
+        self.handing(at, index).wait_recv()
+
+        @pl.when(at < self.count - 2)
+        def _():
+            self.handing(jnp.minimum(at + 1, self.count - 2), index).start()
+
+    def finish(self):
+        def wait(step, unused):
+            self.handing(step, self.place).wait_send()
+            return unused
+
+        lax.fori_loop(0, self.ticks, wait, 0)
+
+
+def ring_scratch(chunk, exchange=False):
+    count = lax.axis_size("ctx")
+    work = (count,) + chunk if exchange else (count * chunk[0],) + chunk[1:]
+    return [pltpu.VMEM(work, jnp.bfloat16), pltpu.VMEM((count - 1,) + chunk, jnp.bfloat16)]
+
+
+def ring_total(chunk, exchange=False):
+    count = lax.axis_size("ctx")
+    work = (count,) + chunk if exchange else (count * chunk[0],) + chunk[1:]
+    return jax.ShapeDtypeStruct(work, jnp.bfloat16)
+
+
+def ring_semaphores(exchange=False):
+    dma, steps = pltpu.SemaphoreType.DMA, 2 * lax.axis_size("ctx") - 2
+    parts = lax.axis_size("fsdp") - 1
+    return [dma((steps,))] * 2 + ([dma((parts,))] * 2 + [dma] if exchange else [])
+
+
+def query_split(width):
+    return width // LANES * 7 // 9 * LANES
+
+
+def out_split(width):
+    return (width // LANES + 1) // 2 * LANES
+
+
+def down_split(blocks, count):
+    each = -(-blocks // count)
+    first = max(1, each // 2)
+    return first, max(1, each - first)
+
+
 class GroupScatter:
     def __init__(self, give_sib, got_sib, give_cross, got_cross, far, got_far, sends, arrivals):
         self.give_sib, self.got_sib = give_sib, got_sib
@@ -415,7 +627,7 @@
 
     def to_cross(self, step):
         return self.copy(
-            self.give_cross.at[step - 1], self.got_cross.at[step - 1], step, self.sibling
+            self.give_cross(step), self.got_cross.at[step - 1], step, self.sibling
         )
 
     def to_far(self, step):
@@ -494,18 +706,23 @@
 
 def ffn_kernel(
     x_ref, low_ref, out_ref, gate_ref, up_ref, down_ref, all_g_ref, gain_ref,
-    layer_ref, resid_grad_ref, branch_ref, g_wide_ref, gate_part_ref, up_part_ref, down_part_ref,
-    gain_grad_ref,
-    all_n_ref, turned_n, turned_act, act_ref, gate_grad, up_grad, resid_ref, layer_own, grad_own,
-    *rest,
+    layer_ref, layer_part_ref, resid_grad_ref, branch_ref, g_wide_ref, gate_part_ref, up_part_ref,
+    down_a_done, down_b_done, gain_grad_ref,
+    all_n_ref, turned_n, turned_act, act_ref, gate_grad, up_grad, resid_ref, grad_own,
+    down_a_work, down_a_land, down_b_work, down_b_land, *rest,
 ):
-    down_scratch, grad_scratch = rest[:6], rest[6:12]
-    n_sends, n_arrivals, down_sends, down_arrivals, grad_sends, grad_arrivals = rest[12:]
+    give_sib, got_sib, give_cross, got_cross, far, got_far = rest[:6]
+    n_sends, n_arrivals, grad_sends, grad_arrivals = rest[6:10]
+    down_a = SumRing(down_a_work, down_a_land, down_a_done, rest[10:12], True)
+    down_b = SumRing(down_b_work, down_b_land, down_b_done, rest[12:14], False)
+    rings = (down_a, down_b)
     group = lax.axis_size("fsdp")
     rows, width = x_ref.shape
     hidden = gate_ref.shape[1]
     barrier = pltpu.get_barrier_semaphore()
-    greeted = greet_group(barrier)
+    greeted = greet_group(barrier) + len(rings)
+    for ring in rings:
+        pl.semaphore_signal(barrier, inc=1, device_id=ring.after, device_id_type=MESH)
     step_in, step_out = hidden_tile(hidden), width_tile(width)
 
     def branch(at):
@@ -522,8 +739,16 @@
     all_n_ref[fsdp] = (resid_ref[...] * scale * gain).astype(jnp.bfloat16)
     pl.semaphore_wait(barrier, greeted)
     gathered.start(all_n_ref.at[fsdp])
-    layer_sum = GroupScatter(*down_scratch, down_sends, down_arrivals)
-    grad_sum = GroupScatter(*grad_scratch, grad_sends, grad_arrivals)
+    grad_sum = GroupScatter(
+        give_sib,
+        got_sib,
+        lambda step: give_cross.at[step - 1],
+        got_cross,
+        far,
+        got_far,
+        grad_sends,
+        grad_arrivals,
+    )
 
     def hidden_part(shard):
         def body(at):
@@ -554,53 +779,69 @@
 
         tiles(width // step_out, body)
 
-    def layer_part(shard, target):
-        def body(at):
-            columns = lane_tile(at, step_out)
-            target[:, columns] = forward_dot(act_ref[shard], down_ref[:, columns]).astype(
-                target.dtype
-            )
-
-        tiles(width // step_out, body)
-
     hidden_part(fsdp)
     gathered.sibling_here()
     sibling = gathered.sibling
     hidden_part(sibling)
     grad_part(sibling, grad_sum.give_sib)
     grad_sum.to_sibling().start()
-    layer_part(sibling, layer_sum.give_sib)
-    layer_sum.to_sibling().start()
     gathered.forward()
     grad_part(fsdp, grad_own)
-    layer_part(fsdp, layer_own)
     for step in range(1, chips):
         ours = gathered.same_core(chips - step)
         theirs = ours + sibling - fsdp
         gathered.crossed(step)
         hidden_part(theirs)
-        grad_part(theirs, grad_sum.give_cross.at[step - 1])
+        grad_part(theirs, give_cross.at[step - 1])
         grad_sum.to_cross(step).start()
         hidden_part(ours)
-        grad_part(ours, grad_sum.far.at[step - 1])
+        grad_part(ours, far.at[step - 1])
         grad_sum.add_cross(step)
-        layer_part(theirs, layer_sum.give_cross.at[step - 1])
-        layer_sum.to_cross(step).start()
-        layer_part(ours, layer_sum.far.at[step - 1])
-        layer_sum.add_cross(step)
+    for shard in range(group):
+        span = slice(shard * rows, (shard + 1) * rows)
+        transpose_into(turned_act.at[:, span], act_ref.at[shard])
+    blocks = hidden // 16
+    first = min(blocks, down_a_work.shape[0])
+
+    def down_tile(at):
+        columns = lane_tile(at, step_out)
+        part = forward_dot(
+            turned_act[...], all_g_ref[:, :, columns].reshape(group * rows, step_out)
+        ).astype(jnp.bfloat16)
+        for begin, end, work in ((0, first, down_a_work), (first, blocks, down_b_work)):
+            if end > begin:
+                work[: end - begin, :, columns] = part[begin * 16 : end * 16].reshape(
+                    end - begin, 16, step_out
+                )
+
+    tiles(width // step_out, down_tile)
+    for work, filled in ((down_a_work, first), (down_b_work, blocks - first)):
+        for spare in range(filled, work.shape[0]):
+            work[spare] = jnp.zeros(work.shape[1:], work.dtype)
+    for ring in rings:
+        ring.start()
+    ticked = [0]
+
+    def ring_tick(at):
+        for ring in rings:
+
+            @pl.when(at < ring.ticks)
+            def _():
+                ring.tick(jnp.minimum(at, ring.ticks - 1))
+
+    def ticking(times, body):
+        begin = ticked[0]
+
+        def step(at):
+            body(at)
+            ring_tick(begin + at)
+
+        tiles(times, step)
+        ticked[0] += times
 
     for shard in range(group):
         span = slice(shard * rows, (shard + 1) * rows)
         transpose_into(turned_n.at[:, span], all_n_ref.at[shard])
-        transpose_into(turned_act.at[:, span], act_ref.at[shard])
-
-    def down_tile(at):
-        columns = lane_tile(at, step_out)
-        down_part_ref[:, columns] = forward_dot(
-            turned_act[...], all_g_ref[:, :, columns].reshape(group * rows, step_out)
-        ).astype(jnp.bfloat16)
-
-    tiles(width // step_out, down_tile)
     own = width // group
     row_blocks = own // 16
     for source, target in ((gate_grad, gate_part_ref), (up_grad, up_part_ref)):
@@ -617,12 +858,21 @@
                         owner * own : (owner + 1) * own, block * LANES : (block + 1) * LANES
                     ].reshape(row_blocks, 16, LANES)
 
-        tiles(hidden // step_in, weight_tile)
+        ticking(hidden // step_in, weight_tile)
         filled = hidden // LANES * row_blocks
         for spare in range(filled, target.shape[1]):
             for owner in range(group):
                 target[owner, spare] = jnp.zeros(target.shape[2:], target.dtype)
 
+    def layer_tile(at):
+        columns = lane_tile(at, step_out)
+        part = forward_dot(
+            act_ref[...].reshape(group * rows, hidden), down_ref[:, columns]
+        ).reshape(group, rows, step_out)
+        layer_part_ref[:, :, columns] = part.astype(jnp.bfloat16)
+
+    ticking(width // step_out, layer_tile)
+    layer_ref[...] = resid_ref[...] + layer_part_ref[fsdp].astype(jnp.float32)
     upstream = grad_sum.total(grad_own[...])
     resid = resid_ref[...]
     scaled = upstream * gain
@@ -650,10 +900,12 @@
                 g_wide_ref[unit, HD:, member * keys : (member + 1) * keys] = turned[
                     half * HD : (half + 1) * HD
                 ]
-    layer_ref[...] = (resid + layer_sum.total(layer_own[...])).astype(jnp.bfloat16)
+    begin = ticked[0]
+    tiles(max(0, down_a.ticks - begin), lambda at: ring_tick(begin + at))
     gathered.sent()
     grad_sum.sent()
-    layer_sum.sent()
+    for ring in rings:
+        ring.finish()
 
 
 def spread(blocks, count):
@@ -668,20 +920,22 @@
     chips = group // 2
     dma = pltpu.SemaphoreType.DMA((2 * chips - 1,))
     bf16 = jnp.bfloat16
+    down_chunks = [(per, 16, width) for per in down_split(hidden // 16, count)]
     return pl.pallas_call(
         ffn_kernel,
         out_shape=[
-            jax.ShapeDtypeStruct((rows, width), bf16),
+            jax.ShapeDtypeStruct((rows, width), jnp.float32),
+            jax.ShapeDtypeStruct((group, rows, width), bf16),
             jax.ShapeDtypeStruct((rows, width), jnp.float32),
             jax.ShapeDtypeStruct((rows, width), bf16),
             jax.ShapeDtypeStruct((units, 2 * HD, wide), bf16),
             jax.ShapeDtypeStruct((group, blocks, 16, LANES), bf16),
             jax.ShapeDtypeStruct((group, blocks, 16, LANES), bf16),
-            jax.ShapeDtypeStruct((hidden, width), bf16),
+            *[jax.ShapeDtypeStruct(chunk, bf16) for chunk in down_chunks],
             jax.ShapeDtypeStruct((1, width), jnp.float32),
         ],
         in_specs=[VMEM] * 8,
-        out_specs=[VMEM] * 8,
+        out_specs=[VMEM] * 10,
         scratch_shapes=[
             pltpu.VMEM((group, rows, width), bf16),
             pltpu.VMEM((width, group * rows), bf16),
@@ -691,10 +945,12 @@
             pltpu.VMEM((group, rows, hidden), bf16),
             pltpu.VMEM((rows, width), jnp.float32),
             pltpu.VMEM((rows, width), jnp.float32),
-            pltpu.VMEM((rows, width), jnp.float32),
+            *ring_scratch(down_chunks[0]),
+            *ring_scratch(down_chunks[1]),
             *scatter_scratch(rows, width),
-            *scatter_scratch(rows, width),
-            *[dma] * 6,
+            *[dma] * 4,
+            *ring_semaphores(),
+            *ring_semaphores(),
         ],
         compiler_params=pltpu.CompilerParams(
             collective_id=2, has_side_effects=True, vmem_limit_bytes=60 << 20
@@ -702,155 +958,17 @@
     )(x, low, full_out, my_gate, my_up, my_down, all_g, gain)
 
 
-class Ring:
-    def __init__(self, work, landing, total, semaphores, forward, exchange=False):
-        self.fsdp, self.ctx = lax.axis_index("fsdp"), lax.axis_index("ctx")
-        self.group, self.count = lax.axis_size("fsdp"), lax.axis_size("ctx")
-        self.work, self.landing, self.total = work, landing, total
-        self.sends, self.arrivals = semaphores[:2]
-        self.part_sends, self.part_arrivals, self.own_sem = semaphores[2:] if exchange else (None,) * 3
-        self.exchange = exchange
-        side = 0 if forward else 1
-        self.place = ring_place(self.ctx, side, self.count)
-        self.after = (self.fsdp, ring_ctx(lax.rem(self.place + 1, self.count), side, self.count))
-        self.ticks = 2 * self.count - 2 + int(exchange)
-
-    def chunk(self, held, index):
-        if self.exchange:
-            return held.at[index]
-        per = held.shape[0] // self.count
-        return held.at[pl.ds(index * per, per)]
-
-    def summing(self, step, index):
-        return self.copy(self.chunk(self.work, index), self.landing.at[step], step)
-
-    def handing(self, step, index):
-        held = self.chunk(self.total, index)
-        return self.copy(held, held, step)
-
-    def copy(self, source, target, step):
-        return pltpu.make_async_remote_copy(
-            src_ref=source,
-            dst_ref=target,
-            send_sem=self.sends.at[step],
-            recv_sem=self.arrivals.at[step],
-            device_id=self.after,
-            device_id_type=MESH,
-        )
-
-    def part(self, index, step):
-        peer = lax.rem(self.fsdp + step, self.group)
-        return pltpu.make_async_remote_copy(
-            src_ref=self.work.at[index, peer],
-            dst_ref=self.total.at[index, self.fsdp],
-            send_sem=self.part_sends.at[step - 1],
-            recv_sem=self.part_arrivals.at[step - 1],
-            device_id=(peer, self.ctx),
-            device_id_type=MESH,
-        )
-
-    def own_part(self, index):
-        return pltpu.make_async_copy(
-            self.work.at[index, self.fsdp], self.total.at[index, self.fsdp], self.own_sem
-        )
-
-    def start(self):
-        self.summing(0, self.place).start()
-
-    def tick(self, at):
-        last = self.count - 2
-        gap = int(self.exchange)
-        step = at - gap * jnp.where(at > last, 1, 0) if self.exchange else at
-        index = lax.rem(self.place + 3 * self.count - 1 - step, self.count)
-
-        def add(target):
-            part, landed = self.chunk(self.work, index), self.landing.at[jnp.minimum(at, last)]
-            for row in range(part.shape[0]):
-                target[row] = (
-                    part[row].astype(jnp.float32) + landed[row].astype(jnp.float32)
-                ).astype(part.dtype)
-
-        @pl.when(at <= last)
-        def _():
-            self.summing(jnp.minimum(at, last), index).wait_recv()
-
-        @pl.when(at < last)
-        def _():
-            add(self.chunk(self.work, index))
-            self.summing(jnp.minimum(at + 1, last), index).start()
-
-        if self.exchange:
-
-            @pl.when(at == last)
-            def _():
-                add(self.chunk(self.work, index))
-                for peer in range(1, self.group):
-                    self.part(index, peer).start()
-                self.own_part(index).start()
-
-            @pl.when(at == last + 1)
-            def _():
-                done = lax.rem(self.place + 1, self.count)
-                self.own_part(done).wait()
-                for peer in range(1, self.group):
-                    self.part(done, peer).wait_recv()
-                self.handing(last + 1, done).start()
-
-        else:
-
-            @pl.when(at == last)
-            def _():
-                add(self.chunk(self.total, index))
-                self.handing(last + 1, index).start()
-
-        @pl.when(at > last + gap)
-        def _():
-            here = jnp.maximum(step, last + 1)
-            self.handing(here, index).wait_recv()
-
-            @pl.when(here < 2 * self.count - 3)
-            def _():
-                self.handing(jnp.minimum(here + 1, 2 * self.count - 3), index).start()
-
-    def finish(self):
-        def wait(step, unused):
-            self.handing(step, self.place).wait_send()
-            return unused
-
-        lax.fori_loop(0, 2 * self.count - 2, wait, 0)
-        if self.exchange:
-            for peer in range(1, self.group):
-                self.part(lax.rem(self.place + 1, self.count), peer).wait_send()
-
-
-def ring_scratch(chunk, exchange=False):
-    count = lax.axis_size("ctx")
-    work = (count,) + chunk if exchange else (count * chunk[0],) + chunk[1:]
-    return [pltpu.VMEM(work, jnp.bfloat16), pltpu.VMEM((count - 1,) + chunk, jnp.bfloat16)]
-
-
-def ring_total(chunk, exchange=False):
-    count = lax.axis_size("ctx")
-    work = (count,) + chunk if exchange else (count * chunk[0],) + chunk[1:]
-    return jax.ShapeDtypeStruct(work, jnp.bfloat16)
-
-
-def ring_semaphores(exchange=False):
-    dma, steps = pltpu.SemaphoreType.DMA, 2 * lax.axis_size("ctx") - 2
-    parts = lax.axis_size("fsdp") - 1
-    return [dma((steps,))] * 2 + ([dma((parts,))] * 2 + [dma] if exchange else [])
-
-
 def back_kernel(
-    q_ref, g_ref, pairs_ref, mix_ref, log_ref, gate_ref, up_ref, down_ref, gain_grad_ref,
-    branch_ref, low_t_ref, normed_t_ref, w_query_ref, w_key_ref, w_value_ref, x_ref, gain_ref,
+    q_ref, g_ref, pairs_ref, mix_ref, log_ref, gate_ref, up_ref, down_a_ref, down_b_ref,
+    layer_base_ref, layer_part_ref, gain_grad_ref, branch_ref, low_t_ref, normed_t_ref, w_query_ref, w_key_ref, w_value_ref, x_ref, gain_ref,
     resid_grad_ref, cos_ref, sin_ref,
-    tokens_ref, gate_total, up_total, down_a_total, down_b_total, out_total, rest_a_total,
-    rest_b_total, peer_got, chain_got,
+    tokens_ref, layer_ref, gate_total, up_total, down_a_total, down_b_total, out_a_total,
+    out_b_total, rest_a_total, rest_b_total, peer_got, chain_got, layer_sib, layer_cross, layer_far,
     kv_ref, stage_ref, final_ref, qg_ref, delta_ref, grad_q_ref,
-    gate_work, gate_land, up_work, up_land, down_a_work, down_a_land, down_b_work, down_b_land,
-    out_work, out_land, rest_a_work, rest_a_land, rest_b_work, rest_b_land,
+    gate_work, gate_land, up_work, up_land, out_a_work, out_a_land, out_b_work, out_b_land,
+    rest_a_work, rest_a_land, rest_b_work, rest_b_land,
     low_all, normed_all, branch_all, query_all, pair_all, upstream_ref, gain_give, gain_got,
+    far_ref, layer_stage,
     *semaphores,
 ):
     steps = Steps()
@@ -866,12 +984,25 @@
 
     gate_ring = Ring(gate_work, gate_land, gate_total, take(5), True, True)
     up_ring = Ring(up_work, up_land, up_total, take(5), False, True)
-    down_a = Ring(down_a_work, down_a_land, down_a_total, take(2), True)
-    down_b = Ring(down_b_work, down_b_land, down_b_total, take(2), False)
-    out_ring = Ring(out_work, out_land, out_total, take(2), True)
+    down_a = SpreadRing(down_a_total, take(2), True)
+    down_b = SpreadRing(down_b_total, take(2), False)
+    out_a = Ring(out_a_work, out_a_land, out_a_total, take(2), True)
+    out_b = Ring(out_b_work, out_b_land, out_b_total, take(2), False)
+    layer_sum = GroupScatter(
+        None,
+        layer_sib,
+        lambda step: layer_part_ref.at[
+            2 * lax.rem(lax.div(fsdp, 2) + group // 2 - step, group // 2) + 1 - lax.rem(fsdp, 2)
+        ],
+        layer_cross,
+        far_ref,
+        layer_far,
+        *take(2),
+    )
+    layer_sum.give_sib = layer_part_ref.at[layer_sum.sibling]
     rest_a = Ring(rest_a_work, rest_a_land, rest_a_total, take(2), True)
     rest_b = Ring(rest_b_work, rest_b_land, rest_b_total, take(2), False)
-    first_rings = (gate_ring, up_ring, down_a, down_b)
+    first_rings = (gate_ring, up_ring, down_a, down_b, out_a, out_b)
     peer_sends, peer_arrivals, chain_sends, chain_arrivals = take(4)
     branch_gather = GroupGather(lambda shard: branch_all.at[shard], *take(2))
     query_gather = GroupGather(lambda shard: query_all.at[shard], *take(2))
@@ -895,9 +1026,8 @@
     for source, target in ((gate_ref, gate_work), (up_ref, up_work)):
         for chunk in range(count):
             load(source.at[:, pl.ds(chunk * n, n)], target.at[chunk])
-    first = down_a_work.shape[0]
-    load(down_ref.at[pl.ds(0, first)], down_a_work)
-    load(down_ref.at[pl.ds(first, down_b_work.shape[0])], down_b_work)
+    for ring, source in ((down_a, down_a_ref), (down_b, down_b_ref)):
+        load(source, ring.chunk(ring.total, ring.first))
     ring_loads = len(loads)
     load(pairs_ref, kv_ref)
     load(branch_ref, branch_all.at[fsdp])
@@ -906,9 +1036,12 @@
     for copy in loads[:ring_loads]:
         copy.wait()
     pl.semaphore_wait(barrier, greeted)
-    for ring in first_rings:
+    for ring in first_rings[:4]:
         ring.start()
     branch_gather.start(branch_ref)
+    layer_sum.to_sibling().start()
+    for step in range(1, group // 2):
+        layer_sum.to_cross(step).start()
 
     def slices(source, target, sends, arrivals, step):
         peer = lax.rem(fsdp + step, group)
@@ -946,16 +1079,19 @@
         copy.wait()
 
     def tick(ring, at):
-        @pl.when(at < ring.ticks)
+        @pl.when(jnp.logical_and(at >= 0, at < ring.ticks))
         def _():
-            ring.tick(jnp.minimum(at, ring.ticks - 1))
+            ring.tick(jnp.clip(at, 0, ring.ticks - 1))
+
+    late = steps.levels // 2 + 1
 
     def pump(at):
+        lag = (0, 0, 0, 0, late, late)
         for turn, ring in enumerate(first_rings):
 
             @pl.when(lax.rem(at, len(first_rings)) == turn)
             def _():
-                tick(ring, lax.div(at, len(first_rings)))
+                tick(ring, lax.div(at, len(first_rings)) - lag[turn])
 
     def back(unit, first, blocks, diagonal):
         kv = kv_ref[pl.ds(first, blocks), unit].reshape(blocks * keys, deep)
@@ -1030,6 +1166,42 @@
                 kv_ref[2 * pair + steps.side] = final_ref[...].astype(kv_ref.dtype)
                 down_chain(pair).start()
 
+    row_blocks = own // 16
+
+    def weight_grad(left, right, begin, end, target, first, loop):
+        span = LANES * next(n for n in (3, 2, 1) if (end - begin) % (n * LANES) == 0)
+
+        def body(at):
+            columns = pl.ds(pl.multiple_of(begin + at * span, LANES), span)
+            part = forward_dot(
+                left[...], right[:, :, columns].reshape(group * rows, span)
+            ).astype(jnp.bfloat16)
+            for block in range(span // LANES):
+                here = first + (at * (span // LANES) + block) * row_blocks
+                target[pl.ds(here, row_blocks)] = part[
+                    :, block * LANES : (block + 1) * LANES
+                ].reshape(row_blocks, 16, LANES)
+
+        loop((end - begin) // span, body)
+        return first + (end - begin) // LANES * row_blocks
+
+    def clear_from(target, first):
+        for spare in range(first, target.shape[0]):
+            target[spare] = jnp.zeros((16, LANES), jnp.bfloat16)
+
+    def out_grad():
+        for copy in turned[: group - 1]:
+            copy.wait_recv()
+        branch_gather.forward()
+        branch_gather.sibling_here()
+        for step in range(1, branch_gather.chips):
+            branch_gather.crossed(step)
+        split = out_split(width)
+        clear_from(out_a_work, weight_grad(low_all, branch_all, 0, split, out_a_work, 0, tiles))
+        clear_from(out_b_work, weight_grad(low_all, branch_all, split, width, out_b_work, 0, tiles))
+        out_a.start()
+        out_b.start()
+
     turns = units // 2
 
     def slot(pair):
@@ -1058,6 +1230,10 @@
             across(pair).start()
 
         combine(pair)
+
+        @pl.when(pair == late - 1)
+        def _():
+            out_grad()
 
     tiles(steps.levels, slot)
     pumped = [steps.levels * turns]
@@ -1118,9 +1294,20 @@
                     jnp.concatenate(parts, axis=0).astype(jnp.bfloat16).T
                 )
     pair_gather.start(pair_all.at[fsdp])
-    branch_gather.forward()
     pump_next(2)
     query_gather.forward()
+    for step in range(1, layer_sum.chips):
+        ours = layer_part_ref.at[2 * lax.rem(layer_sum.chip + layer_sum.chips - step, layer_sum.chips) + layer_sum.core]
+        for source, target in ((ours, far_ref.at[step - 1]), (layer_cross.at[step - 1], layer_stage)):
+            if source is not ours:
+                layer_sum.to_cross(step).wait_recv()
+            copy = pltpu.make_async_copy(source, target, stage_sems.at[0])
+            copy.start()
+            copy.wait()
+        far_ref[step - 1] = (
+            far_ref[step - 1].astype(jnp.float32) + layer_stage[...].astype(jnp.float32)
+        ).astype(jnp.bfloat16)
+        layer_sum.to_far(step).start()
 
     step_out = width_tile(width)
 
@@ -1164,46 +1351,20 @@
     for step in range(1, group):
         gain_copy(step).start()
     pump_next()
-    for copy in turned:
+    for copy in turned[group - 1 :]:
         copy.wait_recv()
-    for gather in (branch_gather, query_gather):
-        gather.sibling_here()
-        for step in range(1, gather.chips):
-            gather.crossed(step)
-    row_blocks = own // 16
-
-    def weight_grad(left, right, begin, end, target, first):
-        span = LANES * next(n for n in (3, 2, 1) if (end - begin) % (n * LANES) == 0)
-
-        def body(at):
-            columns = pl.ds(pl.multiple_of(begin + at * span, LANES), span)
-            part = forward_dot(
-                left[...], right[:, :, columns].reshape(group * rows, span)
-            ).astype(jnp.bfloat16)
-            for block in range(span // LANES):
-                here = first + (at * (span // LANES) + block) * row_blocks
-                target[pl.ds(here, row_blocks)] = part[
-                    :, block * LANES : (block + 1) * LANES
-                ].reshape(row_blocks, 16, LANES)
-
-        pumping((end - begin) // span, body)
-        return first + (end - begin) // LANES * row_blocks
-
-    def clear_from(target, first):
-        for spare in range(first, target.shape[0]):
-            target[spare] = jnp.zeros((16, LANES), jnp.bfloat16)
-
-    clear_from(out_work, weight_grad(low_all, branch_all, 0, width, out_work, 0))
-    out_ring.start()
+    query_gather.sibling_here()
+    for step in range(1, query_gather.chips):
+        query_gather.crossed(step)
     split = query_split(width)
-    filled_a = weight_grad(normed_all, query_all, 0, split, rest_a_work, 0)
-    filled_b = weight_grad(normed_all, query_all, split, width, rest_b_work, 0)
+    filled_a = weight_grad(normed_all, query_all, 0, split, rest_a_work, 0, pumping)
+    filled_b = weight_grad(normed_all, query_all, split, width, rest_b_work, 0, pumping)
     pair_gather.forward()
     pump_next()
     pair_gather.sibling_here()
     for step in range(1, pair_gather.chips):
         pair_gather.crossed(step)
-    filled_b = weight_grad(normed_all, pair_all, 0, 2 * kv_width, rest_b_work, filled_b)
+    filled_b = weight_grad(normed_all, pair_all, 0, 2 * kv_width, rest_b_work, filled_b, pumping)
     gains = gain_give[...]
     for step in range(1, group):
         gain_copy(step).wait_recv()
@@ -1218,19 +1379,31 @@
     rest_b.start()
     begun = pumped[0]
     half = len(first_rings) // 2
-    total_pumps = gate_ring.ticks * len(first_rings)
+    total_pumps = max(gate_ring.ticks, late + out_a.ticks) * len(first_rings)
 
     def last_ticks(at, unused):
         for turn in range(half):
             pump(jnp.minimum(begun + half * at + turn, total_pumps))
-        tick(out_ring, at)
         tick(rest_a, at)
         tick(rest_b, at)
         return unused
 
-    rounds = max(out_ring.ticks, -(-(total_pumps - begun) // half))
+    rounds = max(rest_a.ticks, -(-(total_pumps - begun) // half))
     lax.fori_loop(0, rounds, last_ticks, 0)
-    for ring in first_rings + (out_ring, rest_a, rest_b):
+    layer_sum.to_sibling().wait_recv()
+    layer = layer_base_ref[...]
+    arrived = [layer_sib]
+    for step in range(1, layer_sum.chips):
+        layer_sum.to_far(step).wait_recv()
+        arrived.append(layer_far.at[step - 1])
+    for source in arrived:
+        copy = pltpu.make_async_copy(source, layer_stage, stage_sems.at[0])
+        copy.start()
+        copy.wait()
+        layer = layer + layer_stage[...].astype(jnp.float32)
+    layer_ref[...] = layer.astype(jnp.bfloat16)
+    layer_sum.sent()
+    for ring in first_rings + (rest_a, rest_b):
         ring.finish()
     for copy in turned:
         copy.wait_send()
@@ -1251,19 +1424,10 @@
     tiles(steps.level + 1, sent)
 
 
-def query_split(width):
-    return width // LANES * 7 // 9 * LANES
-
-
-def down_split(blocks, count):
-    each = -(-blocks // count)
-    first = max(1, each // 3)
-    return first, max(1, each - first)
-
-
 def layer_back(
-    q_wide, g_wide, all_pairs, mix, log_total, gate_part, up_part, down_part, gain_grad, branch,
-    low_t, normed_t, w_query, w_key, w_value, x, gain, resid_grad, cosine, sine,
+    q_wide, g_wide, all_pairs, mix, log_total, gate_part, up_part, down_a, down_b, layer_base,
+    layer_parts, gain_grad, branch, low_t, normed_t, w_query, w_key, w_value, x, gain, resid_grad,
+    cosine, sine,
 ):
     group, count = lax.axis_size("fsdp"), lax.axis_size("ctx")
     units, deep, wide = q_wide.shape
@@ -1273,13 +1437,15 @@
     bf16, f32 = jnp.bfloat16, jnp.float32
     dma = pltpu.SemaphoreType.DMA
     wide_chunk = (group, gate_part.shape[1] // count, 16, LANES)
-    down_chunks = [(per,) + down_part.shape[1:] for per in down_split(down_part.shape[0], count)]
     gain_rows = spread(2 * (width // LANES), 16)
     split, row_blocks = query_split(width), own // 16
-    out_chunk, a_chunk, b_chunk = [
+    out_first = out_split(width)
+    chips = group // 2
+    out_a_chunk, out_b_chunk, a_chunk, b_chunk = [
         (spread(held, count) // count, 16, LANES)
         for held in (
-            width // LANES * row_blocks,
+            out_first // LANES * row_blocks,
+            (width - out_first) // LANES * row_blocks,
             split // LANES * row_blocks + gain_rows // 16,
             (width - split + 2 * kv_width) // LANES * row_blocks,
         )
@@ -1289,17 +1455,22 @@
         back_kernel,
         out_shape=[
             jax.ShapeDtypeStruct((rows, width), f32),
+            jax.ShapeDtypeStruct((rows, width), bf16),
             ring_total(wide_chunk, True),
             ring_total(wide_chunk, True),
-            ring_total(down_chunks[0]),
-            ring_total(down_chunks[1]),
-            ring_total(out_chunk),
+            ring_total(down_a.shape),
+            ring_total(down_b.shape),
+            ring_total(out_a_chunk),
+            ring_total(out_b_chunk),
             ring_total(a_chunk),
             ring_total(b_chunk),
             *[jax.ShapeDtypeStruct((levels, units, keys, deep), bf16)] * 2,
+            jax.ShapeDtypeStruct((rows, width), bf16),
+            *[jax.ShapeDtypeStruct((chips - 1, rows, width), bf16)] * 2,
         ],
-        in_specs=[VMEM, VMEM, ANY, VMEM, VMEM, ANY, ANY, ANY, VMEM, ANY, ANY, ANY] + [VMEM] * 8,
-        out_specs=[VMEM] * 8 + [ANY] * 2,
+        in_specs=[VMEM, VMEM, ANY, VMEM, VMEM, ANY, ANY, ANY, ANY, VMEM, ANY, VMEM, ANY, ANY, ANY]
+        + [VMEM] * 8,
+        out_specs=[VMEM] * 10 + [ANY] * 5,
         scratch_shapes=[
             pltpu.VMEM(all_pairs.shape, bf16),
             pltpu.VMEM((2, units, keys, deep), bf16),
@@ -1309,9 +1480,8 @@
             pltpu.VMEM((units, HD, wide), f32),
             *ring_scratch(wide_chunk, True),
             *ring_scratch(wide_chunk, True),
-            *ring_scratch(down_chunks[0]),
-            *ring_scratch(down_chunks[1]),
-            *ring_scratch(out_chunk),
+            *ring_scratch(out_a_chunk),
+            *ring_scratch(out_b_chunk),
             *ring_scratch(a_chunk),
             *ring_scratch(b_chunk),
             pltpu.VMEM((own, group * rows), bf16),
@@ -1322,9 +1492,13 @@
             pltpu.VMEM((rows, width), f32),
             pltpu.VMEM((gain_rows, LANES), f32),
             pltpu.VMEM((group - 1, gain_rows, LANES), f32),
+            pltpu.VMEM((chips - 1, rows, width), bf16),
+            pltpu.VMEM((rows, width), bf16),
             *ring_semaphores(True),
             *ring_semaphores(True),
-            *[kind for _ in range(5) for kind in ring_semaphores()],
+            *[kind for _ in range(4) for kind in ring_semaphores()],
+            *[dma((group - 1,))] * 2,
+            *[kind for _ in range(2) for kind in ring_semaphores()],
             *[dma((levels,))] * 4,
             *[group_semaphores()] * 6,
             *[dma((group - 1,))] * 6,
@@ -1335,8 +1509,9 @@
             collective_id=3, has_side_effects=True, vmem_limit_bytes=62 << 20
         ),
     )(
-        q_wide, g_wide, all_pairs, mix, log_total, gate_part, up_part, down_part, gain_grad, branch,
-        low_t, normed_t, w_query, w_key, w_value, x, gain, resid_grad, cosine, sine,
+        q_wide, g_wide, all_pairs, mix, log_total, gate_part, up_part, down_a, down_b, layer_base,
+        layer_parts, gain_grad, branch, low_t, normed_t, w_query, w_key, w_value, x, gain, resid_grad,
+        cosine, sine,
     )
 
 
@@ -1349,7 +1524,7 @@
 
 
 def finish_kernel(
-    gate_ref, up_ref, down_a_ref, down_b_ref, out_ref, rest_a_ref, rest_b_ref,
+    gate_ref, up_ref, down_a_ref, down_b_ref, out_a_ref, out_b_ref, rest_a_ref, rest_b_ref,
     query_grad, key_grad, value_grad, out_grad, gate_grad, up_grad, down_grad,
 ):
     rows = gate_grad.shape[0]
@@ -1375,7 +1550,9 @@
 
         width, kv_width = query_grad.shape[1], key_grad.shape[1]
         split = query_split(width) // LANES
-        unpack(out_ref, 0, out_grad, 0, width // LANES)
+        middle = out_split(width) // LANES
+        unpack(out_a_ref, 0, out_grad, 0, middle)
+        unpack(out_b_ref, 0, out_grad, middle, width // LANES)
         unpack(rest_a_ref, 0, query_grad, 0, split)
         at = unpack(rest_b_ref, 0, query_grad, split, width // LANES)
         at = unpack(rest_b_ref, at, key_grad, 0, kv_width // LANES)
@@ -1391,7 +1568,7 @@
                 )
 
 
-def finish(gate, up, down_a, down_b, out, rest_a, rest_b, own, width, kv_width, hidden):
+def finish(gate, up, down_a, down_b, out_a, out_b, rest_a, rest_b, own, width, kv_width, hidden):
     count, group, n = gate.shape[:3]
 
     def whole(array):
@@ -1407,10 +1584,10 @@
         finish_kernel,
         grid=(group,),
         out_shape=outs,
-        in_specs=[wide, wide] + [whole(a) for a in (down_a, down_b, out, rest_a, rest_b)],
+        in_specs=[wide, wide] + [whole(a) for a in (down_a, down_b, out_a, out_b, rest_a, rest_b)],
         out_specs=[whole(a) for a in outs[:4]] + [slice_spec, slice_spec, whole(outs[6])],
         compiler_params=pltpu.CompilerParams(vmem_limit_bytes=60 << 20),
-    )(gate, up, down_a, down_b, out, rest_a, rest_b)
+    )(gate, up, down_a, down_b, out_a, out_b, rest_a, rest_b)
 
 
 def on_device(
@@ -1455,7 +1632,10 @@
     (attn_low, low_t, mix_unit, log_total, all_pairs, full_out, my_gate, my_up, all_g) = attend(
         q_wide, pairs, w_out, w_gate, w_up, g_rows
     )
-    layer_out, grad_resid, grad_branch, g_wide, gate_part, up_part, down_part, gain_term_ffn = (
+    (
+        layer_base, layer_parts, grad_resid, grad_branch, g_wide, gate_part, up_part, down_a, down_b,
+        gain_term_ffn,
+    ) = (
         feed_forward(
             x_rows,
             attn_low,
@@ -1469,13 +1649,12 @@
             wide,
         )
     )
-    count = lax.axis_size("ctx")
-    down_blocks = down_part.reshape(-1, 16, width)
-    spare = count * sum(down_split(down_blocks.shape[0], count)) - down_blocks.shape[0]
-    down_blocks = jnp.pad(down_blocks, ((0, spare), (0, 0), (0, 0)))
     freqs = ROTARY_BASE ** (-2.0 * jnp.arange(HD // 2, dtype=jnp.float32) / HD)
     angles = freqs[:, None] * positions.astype(jnp.float32)[None, :]
-    grad_tokens, gate_total, up_total, down_a, down_b, out_sum, rest_a, rest_b, _, _ = layer_back(
+    (
+        grad_tokens, layer_out, gate_total, up_total, down_a, down_b, out_a, out_b, rest_a, rest_b,
+        *_,
+    ) = layer_back(
         q_wide,
         g_wide,
         all_pairs,
@@ -1483,7 +1662,10 @@
         log_total,
         gate_part,
         up_part,
-        down_blocks,
+        down_a,
+        down_b,
+        layer_base,
+        layer_parts,
         gain_term_ffn,
         grad_branch,
         low_t,
@@ -1503,7 +1685,7 @@
     gains = lax.dynamic_slice_in_dim(gains, lax.axis_index("fsdp") * own, own, 1)
     gains = gains.astype(jnp.float32)
     grads = finish(
-        gate_total, up_total, down_a, down_b, out_sum, rest_a, rest_b,
+        gate_total, up_total, down_a, down_b, out_a, out_b, rest_a, rest_b,
         own, width, kv_width, w_down.shape[0],
     )
     return (

time: 434 us -> 424 us (0.977)
  Pallas kernels: 358 us -> 349 us
    pallas_call x1, Pallas kernels: 214 us -> 194 us  [layer_back(): pl.pallas_call(back_kernel, out_shape=[jax.ShapeDtypeStruct((rows, width)...]
    pallas_call x1, Pallas kernels: 62.9 us -> 74.8 us  [feed_forward(): pl.pallas_call(ffn_kernel, out_shape=[jax.ShapeDtypeStruct((rows, width),...]
where the time goes in v7:
time: 424 us
  Pallas kernels  349 us (82%)
  blocking collectives  31.7 us (7%)
  local copies, waits for them, and re-layouts  22.2 us (5%)
  between operations  15 us (4%)
    pallas_call x1, Pallas kernels, layer_back(): pl.pallas_call(back_kernel, out_shape=[jax.ShapeDtypeStruct((rows, width)...  194 us
    pallas_call x1, Pallas kernels, feed_forward(): pl.pallas_call(ffn_kernel, out_shape=[jax.ShapeDtypeStruct((rows, width),...  74.8 us
    pallas_call x1, Pallas kernels, attend(): pl.pallas_call(attend_kernel, out_shape=[jax.ShapeDtypeStruct((sequences...  71.8 us
    all_gather x2, blocking collectives, on_device(): lax.all_gather(weight, 'fsdp', axis=0, tiled=True)  23.2 us
    pallas_call x1, Pallas kernels, finish(): pl.pallas_call(finish_kernel, grid=(group,), out_shape=outs, in_specs=[wi...  9.22 us
    unnamed x1, blocking collectives  8.51 us
  transfers between devices with their start and end apart: 1, of which 0 were waited for; matrix products, arithmetic and copies ran while one was open for 3% of the time, Pallas kernels for 0%

profile of v7, /device:TPU:0, one launch (start us, length us, event | category | flops | bytes accessed | tf_op | source)
XLA Modules:
  0.0 423.5 jit_solution(68069612303892082)
XLA Ops:
  7.2 0.7 all-gather.2.cloned.1.call-update
  7.9 1.2 dynamic-slice
  9.8 0.9 dynamic-update-slice
  10.7 0.9 dynamic-update-slice.1
  11.6 8.5 %all-reduce.3 = (bf16[1152]{0:T(1024)(128)(2,1)S(1)}, bf16[1152]{0:T(1024)(128)(2,1)S(1)}) all-reduce(bf16[1152]{0:T(1024)(128)(2,1)S(1)} %dynamic-update-slice, bf16[1152]{0:T(1024)(128)(2,1)S(1)} %dynamic-update-slice.1), channel_id=1, replica_groups=mesh['fsdp'=4,'ctx'=8] {'fsdp'}, use_global_device_ids=true, to_apply=%add.1 | all-reduce | flops 2304 | bytes 9216
  21.3 1.1 copy.65
  22.9 1.1 copy.76.normed_t_ref
  24.0 0.9 copy.75
  24.8 14.0 %all_gather.18.w_value_ref = bf16[1152,384]{1,0:T(8,128)(2,1)S(1)} all-gather(bf16[288,384]{1,0:T(8,128)(2,1)S(1)} %copy-done.7), channel_id=1, replica_groups=mesh['fsdp'=4,'ctx'=8] {'fsdp'}, dimensions={0}, use_global_device_ids=true | all-gather | bytes 1105920 | tf_op jit(solution)/shard_map/all_gather | solution.py:1600
  40.0 9.2 %all_gather.17.w_key_ref = bf16[1152,384]{1,0:T(8,128)(2,1)S(1)} all-gather(bf16[288,384]{1,0:T(8,128)(2,1)S(1)} %copy-done.8), channel_id=1, replica_groups=mesh['fsdp'=4,'ctx'=8] {'fsdp'}, dimensions={0}, use_global_device_ids=true | all-gather | bytes 1105920 | tf_op jit(solution)/shard_map/all_gather | solution.py:1600
  49.2 0.9 copy.70
  51.7 1.0 copy.74
  52.7 0.8 multiply_sine_fusion
  53.5 4.2 copy.68
  57.7 1.1 fusion.6
  60.1 1.2 concatenate.14.q_ref
  61.3 71.8 %shard_map.194 = (bf16[256,1152]{1,0:T(8,128)(2,1)}, bf16[1152,256]{1,0:T(8,128)(2,1)}, f32[12,64,384]{2,1,0:T(8,128)}, f32[12,1,384]{2,1,0:T(1,128)}, bf16[8,12...) custom-call(bf16[12,128,384]{2,1,0:T(8,128)(2,1)} %concatenate.14.q_, ...), custom_call_target="tpu_custom_call" | custom-call | tf_op jit(solution)/shard_map/pallas_call | solution.py:359
  133.1 74.8 %shard_map.195 = (f32[256,1152]{1,0:T(8,128)}, bf16[4,256,1152]{2,1,0:T(8,128)(2,1)}, f32[256,1152]{1,0:T(8,128)}, bf16[256,1152]{1,0:T(8,128)(2,1)}, bf16[12,12...) custom-call(bf16[256,1152]{1,0:T(8,128)(2,1)} %bitcast.52, ...), custom_call_target="tpu_custom_call" | custom-call | tf_op jit(solution)/shard_map/pallas_call | solution.py:924
  208.0 193.5 %shard_map.196 = (f32[256,1152]{1,0:T(8,128)}, bf16[256,1152]{1,0:T(8,128)(2,1)}, bf16[8,4,14,16,128]{4,3,2,1,0:T(8,128)(2,1)}, bf16[8,4,14,16,128]{4,3,2,1,0:T(...) custom-call(bf16[12,128,384]{2,1,0:T(8,128)(2,1)} %concatenate.14.q_, ...), custom_call_target="tpu_custom_call" | custom-call | tf_op jit(solution)/shard_map/pallas_call | solution.py:1454
  401.5 2.6 copy.95
  404.1 1.9 copy.93
  406.0 0.7 slice.28
  406.8 0.6 slice_reduce_fusion
  407.4 9.2 %shard_map.197 = (f32[288,1152]{1,0:T(8,128)}, f32[288,384]{1,0:T(8,128)}, f32[288,384]{1,0:T(8,128)}, f32[288,1152]{1,0:T(8,128)}, f32[288,3072]{1,0:T(8,128)},...) custom-call(bf16[8,4,14,16,128]{4,3,2,1,0:T(8,128)(2,1)} %get-tuple-element.68.gate_ref, ...), custom_call_target="tpu_custom_call" | custom-call | tf_op jit(solution)/shard_map/pallas_call | solution.py:1583
  (46 shorter events, 5.8 us)
Async XLA Ops:
  7.2 15.3 %copy-start.3 = (bf16[128,2,1152]{2,1,0:T(2,128)(2,1)S(1)}, bf16[128,2,1152]{2,1,0:T(2,128)(2,1)}, u32[]{:S(2)}) copy-start(bf16[128,2,1152]{2,1,0:T(2,128)(2,1)} %param.11) | copy-start | bytes 1769476
  7.2 46.3 %all-gather.2.cloned.1.call-start = ((), (), s32[]{:S(2)}) async-start(), calls=%async_computation | async-start | bytes 3317760 | tf_op jit(solution)/shard_map/all_gather | solution.py:1600
  22.4 16.4 %copy-start = (bf16[128,2,1152]{2,0,1:T(8,128)(2,1)}, bf16[128,2,1152]{2,0,1:T(8,128)(2,1)S(1)}, u32[]{:S(2)}) copy-start(bf16[128,2,1152]{2,0,1:T(8,128)(2,1)S(1)} %copy.65) | copy-start | bytes 1769476
  22.7 1.3 copy-start.6
  22.9 2.0 copy-start.7
  38.8 0.9 copy-start.2
  38.8 1.2 copy-start.8
  49.2 1.6 copy-start.1
  53.5 4.2 copy-start.4
  401.5 2.6 copy-start.5
Sparse Core Ops, SparseCore 0:
  9.6 33.3 all-gather.1

commit v8 on v7

--- a/solution.py
+++ b/solution.py
@@ -14,19 +14,6 @@
 EPSILON = 1e-05
 ROTARY_BASE = 10000.0
 MASKED_SCORE = -1e30
-
-
-def rotary(values, positions, direction):
-    half = values.shape[-1] // 2
-    freqs = ROTARY_BASE ** (-2.0 * jnp.arange(half, dtype=jnp.float32) / values.shape[-1])
-    angles = positions.astype(jnp.float32)[:, None] * freqs[None, :]
-    cosine = jnp.cos(angles)[:, None, :]
-    sine = direction * jnp.sin(angles)[:, None, :]
-    first = values[..., :half]
-    second = values[..., half:]
-    return jnp.concatenate(
-        [first * cosine - second * sine, second * cosine + first * sine], axis=-1
-    )
 
 
 def norm_scale(rows):
@@ -116,6 +103,109 @@
         for step in range(1, self.chips):
             self.crossed(step)
         self.sent()
+
+
+class HalfGather:
+    def __init__(self, held, own_rows, sends, arrivals):
+        self.held, self.own = held, own_rows
+        self.sends, self.arrivals = sends, arrivals
+        self.fsdp, self.ctx = lax.axis_index("fsdp"), lax.axis_index("ctx")
+        self.chips = lax.axis_size("fsdp") // 2
+        self.chip, self.core = lax.div(self.fsdp, 2), lax.rem(self.fsdp, 2)
+        self.sibling = 2 * self.chip + 1 - self.core
+        self.side = lax.rem(self.ctx, 2)
+        self.pair = self.ctx + 1 - 2 * self.side
+        first = -(-own_rows // 32) * 16
+        self.halves = ((0, first), (first, own_rows - first))
+
+    def same_core(self, step):
+        return 2 * lax.rem(self.chip + step, self.chips) + self.core
+
+    def rows(self, shard, half=None):
+        begin, size = (0, self.own) if half is None else self.halves[half]
+        return self.held.at[pl.ds(shard * self.own + begin, size)]
+
+    def copy(self, source, target, semaphore, device):
+        return pltpu.make_async_remote_copy(
+            src_ref=source,
+            dst_ref=target,
+            send_sem=self.sends.at[semaphore],
+            recv_sem=self.arrivals.at[semaphore],
+            device_id=device,
+            device_id_type=MESH,
+        )
+
+    def on_side(self, body):
+        for half in range(2):
+
+            @pl.when(self.side == half)
+            def _(half=half):
+                body(half)
+
+    def across(self, source):
+        return self.copy(source, self.rows(self.fsdp), 0, (self.sibling, self.ctx))
+
+    def out(self, source, step, half):
+        begin, size = self.halves[half]
+        return self.copy(
+            source.at[pl.ds(begin, size)],
+            self.rows(self.fsdp, half),
+            step,
+            (self.same_core(step), self.ctx),
+        )
+
+    def to_pair(self, step, half):
+        part = self.rows(self.same_core(self.chips - step), half)
+        return self.copy(part, part, self.chips - 1 + step, (self.fsdp, self.pair))
+
+    def onward(self, step):
+        part = self.rows(self.same_core(self.chips - step))
+        return self.copy(part, part, 2 * self.chips - 2 + step, (self.sibling, self.ctx))
+
+    def start(self, source):
+        def send(half):
+            for step in range(1, self.chips):
+                self.out(source, step, half).start()
+
+        self.on_side(send)
+        self.across(source).start()
+
+    def to_pairs(self):
+        def forward(half):
+            for step in range(1, self.chips):
+                self.out(self.rows(self.fsdp), step, half).wait_recv()
+                self.to_pair(step, half).start()
+
+        self.on_side(forward)
+
+    def to_sibling(self):
+        def forward(half):
+            for step in range(1, self.chips):
+                self.to_pair(step, 1 - half).wait_recv()
+
+        self.on_side(forward)
+        for step in range(1, self.chips):
+            self.onward(step).start()
+
+    def arrived(self):
+        self.across(self.rows(self.fsdp)).wait_recv()
+        for step in range(1, self.chips):
+            self.onward(step).wait_recv()
+
+    def sent(self):
+        def wait(half):
+            for step in range(1, self.chips):
+                self.out(self.rows(self.fsdp), step, half).wait_send()
+                self.to_pair(step, half).wait_send()
+
+        self.on_side(wait)
+        self.across(self.rows(self.fsdp)).wait_send()
+        for step in range(1, self.chips):
+            self.onward(step).wait_send()
+
+
+def half_semaphores(many):
+    return pltpu.SemaphoreType.DMA((many, 3 * (lax.axis_size("fsdp") // 2) - 2))
 
 
 def group_semaphores():
@@ -165,20 +255,76 @@
 
 
 def attend_kernel(
-    q_ref, kv_ref, out_ref, gate_ref, up_ref, g_ref,
+    x_ref, gain_ref, cos_ref, sin_ref, query_ref, key_ref, value_ref, out_ref, gate_ref, up_ref, g_ref,
+    q_ref, normed_t_ref, gains_ref, full_query, full_key, full_value,
     low_ref, low_t_ref, mix_ref, log_ref, all_ref, full_out_ref, my_gate_ref, my_up_ref, all_g_ref,
+    normed_ref, key_rows, gain_all,
     top_ref, total_ref, chain_sends, chain_arrivals, peer_sends, peer_arrivals,
+    half_sends, half_arrivals, gain_sends, gain_arrivals,
     out_sends, out_arrivals, g_sends, g_arrivals, part_sends, part_arrivals, local_sems,
 ):
     steps = Steps()
     fsdp, ctx, group = steps.fsdp, steps.ctx, lax.axis_size("fsdp")
     units, deep, wide = q_ref.shape
-    keys = kv_ref.shape[1]
+    keys = all_ref.shape[2]
     per_part = units // PARTS
+    rows_count, width = x_ref.shape
+    own = query_ref.shape[0]
+    sequences, groups = units // KVH, H // KVH
     barrier = pltpu.get_barrier_semaphore()
     greeted = steps.greet(barrier) + greet_group(barrier)
-    all_ref[ctx] = kv_ref[...]
+    span = KVH * HD
+    pieces = [(key_ref, full_key, 0), (value_ref, full_value, 0)]
+    pieces += [(query_ref, full_query, start) for start in range(0, width, span)]
+    gathers = []
+    for at, (source, target, start) in enumerate(pieces):
+        columns = pl.ds(start, span)
+        gather = HalfGather(
+            target.at[:, columns], own, half_sends.at[at], half_arrivals.at[at]
+        )
+        gathers.append((gather, source.at[:, columns]))
+    own_rows = pl.ds(fsdp * own, own)
+    own_copies = [
+        pltpu.make_async_copy(source, target.at[own_rows], local_sems.at[4 + at])
+        for at, (source, target) in enumerate(
+            ((key_ref, full_key), (value_ref, full_value), (query_ref, full_query))
+        )
+    ]
+    for copy in own_copies:
+        copy.start()
+    gain_all[fsdp] = gain_ref[...]
     pl.semaphore_wait(barrier, greeted)
+
+    def gain_copy(step):
+        peer = lax.rem(fsdp + step, group)
+        return pltpu.make_async_remote_copy(
+            src_ref=gain_ref,
+            dst_ref=gain_all.at[fsdp],
+            send_sem=gain_sends.at[step - 1],
+            recv_sem=gain_arrivals.at[step - 1],
+            device_id=(peer, ctx),
+            device_id_type=MESH,
+        )
+
+    for step in range(1, group):
+        gain_copy(step).start()
+    for gather, source in gathers:
+        gather.start(source)
+    inputs = x_ref[...].astype(jnp.float32)
+    scale = norm_scale(inputs)
+    q_ref[:, HD:, :] = jnp.zeros((units, HD, wide), q_ref.dtype)
+    for step in range(1, group):
+        gain_copy(step).wait_recv()
+    gains = jnp.concatenate([gain_all[shard][:, :own] for shard in range(group)], axis=1)
+    gains_ref[...] = gains
+    normed_ref[...] = (inputs * scale * gains[:1]).astype(jnp.bfloat16)
+    cosine, sine = cos_ref[...], sin_ref[...]
+
+    def turn(columns):
+        first, second = columns[: HD // 2], columns[HD // 2 :]
+        return jnp.concatenate(
+            [first * cosine - second * sine, second * cosine + first * sine], axis=0
+        ).astype(jnp.bfloat16)
 
     def block_copy(level, part, side, semaphores, arrivals, arrives, device):
         block = 2 * (steps.level - level) + side
@@ -207,17 +353,60 @@
         def _():
             chain(level, part).start()
 
-    for part in range(PARTS):
-        pass_on(0, part)
-
-        @pl.when(steps.side == 0)
-        def _():
-            across(0, part).start()
-
-    rows = out_ref.shape[0]
+    def project(at):
+        _, weight, start = pieces[at]
+        made = forward_dot(normed_ref[...], weight[:, start : start + span])
+        if at == 0:
+            key_rows[...] = made
+            return
+        for sequence in range(sequences):
+            block = slice(sequence * keys, (sequence + 1) * keys)
+            for pair in range(span // (2 * HD)):
+                columns = slice(pair * 2 * HD, (pair + 1) * 2 * HD)
+                turned = made[block, columns].T
+                if at == 1:
+                    turned_keys = key_rows[block, columns].T
+                    for half in range(2):
+                        held = slice(half * HD, (half + 1) * HD)
+                        both = jnp.concatenate(
+                            [turn(turned_keys[held]), turned[held].astype(jnp.bfloat16)], axis=0
+                        )
+                        all_ref[ctx, sequence * KVH + 2 * pair + half] = both.T
+                else:
+                    for half in range(2):
+                        head = start // HD + 2 * pair + half
+                        unit, member = sequence * KVH + head // groups, head % groups
+                        part = turn(turned[half * HD : (half + 1) * HD])
+                        q_ref[unit, :HD, member * keys : (member + 1) * keys] = part * jnp.bfloat16(
+                            HD ** (-0.5)
+                        )
+        if at == 1:
+            for part in range(PARTS):
+                pass_on(0, part)
+
+                @pl.when(steps.side == 0)
+                def _():
+                    across(0, part).start()
+
+    last = len(pieces)
+    for at in range(last + 2):
+        if at < last:
+            gathers[at][0].to_pairs()
+        if 1 <= at <= last:
+            gathers[at - 1][0].to_sibling()
+        if at == 1:
+            for column in range(width // LANES):
+                columns = slice(column * LANES, (column + 1) * LANES)
+                normed_t_ref[columns, :] = normed_ref[:, columns].T
+            for copy in own_copies:
+                copy.wait()
+        if at >= 2:
+            gathers[at - 2][0].arrived()
+            project(at - 2)
+
     columns = my_gate_ref.shape[1]
     gathered = GroupGather(
-        lambda shard: full_out_ref.at[pl.ds(shard * rows, rows)], out_sends, out_arrivals
+        lambda shard: full_out_ref.at[pl.ds(shard * own, own)], out_sends, out_arrivals
     )
     gathered.start(out_ref)
     gathered_g = GroupGather(lambda shard: all_g_ref.at[shard], g_sends, g_arrivals)
@@ -225,7 +414,6 @@
     own_g = pltpu.make_async_copy(g_ref, all_g_ref.at[fsdp], local_sems.at[3])
     own_g.start()
     background = [own_g]
-    own_rows = pl.ds(fsdp * rows, rows)
     own_out = pltpu.make_async_copy(out_ref, full_out_ref.at[own_rows], local_sems.at[2])
     own_out.start()
     background.append(own_out)
@@ -242,13 +430,13 @@
             )
             copy.start()
             background.append(copy)
-        own = pltpu.make_async_copy(
+        own_part = pltpu.make_async_copy(
             source.at[:, pl.ds(pl.multiple_of(fsdp * columns, LANES), columns)],
             target.at[own_rows],
             local_sems.at[which],
         )
-        own.start()
-        background.append(own)
+        own_part.start()
+        background.append(own_part)
 
     def add(unit, kv):
         scores = jnp.dot(kv, q_ref[unit], preferred_element_type=jnp.float32)
@@ -270,7 +458,7 @@
         lax.fori_loop(0, count // 2, two, 0)
 
     def diagonal(unit):
-        kv = kv_ref[unit]
+        kv = all_ref[ctx, unit]
         scores = jnp.dot(kv, q_ref[unit], preferred_element_type=jnp.float32)
         scores = jnp.where(causal(keys, wide, scores.shape), scores, MASKED_SCORE)
         top = jnp.max(scores, axis=0, keepdims=True)
@@ -311,18 +499,21 @@
         log_ref[unit] = top_ref[unit] + jnp.log(total)
 
     over_units(close, 0, units)
-    groups = wide // keys
-    for sequence in range(units // KVH):
+    for sequence in range(sequences):
         for pair in range(H // 2):
             heads = []
             for head in (2 * pair, 2 * pair + 1):
                 unit, member = sequence * KVH + head // groups, head % groups
                 heads.append(mix_ref[unit, :, member * keys : (member + 1) * keys])
             tile = jnp.concatenate(heads, axis=0).astype(low_ref.dtype)
-            span = slice(sequence * keys, (sequence + 1) * keys)
+            block = slice(sequence * keys, (sequence + 1) * keys)
             columns = slice(pair * 2 * HD, (pair + 1) * 2 * HD)
-            low_t_ref[columns, span] = tile
-            low_ref[span, columns] = tile.T
+            low_t_ref[columns, block] = tile
+            low_ref[block, columns] = tile.T
+    for gather, _ in gathers:
+        gather.sent()
+    for step in range(1, group):
+        gain_copy(step).wait_send()
     gathered.finish()
     gathered_g.finish()
     for copy in background:
@@ -348,45 +539,59 @@
 VMEM = pl.BlockSpec(memory_space=pltpu.VMEM)
 
 
-def attend(q_wide, pairs, w_out, w_gate, w_up, g_rows):
+def attend(x, gains, cosine, sine, w_query, w_key, w_value, w_out, w_gate, w_up, g_rows, sequences):
     group, count = lax.axis_size("fsdp"), lax.axis_size("ctx")
-    units, deep, wide = q_wide.shape
-    keys = pairs.shape[1]
-    rows, width = w_out.shape
-    hidden = w_gate.shape[1] // group
+    rows, width = x.shape
+    own, hidden = w_query.shape[0], w_gate.shape[1] // group
+    keys, units, deep = rows // sequences, sequences * KVH, 2 * HD
+    wide = H // KVH * keys
+    kv_width = KVH * HD
     dma = pltpu.SemaphoreType.DMA
-    sequences = units // KVH
+    bf16, f32 = jnp.bfloat16, jnp.float32
+    pieces = 2 + width // kv_width
     return pl.pallas_call(
         attend_kernel,
         out_shape=[
-            jax.ShapeDtypeStruct((sequences * keys, width), jnp.bfloat16),
-            jax.ShapeDtypeStruct((width, sequences * keys), jnp.bfloat16),
-            jax.ShapeDtypeStruct((units, HD, wide), jnp.float32),
-            jax.ShapeDtypeStruct((units, 1, wide), jnp.float32),
-            jax.ShapeDtypeStruct((count,) + pairs.shape, jnp.bfloat16),
-            jax.ShapeDtypeStruct((group * rows, width), jnp.bfloat16),
-            jax.ShapeDtypeStruct((group * rows, hidden), jnp.bfloat16),
-            jax.ShapeDtypeStruct((group * rows, hidden), jnp.bfloat16),
-            jax.ShapeDtypeStruct((group,) + g_rows.shape, jnp.bfloat16),
+            jax.ShapeDtypeStruct((units, deep, wide), bf16),
+            jax.ShapeDtypeStruct((width, rows), bf16),
+            jax.ShapeDtypeStruct((gains.shape[0], width), f32),
+            jax.ShapeDtypeStruct((width, width), bf16),
+            jax.ShapeDtypeStruct((width, kv_width), bf16),
+            jax.ShapeDtypeStruct((width, kv_width), bf16),
+            jax.ShapeDtypeStruct((rows, width), bf16),
+            jax.ShapeDtypeStruct((width, rows), bf16),
+            jax.ShapeDtypeStruct((units, HD, wide), f32),
+            jax.ShapeDtypeStruct((units, 1, wide), f32),
+            jax.ShapeDtypeStruct((count, units, keys, deep), bf16),
+            jax.ShapeDtypeStruct((width, width), bf16),
+            jax.ShapeDtypeStruct((width, hidden), bf16),
+            jax.ShapeDtypeStruct((width, hidden), bf16),
+            jax.ShapeDtypeStruct((group, rows, width), bf16),
         ],
-        in_specs=[VMEM, VMEM, ANY, ANY, ANY, ANY],
-        out_specs=[VMEM] * 5 + [ANY] * 4,
+        in_specs=[VMEM] * 4 + [ANY] * 7,
+        out_specs=[VMEM] * 11 + [ANY] * 4,
         scratch_shapes=[
-            pltpu.VMEM((units, 1, wide), jnp.float32),
-            pltpu.VMEM((units, 1, wide), jnp.float32),
+            pltpu.VMEM((rows, width), bf16),
+            pltpu.VMEM((rows, kv_width), f32),
+            pltpu.VMEM((group,) + gains.shape, f32),
+            pltpu.VMEM((units, 1, wide), f32),
+            pltpu.VMEM((units, 1, wide), f32),
             dma((count // 2, PARTS)),
             dma((count // 2 + 1, PARTS)),
             dma((count // 2, PARTS)),
             dma((count // 2, PARTS)),
+            half_semaphores(pieces),
+            half_semaphores(pieces),
+            *[dma((group - 1,))] * 2,
             *[group_semaphores()] * 4,
             dma((2, group - 1)),
             dma((2, group - 1)),
-            dma((4,)),
+            dma((7,)),
         ],
         compiler_params=pltpu.CompilerParams(
-            collective_id=1, has_side_effects=True, vmem_limit_bytes=56 << 20
+            collective_id=1, has_side_effects=True, vmem_limit_bytes=60 << 20
         ),
-    )(q_wide, pairs, w_out, w_gate, w_up, g_rows)
+    )(x, gains, cosine, sine, w_query, w_key, w_value, w_out, w_gate, w_up, g_rows)
 
 
 class Ring:
@@ -1515,14 +1720,6 @@
     )
 
 
-def unit_columns(rows, seq_count, block_len):
-    groups = H // KVH
-    split = rows.reshape(seq_count, block_len, KVH, groups, HD)
-    return jnp.transpose(split, (0, 2, 4, 3, 1)).reshape(
-        seq_count * KVH, HD, groups * block_len
-    )
-
-
 def finish_kernel(
     gate_ref, up_ref, down_a_ref, down_b_ref, out_a_ref, out_b_ref, rest_a_ref, rest_b_ref,
     query_grad, key_grad, value_grad, out_grad, gate_grad, up_grad, down_grad,
@@ -1596,41 +1793,23 @@
     block_len, seq_count, width = tokens.shape
     rows_count = block_len * seq_count
     kv_width = KVH * HD
-    full_query, full_key, full_value = [
-        lax.all_gather(weight, "fsdp", axis=0, tiled=True) for weight in (w_query, w_key, w_value)
-    ]
-    full_gain_attn, full_gain_ffn = [
-        lax.all_gather(gain, "fsdp", axis=0, tiled=True) for gain in (gain_attn, gain_ffn)
-    ]
-    my_down = w_down
-    my_start = lax.axis_index("ctx") * block_len
-    positions = my_start + jnp.arange(block_len, dtype=jnp.int32)
+    positions = lax.axis_index("ctx") * block_len + jnp.arange(block_len, dtype=jnp.int32)
+    freqs = ROTARY_BASE ** (-2.0 * jnp.arange(HD // 2, dtype=jnp.float32) / HD)
+    angles = freqs[:, None] * positions.astype(jnp.float32)[None, :]
+    cosine, sine = jnp.cos(angles), jnp.sin(angles)
     x_rows = jnp.swapaxes(tokens, 0, 1).reshape(rows_count, width)
     g_rows = jnp.swapaxes(cotangent, 0, 1).reshape(rows_count, width)
-    inputs = x_rows.astype(jnp.float32)
-    scale_attn = norm_scale(inputs)
-    normed_attn = (inputs * scale_attn * full_gain_attn.astype(jnp.float32)).astype(jnp.bfloat16)
-    query_raw = forward_dot(normed_attn, full_query)
-    key_raw = forward_dot(normed_attn, full_key)
-    value_raw = forward_dot(normed_attn, full_value)
+    own = gain_attn.shape[0]
     units = seq_count * KVH
     wide = H // KVH * block_len
-    queries = (
-        rotary(query_raw.reshape(seq_count, block_len, H, HD), positions, 1.0)
-        .astype(jnp.bfloat16)
-        .reshape(rows_count, width)
+    own_gains = jnp.pad(
+        jnp.stack([gain_attn, gain_ffn]).astype(jnp.float32), ((0, 6), (0, spread(own, LANES) - own))
     )
-    keys_local = rotary(
-        key_raw.reshape(seq_count, block_len, KVH, HD), positions, 1.0
-    ).astype(jnp.bfloat16)
-    values_local = value_raw.astype(jnp.bfloat16).reshape(seq_count, block_len, KVH, HD)
-    pairs = jnp.swapaxes(
-        jnp.concatenate([keys_local, values_local], axis=-1), 1, 2
-    ).reshape(units, block_len, 2 * HD)
-    q_unit = unit_columns(queries * jnp.bfloat16(HD ** (-0.5)), seq_count, block_len)
-    q_wide = jnp.concatenate([q_unit, jnp.zeros_like(q_unit)], axis=1)
-    (attn_low, low_t, mix_unit, log_total, all_pairs, full_out, my_gate, my_up, all_g) = attend(
-        q_wide, pairs, w_out, w_gate, w_up, g_rows
+    (
+        q_wide, normed_t, gains, full_query, full_key, full_value, attn_low, low_t, mix_unit, log_total,
+        all_pairs, full_out, my_gate, my_up, all_g,
+    ) = attend(
+        x_rows, own_gains, cosine, sine, w_query, w_key, w_value, w_out, w_gate, w_up, g_rows, seq_count
     )
     (
         layer_base, layer_parts, grad_resid, grad_branch, g_wide, gate_part, up_part, down_a, down_b,
@@ -1644,13 +1823,11 @@
             my_up,
             w_down,
             all_g,
-            full_gain_ffn.astype(jnp.float32)[None],
+            gains[1:2],
             units,
             wide,
         )
     )
-    freqs = ROTARY_BASE ** (-2.0 * jnp.arange(HD // 2, dtype=jnp.float32) / HD)
-    angles = freqs[:, None] * positions.astype(jnp.float32)[None, :]
     (
         grad_tokens, layer_out, gate_total, up_total, down_a, down_b, out_a, out_b, rest_a, rest_b,
         *_,
@@ -1669,21 +1846,20 @@
         gain_term_ffn,
         grad_branch,
         low_t,
-        normed_attn.T,
+        normed_t,
         full_query,
         full_key,
         full_value,
         x_rows,
-        full_gain_attn.astype(jnp.float32)[None],
+        gains[:1],
         grad_resid,
-        jnp.cos(angles),
-        jnp.sin(angles),
+        cosine,
+        sine,
     )
-    own = gain_attn.shape[0]
     filled = query_split(width) // LANES * (own // 16)
-    gains = rest_a[filled:].reshape(-1, LANES)[: 2 * (width // LANES)].reshape(2, width)
-    gains = lax.dynamic_slice_in_dim(gains, lax.axis_index("fsdp") * own, own, 1)
-    gains = gains.astype(jnp.float32)
+    gain_grads = rest_a[filled:].reshape(-1, LANES)[: 2 * (width // LANES)].reshape(2, width)
+    gain_grads = lax.dynamic_slice_in_dim(gain_grads, lax.axis_index("fsdp") * own, own, 1)
+    gain_grads = gain_grads.astype(jnp.float32)
     grads = finish(
         gate_total, up_total, down_a, down_b, out_a, out_b, rest_a, rest_b,
         own, width, kv_width, w_down.shape[0],
@@ -1692,8 +1868,8 @@
         jnp.swapaxes(layer_out.reshape(seq_count, block_len, width), 0, 1),
         jnp.swapaxes(grad_tokens.reshape(seq_count, block_len, width), 0, 1),
         *grads,
-        gains[0],
-        gains[1],
+        gain_grads[0],
+        gain_grads[1],
     )
 
 

time: 424 us -> 398 us (0.939)
  Pallas kernels: 349 us -> 383 us
  blocking collectives: 31.7 us -> 0 us
  between operations: 15 us -> 0.9 us
  local copies, waits for them, and re-layouts: 22.2 us -> 12.5 us
    pallas_call x1, Pallas kernels: 71.8 us -> 96.3 us  [attend(): pl.pallas_call(attend_kernel, out_shape=[jax.ShapeDtypeStruct((units, dee...]
    all_gather x2 -> x0, blocking collectives: 23.2 us -> none  [on_device(): lax.all_gather(weight, 'fsdp', axis=0, tiled=True)]
    pallas_call x1, Pallas kernels: 74.8 us -> 84.5 us  [feed_forward(): pl.pallas_call(ffn_kernel, out_shape=[jax.ShapeDtypeStruct((rows, width),...]
    unnamed x1 -> x0, blocking collectives: 8.51 us -> none
    dot_general x2 -> x0, local copies, waits for them, and re-layouts: 5.02 us -> none  [forward_dot(): return jnp.dot(left, right, preferred_element_type=jnp.float32)]
    unnamed x24 -> x2, local copies, waits for them, and re-layouts: 4.58 us -> 0.01 us
  transfers between devices with their start and end apart: 1 -> 0, of which waited for: 0 -> 0; matrix products, arithmetic and copies ran while one was open for 3% -> 0% of each run, Pallas kernels for 0% -> 0%
where the time goes in v8:
time: 398 us
  Pallas kernels  383 us (96%)
  local copies, waits for them, and re-layouts  12.5 us (3%)
    pallas_call x1, Pallas kernels, layer_back(): pl.pallas_call(back_kernel, out_shape=[jax.ShapeDtypeStruct((rows, width)...  193 us
    pallas_call x1, Pallas kernels, attend(): pl.pallas_call(attend_kernel, out_shape=[jax.ShapeDtypeStruct((units, dee...  96.3 us
    pallas_call x1, Pallas kernels, feed_forward(): pl.pallas_call(ffn_kernel, out_shape=[jax.ShapeDtypeStruct((rows, width),...  84.5 us
    pallas_call x1, Pallas kernels, finish(): pl.pallas_call(finish_kernel, grid=(group,), out_shape=outs, in_specs=[wi...  9.22 us

profile of v8, /device:TPU:0, one launch (start us, length us, event | category | flops | bytes accessed | tf_op | source)
XLA Modules:
  0.0 397.6 jit_solution(4723452119333067001)
XLA Ops:
  0.7 0.7 stack.9
  1.4 0.7 stack.10
  2.0 0.6 fusion.6.gain_ref
  2.7 0.8 multiply_sine_fusion
  3.4 1.9 copy.22
  5.3 1.9 copy.23
  7.3 96.3 %shard_map.194 = (bf16[12,128,384]{2,1,0:T(8,128)(2,1)}, bf16[1152,256]{1,0:T(8,128)(2,1)}, f32[8,1152]{1,0:T(8,128)}, bf16[1152,1152]{1,0:T(8,128)(2,1)}, bf16[...) custom-call(bf16[256,1152]{1,0:T(8,128)(2,1)} %bitcast.13, ...), custom_call_target="tpu_custom_call" | custom-call | tf_op jit(solution)/shard_map/pallas_call | solution.py:552
  103.6 1.4 fusion.7
  105.0 84.5 %shard_map.195 = (f32[256,1152]{1,0:T(8,128)}, bf16[4,256,1152]{2,1,0:T(8,128)(2,1)}, f32[256,1152]{1,0:T(8,128)}, bf16[256,1152]{1,0:T(8,128)(2,1)}, bf16[12,12...) custom-call(bf16[256,1152]{1,0:T(8,128)(2,1)} %bitcast.14, ...), custom_call_target="tpu_custom_call" | custom-call | tf_op jit(solution)/shard_map/pallas_call | solution.py:1129
  189.5 192.7 %shard_map.196 = (f32[256,1152]{1,0:T(8,128)}, bf16[256,1152]{1,0:T(8,128)(2,1)}, bf16[8,4,14,16,128]{4,3,2,1,0:T(8,128)(2,1)}, bf16[8,4,14,16,128]{4,3,2,1,0:T(...) custom-call(bf16[12,128,384]{2,1,0:T(8,128)(2,1)} %get-tuple-element, ...), custom_call_target="tpu_custom_call" | custom-call | tf_op jit(solution)/shard_map/pallas_call | solution.py:1659
  382.2 0.0 copy-start
  382.2 2.6 copy.29
  384.8 0.0 copy-done
  384.8 1.9 copy.28
  386.8 0.7 slice.20
  387.5 0.1 dynamic-slice_convert_fusion
  387.6 0.6 slice_reduce_fusion
  388.2 9.2 %shard_map.197 = (f32[288,1152]{1,0:T(8,128)}, f32[288,384]{1,0:T(8,128)}, f32[288,384]{1,0:T(8,128)}, f32[288,1152]{1,0:T(8,128)}, f32[288,3072]{1,0:T(8,128)},...) custom-call(bf16[8,4,14,16,128]{4,3,2,1,0:T(8,128)(2,1)} %get-tuple-element.80.gate_ref, ...), custom_call_target="tpu_custom_call" | custom-call | tf_op jit(solution)/shard_map/pallas_call | solution.py:1780
  (4 shorter events, 0.0 us)
Async XLA Ops:
  382.2 2.6 copy-start

commit v9 on v8

--- a/solution.py
+++ b/solution.py
@@ -1,3 +1,5 @@
+import functools
+
 import jax
 import jax.numpy as jnp
 from jax import lax
@@ -792,6 +794,11 @@
     return [dma((steps,))] * 2 + ([dma((parts,))] * 2 + [dma] if exchange else [])
 
 
+def wide_split(width):
+    group, count = lax.axis_size("fsdp"), lax.axis_size("ctx")
+    return 2 if FF // group // LANES * (width // group // 16) >= 4 * count else 1
+
+
 def query_split(width):
     return width // LANES * 7 // 9 * LANES
 
@@ -802,8 +809,8 @@
 
 def down_split(blocks, count):
     each = -(-blocks // count)
-    first = max(1, each // 2)
-    return first, max(1, each - first)
+    rings = 4 if each >= 4 else 2
+    return [max(1, (each + at) // rings) for at in range(rings)]
 
 
 class GroupScatter:
@@ -912,21 +919,29 @@
 def ffn_kernel(
     x_ref, low_ref, out_ref, gate_ref, up_ref, down_ref, all_g_ref, gain_ref,
     layer_ref, layer_part_ref, resid_grad_ref, branch_ref, g_wide_ref, gate_part_ref, up_part_ref,
-    down_a_done, down_b_done, gain_grad_ref,
-    all_n_ref, turned_n, turned_act, act_ref, gate_grad, up_grad, resid_ref, grad_own,
-    down_a_work, down_a_land, down_b_work, down_b_land, *rest,
+    *rest,
 ):
-    give_sib, got_sib, give_cross, got_cross, far, got_far = rest[:6]
-    n_sends, n_arrivals, grad_sends, grad_arrivals = rest[6:10]
-    down_a = SumRing(down_a_work, down_a_land, down_a_done, rest[10:12], True)
-    down_b = SumRing(down_b_work, down_b_land, down_b_done, rest[12:14], False)
-    rings = (down_a, down_b)
+    downs = len(down_split(gate_ref.shape[1] // 16, lax.axis_size("ctx")))
+    taken = iter(rest)
+
+    def take(number):
+        return [next(taken) for _ in range(number)]
+
+    down_done, (gain_grad_ref,) = take(downs), take(1)
+    all_n_ref, turned_n, turned_act, act_ref, gate_grad, up_grad, resid_ref, grad_own = take(8)
+    down_scratch = take(2 * downs)
+    give_sib, got_sib, give_cross, got_cross, far, got_far = take(6)
+    n_sends, n_arrivals, grad_sends, grad_arrivals = take(4)
+    rings = [
+        SumRing(*down_scratch[2 * at : 2 * at + 2], down_done[at], take(2), at % 2 == 0)
+        for at in range(downs)
+    ]
     group = lax.axis_size("fsdp")
     rows, width = x_ref.shape
     hidden = gate_ref.shape[1]
     barrier = pltpu.get_barrier_semaphore()
-    greeted = greet_group(barrier) + len(rings)
-    for ring in rings:
+    greeted = greet_group(barrier) + 2
+    for ring in rings[:2]:
         pl.semaphore_signal(barrier, inc=1, device_id=ring.after, device_id_type=MESH)
     step_in, step_out = hidden_tile(hidden), width_tile(width)
 
@@ -992,6 +1007,11 @@
     grad_sum.to_sibling().start()
     gathered.forward()
     grad_part(fsdp, grad_own)
+    def turn_act(shard):
+        transpose_into(turned_act.at[:, lane_tile(shard, rows)], act_ref.at[shard])
+
+    turn_act(fsdp)
+    turn_act(sibling)
     for step in range(1, chips):
         ours = gathered.same_core(chips - step)
         theirs = ours + sibling - fsdp
@@ -1002,26 +1022,29 @@
         hidden_part(ours)
         grad_part(ours, far.at[step - 1])
         grad_sum.add_cross(step)
-    for shard in range(group):
-        span = slice(shard * rows, (shard + 1) * rows)
-        transpose_into(turned_act.at[:, span], act_ref.at[shard])
+        turn_act(theirs)
+        turn_act(ours)
     blocks = hidden // 16
-    first = min(blocks, down_a_work.shape[0])
+    spans, first = [], 0
+    for ring in rings:
+        last = min(blocks, first + ring.work.shape[0])
+        spans.append((first, last, ring.work))
+        first = last
 
     def down_tile(at):
         columns = lane_tile(at, step_out)
         part = forward_dot(
             turned_act[...], all_g_ref[:, :, columns].reshape(group * rows, step_out)
         ).astype(jnp.bfloat16)
-        for begin, end, work in ((0, first, down_a_work), (first, blocks, down_b_work)):
+        for begin, end, work in spans:
             if end > begin:
                 work[: end - begin, :, columns] = part[begin * 16 : end * 16].reshape(
                     end - begin, 16, step_out
                 )
 
     tiles(width // step_out, down_tile)
-    for work, filled in ((down_a_work, first), (down_b_work, blocks - first)):
-        for spare in range(filled, work.shape[0]):
+    for begin, end, work in spans:
+        for spare in range(end - begin, work.shape[0]):
             work[spare] = jnp.zeros(work.shape[1:], work.dtype)
     for ring in rings:
         ring.start()
@@ -1106,7 +1129,7 @@
                     half * HD : (half + 1) * HD
                 ]
     begin = ticked[0]
-    tiles(max(0, down_a.ticks - begin), lambda at: ring_tick(begin + at))
+    tiles(max(0, rings[0].ticks - begin), lambda at: ring_tick(begin + at))
     gathered.sent()
     grad_sum.sent()
     for ring in rings:
@@ -1121,7 +1144,7 @@
     group, count = lax.axis_size("fsdp"), lax.axis_size("ctx")
     rows, width = x.shape
     hidden = my_gate.shape[1]
-    blocks = spread(hidden // LANES * (width // group // 16), count)
+    blocks = spread(hidden // LANES * (width // group // 16), wide_split(width) * count)
     chips = group // 2
     dma = pltpu.SemaphoreType.DMA((2 * chips - 1,))
     bf16 = jnp.bfloat16
@@ -1140,7 +1163,7 @@
             jax.ShapeDtypeStruct((1, width), jnp.float32),
         ],
         in_specs=[VMEM] * 8,
-        out_specs=[VMEM] * 10,
+        out_specs=[VMEM] * (8 + len(down_chunks)),
         scratch_shapes=[
             pltpu.VMEM((group, rows, width), bf16),
             pltpu.VMEM((width, group * rows), bf16),
@@ -1150,12 +1173,10 @@
             pltpu.VMEM((group, rows, hidden), bf16),
             pltpu.VMEM((rows, width), jnp.float32),
             pltpu.VMEM((rows, width), jnp.float32),
-            *ring_scratch(down_chunks[0]),
-            *ring_scratch(down_chunks[1]),
+            *[kind for chunk in down_chunks for kind in ring_scratch(chunk)],
             *scatter_scratch(rows, width),
             *[dma] * 4,
-            *ring_semaphores(),
-            *ring_semaphores(),
+            *[kind for _ in down_chunks for kind in ring_semaphores()],
         ],
         compiler_params=pltpu.CompilerParams(
             collective_id=2, has_side_effects=True, vmem_limit_bytes=60 << 20
@@ -1164,33 +1185,39 @@
 
 
 def back_kernel(
-    q_ref, g_ref, pairs_ref, mix_ref, log_ref, gate_ref, up_ref, down_a_ref, down_b_ref,
-    layer_base_ref, layer_part_ref, gain_grad_ref, branch_ref, low_t_ref, normed_t_ref, w_query_ref, w_key_ref, w_value_ref, x_ref, gain_ref,
-    resid_grad_ref, cos_ref, sin_ref,
-    tokens_ref, layer_ref, gate_total, up_total, down_a_total, down_b_total, out_a_total,
-    out_b_total, rest_a_total, rest_b_total, peer_got, chain_got, layer_sib, layer_cross, layer_far,
-    kv_ref, stage_ref, final_ref, qg_ref, delta_ref, grad_q_ref,
-    gate_work, gate_land, up_work, up_land, out_a_work, out_a_land, out_b_work, out_b_land,
-    rest_a_work, rest_a_land, rest_b_work, rest_b_land,
-    low_all, normed_all, branch_all, query_all, pair_all, upstream_ref, gain_give, gain_got,
-    far_ref, layer_stage,
-    *semaphores,
+    down_blocks, q_ref, g_ref, log_ref, gain_grad_ref, gain_ref, cos_ref, sin_ref,
+    pairs_ref, mix_in, gate_ref, up_ref, layer_base_in, layer_part_ref, branch_ref, low_t_ref,
+    normed_t_ref, w_query_in, w_key_in, w_value_in, x_in, resid_grad_in, *rest,
 ):
+    taken = iter(rest)
+
+    def take(number):
+        return [next(taken) for _ in range(number)]
+
+    halves, downs = wide_split(x_in.shape[1]), len(down_blocks)
+    down_refs = take(downs)
+    tokens_ref, layer_ref = take(2)
+    wide_totals, down_totals = take(2 * halves), take(downs)
+    out_a_total, out_b_total, rest_a_total, rest_b_total = take(4)
+    peer_got, chain_got, layer_sib, layer_cross, layer_far = take(5)
+    kv_ref, stage_ref, final_ref, qg_ref, delta_ref, grad_q_ref = take(6)
+    wide_scratch = take(4 * halves)
+    out_a_work, out_a_land, out_b_work, out_b_land = take(4)
+    rest_a_work, rest_a_land, rest_b_work, rest_b_land = take(4)
+    low_all, normed_all, branch_all, query_all, pair_all, upstream_ref, gain_give, gain_got = take(8)
+    far_ref, layer_stage = take(2)
+    mix_ref, layer_base_ref, w_query_ref, w_key_ref, w_value_ref, x_ref, resid_grad_ref = take(7)
     steps = Steps()
     fsdp, ctx, group, count = steps.fsdp, steps.ctx, lax.axis_size("fsdp"), lax.axis_size("ctx")
     units, deep, wide = q_ref.shape
     keys = pairs_ref.shape[2]
     rows, width = x_ref.shape
     own = width // group
-    taken = iter(semaphores)
-
-    def take(number):
-        return [next(taken) for _ in range(number)]
-
-    gate_ring = Ring(gate_work, gate_land, gate_total, take(5), True, True)
-    up_ring = Ring(up_work, up_land, up_total, take(5), False, True)
-    down_a = SpreadRing(down_a_total, take(2), True)
-    down_b = SpreadRing(down_b_total, take(2), False)
+    wide_rings = [
+        Ring(*wide_scratch[2 * at : 2 * at + 2], wide_totals[at], take(5), at < halves, True)
+        for at in range(2 * halves)
+    ]
+    down_rings = [SpreadRing(total, take(2), at % 2 == 0) for at, total in enumerate(down_totals)]
     out_a = Ring(out_a_work, out_a_land, out_a_total, take(2), True)
     out_b = Ring(out_b_work, out_b_land, out_b_total, take(2), False)
     layer_sum = GroupScatter(
@@ -1207,7 +1234,12 @@
     layer_sum.give_sib = layer_part_ref.at[layer_sum.sibling]
     rest_a = Ring(rest_a_work, rest_a_land, rest_a_total, take(2), True)
     rest_b = Ring(rest_b_work, rest_b_land, rest_b_total, take(2), False)
-    first_rings = (gate_ring, up_ring, down_a, down_b, out_a, out_b)
+    first_rings = []
+    for at in range(halves):
+        first_rings += [wide_rings[at], wide_rings[halves + at]]
+        first_rings += down_rings[at * downs // halves : (at + 1) * downs // halves]
+    begun_rings = len(first_rings)
+    first_rings += [out_a, out_b]
     peer_sends, peer_arrivals, chain_sends, chain_arrivals = take(4)
     branch_gather = GroupGather(lambda shard: branch_all.at[shard], *take(2))
     query_gather = GroupGather(lambda shard: query_all.at[shard], *take(2))
@@ -1217,7 +1249,7 @@
 
     barrier = pltpu.get_barrier_semaphore()
     greeted = steps.greet(barrier) + greet_group(barrier) + 2
-    for device in (gate_ring.after, up_ring.after):
+    for device in (out_a.after, out_b.after):
         pl.semaphore_signal(barrier, inc=1, device_id=device, device_id_type=MESH)
 
     loads = []
@@ -1227,21 +1259,33 @@
         copy.start()
         loads.append(copy)
 
-    n = gate_work.shape[2]
-    for source, target in ((gate_ref, gate_work), (up_ref, up_work)):
+    n = wide_scratch[0].shape[2]
+    for at, ring in enumerate(wide_rings):
+        source = (gate_ref, up_ref)[at // halves]
         for chunk in range(count):
-            load(source.at[:, pl.ds(chunk * n, n)], target.at[chunk])
-    for ring, source in ((down_a, down_a_ref), (down_b, down_b_ref)):
+            load(source.at[:, pl.ds((at % halves * count + chunk) * n, n)], ring.work.at[chunk])
+    for ring, source in zip(down_rings, down_refs):
         load(source, ring.chunk(ring.total, ring.first))
     ring_loads = len(loads)
     load(pairs_ref, kv_ref)
+    load(mix_in, mix_ref)
     load(branch_ref, branch_all.at[fsdp])
     load(low_t_ref.at[pl.ds(fsdp * own, own)], low_all.at[:, lane_tile(fsdp, rows)])
     load(normed_t_ref.at[pl.ds(fsdp * own, own)], normed_all.at[:, lane_tile(fsdp, rows)])
+    slot_loads = len(loads)
+    for source, target in (
+        (layer_base_in, layer_base_ref),
+        (w_query_in, w_query_ref),
+        (w_key_in, w_key_ref),
+        (w_value_in, w_value_ref),
+        (x_in, x_ref),
+        (resid_grad_in, resid_grad_ref),
+    ):
+        load(source, target)
     for copy in loads[:ring_loads]:
         copy.wait()
     pl.semaphore_wait(barrier, greeted)
-    for ring in first_rings[:4]:
+    for ring in first_rings[:begun_rings]:
         ring.start()
     branch_gather.start(branch_ref)
     layer_sum.to_sibling().start()
@@ -1279,9 +1323,9 @@
         )
         grad_q_ref[unit] = jnp.zeros((HD, wide), jnp.float32)
 
+    for copy in loads[ring_loads:slot_loads]:
+        copy.wait()
     tiles(units, prepare)
-    for copy in loads[ring_loads:]:
-        copy.wait()
 
     def tick(ring, at):
         @pl.when(jnp.logical_and(at >= 0, at < ring.ticks))
@@ -1291,7 +1335,7 @@
     late = steps.levels // 2 + 1
 
     def pump(at):
-        lag = (0, 0, 0, 0, late, late)
+        lag = [0] * begun_rings + [late, late]
         for turn, ring in enumerate(first_rings):
 
             @pl.when(lax.rem(at, len(first_rings)) == turn)
@@ -1408,6 +1452,7 @@
         out_b.start()
 
     turns = units // 2
+    rings = max(turns, len(first_rings))
 
     def slot(pair):
         def turn(at):
@@ -1426,9 +1471,10 @@
                 for unit in (2 * at, 2 * at + 1):
                     back(unit, ctx - 1, 1, False)
 
-            pump(pair * turns + at)
+            pump(pair * rings + at)
 
         tiles(turns, turn)
+        tiles(rings - turns, lambda at: pump(pair * rings + turns + at))
 
         @pl.when(jnp.logical_or(pair < steps.level, (pair == steps.level) & (steps.side == 1)))
         def _():
@@ -1441,7 +1487,7 @@
             out_grad()
 
     tiles(steps.levels, slot)
-    pumped = [steps.levels * turns]
+    pumped = [steps.levels * rings]
 
     def pump_next(times=1):
         def body(at, unused, begin=pumped[0]):
@@ -1482,7 +1528,8 @@
             query_all[fsdp, span, pair * 2 * HD : (pair + 1) * 2 * HD] = (
                 jnp.concatenate(heads, axis=0).astype(jnp.bfloat16).T
             )
-        pump_next()
+            if pair % 3 == 2:
+                pump_next()
     query_gather.start(query_all.at[fsdp])
     combine(steps.levels)
     kv_width = KVH * HD
@@ -1524,6 +1571,8 @@
             + dot_columns(pair_all[fsdp, :, kv_width:], w_value_ref[columns, :])
         )
 
+    for copy in loads[slot_loads:]:
+        copy.wait()
     pumping(width // step_out, upstream_tile)
     inputs = x_ref[...].astype(jnp.float32)
     scale = norm_scale(inputs)
@@ -1583,8 +1632,9 @@
     rest_a.start()
     rest_b.start()
     begun = pumped[0]
-    half = len(first_rings) // 2
-    total_pumps = max(gate_ring.ticks, late + out_a.ticks) * len(first_rings)
+    total_pumps = max(wide_rings[0].ticks, late + out_a.ticks) * len(first_rings)
+
+    half = -(-(total_pumps - begun) // rest_a.ticks)
 
     def last_ticks(at, unused):
         for turn in range(half):
@@ -1593,8 +1643,7 @@
         tick(rest_b, at)
         return unused
 
-    rounds = max(rest_a.ticks, -(-(total_pumps - begun) // half))
-    lax.fori_loop(0, rounds, last_ticks, 0)
+    lax.fori_loop(0, rest_a.ticks, last_ticks, 0)
     layer_sum.to_sibling().wait_recv()
     layer = layer_base_ref[...]
     arrived = [layer_sib]
@@ -1608,7 +1657,7 @@
         layer = layer + layer_stage[...].astype(jnp.float32)
     layer_ref[...] = layer.astype(jnp.bfloat16)
     layer_sum.sent()
-    for ring in first_rings + (rest_a, rest_b):
+    for ring in first_rings + [rest_a, rest_b]:
         ring.finish()
     for copy in turned:
         copy.wait_send()
@@ -1630,9 +1679,8 @@
 
 
 def layer_back(
-    q_wide, g_wide, all_pairs, mix, log_total, gate_part, up_part, down_a, down_b, layer_base,
-    layer_parts, gain_grad, branch, low_t, normed_t, w_query, w_key, w_value, x, gain, resid_grad,
-    cosine, sine,
+    q_wide, g_wide, log_total, gain_grad, gain, cosine, sine, all_pairs, mix, gate_part, up_part,
+    layer_base, layer_parts, branch, low_t, normed_t, w_query, w_key, w_value, x, resid_grad, downs,
 ):
     group, count = lax.axis_size("fsdp"), lax.axis_size("ctx")
     units, deep, wide = q_wide.shape
@@ -1641,12 +1689,13 @@
     own, kv_width = width // group, w_key.shape[1]
     bf16, f32 = jnp.bfloat16, jnp.float32
     dma = pltpu.SemaphoreType.DMA
-    wide_chunk = (group, gate_part.shape[1] // count, 16, LANES)
+    halves = wide_split(width)
+    wide_chunk = (group, gate_part.shape[1] // (halves * count), 16, LANES)
     gain_rows = spread(2 * (width // LANES), 16)
     split, row_blocks = query_split(width), own // 16
     out_first = out_split(width)
     chips = group // 2
-    out_a_chunk, out_b_chunk, a_chunk, b_chunk = [
+    small_chunks = [
         (spread(held, count) // count, 16, LANES)
         for held in (
             out_first // LANES * row_blocks,
@@ -1656,26 +1705,21 @@
         )
     ]
     levels = count // 2
+    loaded = [mix, layer_base, w_query, w_key, w_value, x, resid_grad]
     return pl.pallas_call(
-        back_kernel,
+        functools.partial(back_kernel, [part.shape[0] for part in downs]),
         out_shape=[
             jax.ShapeDtypeStruct((rows, width), f32),
             jax.ShapeDtypeStruct((rows, width), bf16),
-            ring_total(wide_chunk, True),
-            ring_total(wide_chunk, True),
-            ring_total(down_a.shape),
-            ring_total(down_b.shape),
-            ring_total(out_a_chunk),
-            ring_total(out_b_chunk),
-            ring_total(a_chunk),
-            ring_total(b_chunk),
+            *[ring_total(wide_chunk, True)] * (2 * halves),
+            *[ring_total(part.shape) for part in downs],
+            *[ring_total(chunk) for chunk in small_chunks],
             *[jax.ShapeDtypeStruct((levels, units, keys, deep), bf16)] * 2,
             jax.ShapeDtypeStruct((rows, width), bf16),
             *[jax.ShapeDtypeStruct((chips - 1, rows, width), bf16)] * 2,
         ],
-        in_specs=[VMEM, VMEM, ANY, VMEM, VMEM, ANY, ANY, ANY, ANY, VMEM, ANY, VMEM, ANY, ANY, ANY]
-        + [VMEM] * 8,
-        out_specs=[VMEM] * 10 + [ANY] * 5,
+        in_specs=[VMEM] * 7 + [ANY] * (14 + len(downs)),
+        out_specs=[VMEM] * (6 + 2 * halves + len(downs)) + [ANY] * 5,
         scratch_shapes=[
             pltpu.VMEM(all_pairs.shape, bf16),
             pltpu.VMEM((2, units, keys, deep), bf16),
@@ -1683,12 +1727,8 @@
             pltpu.VMEM((units, 2 * wide, deep), bf16),
             pltpu.VMEM((units, 1, wide), f32),
             pltpu.VMEM((units, HD, wide), f32),
-            *ring_scratch(wide_chunk, True),
-            *ring_scratch(wide_chunk, True),
-            *ring_scratch(out_a_chunk),
-            *ring_scratch(out_b_chunk),
-            *ring_scratch(a_chunk),
-            *ring_scratch(b_chunk),
+            *[kind for _ in range(2 * halves) for kind in ring_scratch(wide_chunk, True)],
+            *[kind for chunk in small_chunks for kind in ring_scratch(chunk)],
             pltpu.VMEM((own, group * rows), bf16),
             pltpu.VMEM((own, group * rows), bf16),
             pltpu.VMEM((group, rows, width), bf16),
@@ -1699,35 +1739,38 @@
             pltpu.VMEM((group - 1, gain_rows, LANES), f32),
             pltpu.VMEM((chips - 1, rows, width), bf16),
             pltpu.VMEM((rows, width), bf16),
-            *ring_semaphores(True),
-            *ring_semaphores(True),
-            *[kind for _ in range(4) for kind in ring_semaphores()],
+            *[pltpu.VMEM(array.shape, array.dtype) for array in loaded],
+            *[kind for _ in range(2 * halves) for kind in ring_semaphores(True)],
+            *[kind for _ in range(len(downs) + 2) for kind in ring_semaphores()],
             *[dma((group - 1,))] * 2,
             *[kind for _ in range(2) for kind in ring_semaphores()],
             *[dma((levels,))] * 4,
             *[group_semaphores()] * 6,
             *[dma((group - 1,))] * 6,
-            dma((6 + 2 * count,)),
+            dma((11 + len(downs) + 2 * halves * count,)),
             dma((2,)),
         ],
         compiler_params=pltpu.CompilerParams(
             collective_id=3, has_side_effects=True, vmem_limit_bytes=62 << 20
         ),
     )(
-        q_wide, g_wide, all_pairs, mix, log_total, gate_part, up_part, down_a, down_b, layer_base,
-        layer_parts, gain_grad, branch, low_t, normed_t, w_query, w_key, w_value, x, gain, resid_grad,
-        cosine, sine,
+        q_wide, g_wide, log_total, gain_grad, gain, cosine, sine, all_pairs, mix, gate_part, up_part,
+        layer_base, layer_parts, branch, low_t, normed_t, w_query, w_key, w_value, x, resid_grad,
+        *downs,
     )
 
 
-def finish_kernel(
-    gate_ref, up_ref, down_a_ref, down_b_ref, out_a_ref, out_b_ref, rest_a_ref, rest_b_ref,
-    query_grad, key_grad, value_grad, out_grad, gate_grad, up_grad, down_grad,
-):
+def finish_kernel(halves, downs, *refs):
+    wides, refs = refs[: 2 * halves], refs[2 * halves :]
+    down_refs, refs = refs[:downs], refs[downs:]
+    out_a_ref, out_b_ref, rest_a_ref, rest_b_ref = refs[:4]
+    query_grad, key_grad, value_grad, out_grad, gate_grad, up_grad, down_grad = refs[4:]
     rows = gate_grad.shape[0]
     row_blocks = rows // 16
-    for source, target in ((gate_ref, gate_grad), (up_ref, up_grad)):
-        held = source[...].reshape((-1,) + source.shape[3:])
+    for sources, target in ((wides[:halves], gate_grad), (wides[halves:], up_grad)):
+        held = jnp.concatenate(
+            [source[...].reshape((-1,) + source.shape[3:]) for source in sources], axis=0
+        )
         for block in range(target.shape[1] // LANES):
             target[:, block * LANES : (block + 1) * LANES] = (
                 held[block * row_blocks : (block + 1) * row_blocks]
@@ -1754,19 +1797,20 @@
         at = unpack(rest_b_ref, 0, query_grad, split, width // LANES)
         at = unpack(rest_b_ref, at, key_grad, 0, kv_width // LANES)
         unpack(rest_b_ref, at, value_grad, 0, kv_width // LANES)
-        blocks = down_grad.shape[0] // 16
-        first = min(down_a_ref.shape[0], blocks)
-        for begin, end, source in ((0, first, down_a_ref), (first, blocks, down_b_ref)):
+        blocks, begin = down_grad.shape[0] // 16, 0
+        for source in down_refs:
+            end = min(blocks, begin + source.shape[0])
             if end > begin:
                 down_grad[begin * 16 : end * 16, :] = (
                     source[: end - begin]
                     .reshape((end - begin) * 16, down_grad.shape[1])
                     .astype(jnp.float32)
                 )
-
-
-def finish(gate, up, down_a, down_b, out_a, out_b, rest_a, rest_b, own, width, kv_width, hidden):
-    count, group, n = gate.shape[:3]
+            begin = end
+
+
+def finish(wides, downs, smalls, own, width, kv_width, hidden):
+    count, group, n = wides[0].shape[:3]
 
     def whole(array):
         return pl.BlockSpec(array.shape, lambda part, rank=len(array.shape): (0,) * rank)
@@ -1778,13 +1822,13 @@
     ] + [jax.ShapeDtypeStruct((hidden, width), jnp.float32)]
     slice_spec = pl.BlockSpec((own, FF // group), lambda part: (0, part))
     return pl.pallas_call(
-        finish_kernel,
+        functools.partial(finish_kernel, len(wides) // 2, len(downs)),
         grid=(group,),
         out_shape=outs,
-        in_specs=[wide, wide] + [whole(a) for a in (down_a, down_b, out_a, out_b, rest_a, rest_b)],
+        in_specs=[wide] * len(wides) + [whole(a) for a in (*downs, *smalls)],
         out_specs=[whole(a) for a in outs[:4]] + [slice_spec, slice_spec, whole(outs[6])],
         compiler_params=pltpu.CompilerParams(vmem_limit_bytes=60 << 20),
-    )(gate, up, down_a, down_b, out_a, out_b, rest_a, rest_b)
+    )(*wides, *downs, *smalls)
 
 
 def on_device(
@@ -1811,59 +1855,24 @@
     ) = attend(
         x_rows, own_gains, cosine, sine, w_query, w_key, w_value, w_out, w_gate, w_up, g_rows, seq_count
     )
-    (
-        layer_base, layer_parts, grad_resid, grad_branch, g_wide, gate_part, up_part, down_a, down_b,
-        gain_term_ffn,
-    ) = (
+    layer_base, layer_parts, grad_resid, grad_branch, g_wide, gate_part, up_part, *downs = (
         feed_forward(
-            x_rows,
-            attn_low,
-            full_out,
-            my_gate,
-            my_up,
-            w_down,
-            all_g,
-            gains[1:2],
-            units,
-            wide,
+            x_rows, attn_low, full_out, my_gate, my_up, w_down, all_g, gains[1:2], units, wide
         )
     )
-    (
-        grad_tokens, layer_out, gate_total, up_total, down_a, down_b, out_a, out_b, rest_a, rest_b,
-        *_,
-    ) = layer_back(
-        q_wide,
-        g_wide,
-        all_pairs,
-        mix_unit,
-        log_total,
-        gate_part,
-        up_part,
-        down_a,
-        down_b,
-        layer_base,
-        layer_parts,
-        gain_term_ffn,
-        grad_branch,
-        low_t,
-        normed_t,
-        full_query,
-        full_key,
-        full_value,
-        x_rows,
-        gains[:1],
-        grad_resid,
-        cosine,
-        sine,
+    downs, gain_term_ffn = downs[:-1], downs[-1]
+    grad_tokens, layer_out, *sums = layer_back(
+        q_wide, g_wide, log_total, gain_term_ffn, gains[:1], cosine, sine, all_pairs, mix_unit,
+        gate_part, up_part, layer_base, layer_parts, grad_branch, low_t, normed_t, full_query,
+        full_key, full_value, x_rows, grad_resid, downs,
     )
+    wides, sums = sums[: 2 * wide_split(width)], sums[2 * wide_split(width) :]
+    smalls = sums[len(downs) : len(downs) + 4]
     filled = query_split(width) // LANES * (own // 16)
-    gain_grads = rest_a[filled:].reshape(-1, LANES)[: 2 * (width // LANES)].reshape(2, width)
+    gain_grads = smalls[2][filled:].reshape(-1, LANES)[: 2 * (width // LANES)].reshape(2, width)
     gain_grads = lax.dynamic_slice_in_dim(gain_grads, lax.axis_index("fsdp") * own, own, 1)
     gain_grads = gain_grads.astype(jnp.float32)
-    grads = finish(
-        gate_total, up_total, down_a, down_b, out_a, out_b, rest_a, rest_b,
-        own, width, kv_width, w_down.shape[0],
-    )
+    grads = finish(wides, sums[: len(downs)], smalls, own, width, kv_width, w_down.shape[0])
     return (
         jnp.swapaxes(layer_out.reshape(seq_count, block_len, width), 0, 1),
         jnp.swapaxes(grad_tokens.reshape(seq_count, block_len, width), 0, 1),

time: 398 us -> 401 us (level)
    pallas_call x2, Pallas kernels: 202 us -> 206 us  [the longest x1 197 us: layer_back(): pl.pallas_call(functools.partial(back_kernel, [part.shape[0] for part in...]
where the time goes in v9:
time: 401 us; the launch traced here: 400 us
  Pallas kernels  385 us (96%)
  local copies, waits for them, and re-layouts  12.5 us (3%)
    pallas_call x1, Pallas kernels, layer_back(): pl.pallas_call(functools.partial(back_kernel, [part.shape[0] for part in...  197 us
    pallas_call x1, Pallas kernels, attend(): pl.pallas_call(attend_kernel, out_shape=[jax.ShapeDtypeStruct((units, dee...  96.6 us
    pallas_call x1, Pallas kernels, feed_forward(): pl.pallas_call(ffn_kernel, out_shape=[jax.ShapeDtypeStruct((rows, width),...  82.5 us
    pallas_call x1, Pallas kernels, finish(): pl.pallas_call(functools.partial(finish_kernel, len(wides) // 2, len(down...  9.51 us

profile of v9, /device:TPU:0, one launch (start us, length us, event | category | flops | bytes accessed | tf_op | source)
XLA Modules:
  0.0 400.4 jit_solution(18422561126316936548)
XLA Ops:
  0.7 0.7 stack.9
  1.4 0.7 stack.10
  2.0 0.6 fusion.6.gain_ref
  2.7 0.8 multiply_sine_fusion
  3.4 1.9 copy.22
  5.3 1.9 copy.23
  7.3 96.6 %shard_map.194 = (bf16[12,128,384]{2,1,0:T(8,128)(2,1)}, bf16[1152,256]{1,0:T(8,128)(2,1)}, f32[8,1152]{1,0:T(8,128)}, bf16[1152,1152]{1,0:T(8,128)(2,1)}, bf16[...) custom-call(bf16[256,1152]{1,0:T(8,128)(2,1)} %bitcast.13, ...), custom_call_target="tpu_custom_call" | custom-call | tf_op jit(solution)/shard_map/pallas_call | solution.py:554
  103.9 1.4 fusion.7
  105.4 82.5 %shard_map.195 = (f32[256,1152]{1,0:T(8,128)}, bf16[4,256,1152]{2,1,0:T(8,128)(2,1)}, f32[256,1152]{1,0:T(8,128)}, bf16[256,1152]{1,0:T(8,128)(2,1)}, bf16[12,12...) custom-call(bf16[256,1152]{1,0:T(8,128)(2,1)} %bitcast.14, ...), custom_call_target="tpu_custom_call" | custom-call | tf_op jit(solution)/shard_map/pallas_call | solution.py:1152
  187.8 196.8 %shard_map.196 = (f32[256,1152]{1,0:T(8,128)}, bf16[256,1152]{1,0:T(8,128)(2,1)}, bf16[8,4,7,16,128]{4,3,2,1,0:T(8,128)(2,1)}, bf16[8,4,7,16,128]{4,3,2,1,0:T(8,...) custom-call(bf16[12,128,384]{2,1,0:T(8,128)(2,1)} %get-tuple-element, ...), custom_call_target="tpu_custom_call" | custom-call | tf_op jit(solution)/shard_map/pallas_call | solution.py:1709
  384.7 0.0 copy-start
  384.7 2.6 copy.29
  387.3 0.0 copy-done
  387.3 1.9 copy.28
  389.2 0.7 slice.20
  389.9 0.1 dynamic-slice_convert_fusion
  390.0 0.6 slice_reduce_fusion
  390.6 9.5 %shard_map.197 = (f32[288,1152]{1,0:T(8,128)}, f32[288,384]{1,0:T(8,128)}, f32[288,384]{1,0:T(8,128)}, f32[288,1152]{1,0:T(8,128)}, f32[288,3072]{1,0:T(8,128)},...) custom-call(bf16[8,4,7,16,128]{4,3,2,1,0:T(8,128)(2,1)} %get-tuple-element.88.refs_0_, ...), custom_call_target="tpu_custom_call" | custom-call | tf_op jit(solution)/shard_map/pallas_call | solution.py:1824
  (4 shorter events, 0.0 us)
Async XLA Ops:
  384.7 2.6 copy-start
